TPU v7x, 32 devices: a whole 2x2x4 slice. The times are simulated.
32 devices in a mesh: grp: 2 (over x), view: 16 (over z, y, core).
Axes of the slice: x: 2, y: 2, z: 4, core: 2. Of those that a mesh axis runs over, the one named last changes fastest.
Arguments:
- volume: float32 [64, 16, 2, 512], P(('grp', 'view')), may hold values from 0 to 2
- footprint: bfloat16 [64, 2, 512, 896], P(('grp', 'view')), may hold values from -0.1875 to 0.1875
- measured: bfloat16 [256, 64, 896], P(('grp', 'view')), may hold values from 0 to 3
- angle_index: int32 [256], P(('grp', 'view')), may hold values from 0 to 1
- cover: int32 [256, 4], P(('grp', 'view')), may hold values from 0 to 63, as said below
- offset: int32 [256, 4], P(('grp', 'view')), may hold values from 0 to 48
- count: int32 [256], P(('grp', 'view')), may hold values from 1 to 4
Outputs:
- gradient: float32 [64, 16, 2, 512], P(('grp', 'view'))
Inputs may be any that keep to these rules, and one draw needn't show every extreme that they name: Let p = v // 8. cover[v,k] lies between max(p - 4, 0) * 2 and min(p + 5, 32) * 2 - 1, and both ends are named by some slot 0 of p's views.
All inputs are finite; a program needn't handle non-finite values.
Results may differ from a plain program's by a relative error of at most 0.0019.
Values may be sent and summed in bfloat16 or wider, within the bound.
No kernel may reach another device: no remote copies, remote signals or barrier semaphores. Data moves between devices by JAX's collectives and lax.ppermute only.
A program may use at most 64 MiB of HBM per device.

v0:
```python
import jax
import jax.numpy as jnp
from jax import lax
from jax.sharding import PartitionSpec as P

REACH = 4


DELTA = 0.5
PRIOR_WEIGHT = 2.0


def passed_along(shard, axis, by):
    peers = lax.axis_size(axis)
    pairs = [(i, i + by) for i in range(peers) if 0 <= i + by < peers]
    return lax.ppermute(shard, axis, pairs)


def padded_2(block, sides, width):
    for axis, dim in sides:
        count = lax.axis_size(axis)
        forward = [(i, i + 1) for i in range(count - 1)]
        backward = [(target, source) for source, target in forward]
        low = lax.ppermute(
            lax.slice_in_dim(block, block.shape[dim] - width, None, axis=dim), axis, forward
        )
        high = lax.ppermute(lax.slice_in_dim(block, 0, width, axis=dim), axis, backward)
        block = jnp.concatenate([low, block, high], axis=dim)
    return block


def shards(volume, footprint, measured, angle_index, cover, offset, count):
    local_blocks, slab_rows, strip_rows, row_width = volume.shape
    view_count, det_rows, channels = measured.shape
    table_count = footprint.shape[0]
    slot_count = cover.shape[1]
    plane = strip_rows * row_width
    total_dev = lax.axis_size(("grp", "view"))
    position = lax.axis_index(("grp", "view"))
    vol_bf = volume.astype(jnp.bfloat16)
    pieces = []
    for step in range(-REACH, REACH + 1):
        if step == 0:
            pieces.append(vol_bf)
        else:
            pieces.append(passed_along(vol_bf, ("grp", "view"), -step))
    window = jnp.concatenate(pieces, 0)
    win_blocks = window.shape[0]
    win_rows = window.reshape(win_blocks * slab_rows, plane)
    tables = footprint.reshape(table_count, plane, channels)
    base = (position - REACH) * local_blocks
    highest = lax.Precision.HIGHEST
    table_proj = jnp.stack(
        [
            jnp.dot(win_rows, tables[table], preferred_element_type=jnp.float32)
            for table in range(table_count)
        ],
        0,
    )
    table_proj = table_proj.reshape(table_count * win_blocks, slab_rows * channels)
    local_idx = cover - base
    slot_iota = jnp.arange(slot_count, dtype=jnp.int32)
    alive = (slot_iota[None, :] < count[:, None]).astype(jnp.float32)
    pick_key = angle_index[:, None] * win_blocks + local_idx
    select = (
        pick_key[:, :, None] == jnp.arange(table_count * win_blocks, dtype=jnp.int32)[None, None, :]
    ).astype(jnp.float32)
    gathered = jnp.dot(
        select.reshape(view_count * slot_count, table_count * win_blocks),
        table_proj,
        precision=highest,
        preferred_element_type=jnp.float32,
    )
    gathered = gathered.reshape(view_count, slot_count, slab_rows, channels)
    row_target = offset[:, :, None] + jnp.arange(slab_rows, dtype=jnp.int32)[None, None, :]
    row_hit = (
        row_target[:, :, :, None] == jnp.arange(det_rows, dtype=jnp.int32)[None, None, None, :]
    ).astype(jnp.float32)
    placing = row_hit * alive[:, :, None, None]
    forward_projection = jnp.einsum(
        "vkir,vkic->vrc", placing, gathered, precision=highest, preferred_element_type=jnp.float32
    )
    measured_float = measured.astype(jnp.float32)
    weighted_residual = (jnp.exp(-measured_float) * (forward_projection - measured_float)).astype(
        jnp.bfloat16
    )
    picked = jnp.einsum(
        "vkir,vrc->vkic",
        row_hit.astype(jnp.bfloat16),
        weighted_residual,
        preferred_element_type=jnp.float32,
    ).astype(jnp.bfloat16)
    back = jnp.zeros((view_count * slot_count * slab_rows, plane), jnp.float32)
    for table in range(table_count):
        table_mask = (angle_index == table).astype(jnp.bfloat16)[:, None, None, None]
        masked = (picked * table_mask).reshape(view_count * slot_count * slab_rows, channels)
        back = back + lax.dot_general(
            masked, tables[table], (((1,), (1,)), ((), ())), preferred_element_type=jnp.float32
        )
    back = back.reshape(view_count * slot_count, slab_rows * plane)
    scatter_rows = (
        local_idx[:, :, None] == jnp.arange(win_blocks, dtype=jnp.int32)[None, None, :]
    ).astype(jnp.float32) * alive[:, :, None]
    scatter_rows = scatter_rows.reshape(view_count * slot_count, win_blocks)
    win_grad = lax.dot_general(
        scatter_rows,
        back,
        (((0,), (0,)), ((), ())),
        precision=highest,
        preferred_element_type=jnp.float32,
    )
    parts = win_grad.reshape((2 * REACH + 1, local_blocks, slab_rows, strip_rows, row_width))
    data_grad = parts[REACH]
    for step in range(-REACH, REACH + 1):
        if step != 0:
            data_grad = data_grad + passed_along(parts[REACH + step], ("grp", "view"), step)
    slices_here = local_blocks * slab_rows
    flat = volume.reshape(slices_here, strip_rows, row_width)
    padded = padded_2(flat, ((("grp", "view"), 0),), 1)
    global_row = position * slices_here + jnp.arange(slices_here, dtype=jnp.int32)
    lower_ok = (global_row > 0)[:, None, None]
    upper_ok = (global_row < total_dev * slices_here - 1)[:, None, None]
    prior = jnp.where(lower_ok, jnp.clip(flat - padded[:-2], -DELTA, DELTA), 0.0)
    prior = prior + jnp.where(upper_ok, jnp.clip(flat - padded[2:], -DELTA, DELTA), 0.0)
    ydiff = jnp.clip(flat[:, 1:] - flat[:, :-1], -DELTA, DELTA)
    prior = (
        prior + jnp.pad(ydiff, ((0, 0), (1, 0), (0, 0))) - jnp.pad(ydiff, ((0, 0), (0, 1), (0, 0)))
    )
    xdiff = jnp.clip(flat[:, :, 1:] - flat[:, :, :-1], -DELTA, DELTA)
    prior = (
        prior + jnp.pad(xdiff, ((0, 0), (0, 0), (1, 0))) - jnp.pad(xdiff, ((0, 0), (0, 0), (0, 1)))
    )
    return data_grad + PRIOR_WEIGHT * prior.reshape(volume.shape)


def solution(mesh):
    in_specs = (
        P(("grp", "view"), None, None, None),
        P(("grp", "view"), None, None, None),
        P(("grp", "view"), None, None),
        P(("grp", "view")),
        P(("grp", "view"), None),
        P(("grp", "view"), None),
        P(("grp", "view")),
    )
    out_specs = P(("grp", "view"), None, None, None)
    return jax.shard_map(shards, mesh=mesh, in_specs=in_specs, out_specs=out_specs, check_vma=False)
```

profile of v0, /device:TPU:3, one launch (start us, length us, event | category | flops | bytes accessed | tf_op | source)
XLA Modules:
  0.0 93.5 jit_solution(663022086720189765)
XLA Ops:
  0.0 0.9 %convert_element_type.56 = bf16[2,16,2,512]{3,2,1,0:T(2,128)(2,1)S(1)} convert(f32[2,16,2,512]{3,2,1,0:T(2,128)} %param.7) | non-fusion elementwise | flops 32768 | bytes 196608 | tf_op jit(solution)/shard_map/convert_element_type | solution.py:40
  1.0 3.2 %collective-permute-start = (bf16[2,16,2,512]{3,2,1,0:T(2,128)(2,1)S(1)}, bf16[2,16,2,512]{3,2,1,0:T(2,128)(2,1)S(1)}, u32[]{:S(2)}, u32[]{:S(2)}) collective-permute-start(bf16[2,16,2,512]{3,2,1,0:T(2,128)(2,1)S(1)} %convert_element_type.56), channel_id=1, source_target_pairs={{0,4},{1,5},{2,6},{3,7},{4,8},{5,9},{6,10},{7,11},{8,12},{9,13},{1... | collective-permute-start | bytes 196616 | tf_op jit(solution)/shard_map/ppermute | solution.py:16
  4.2 4.0 %collective-permute-start.1 = (bf16[2,16,2,512]{3,2,1,0:T(2,128)(2,1)S(1)}, bf16[2,16,2,512]{3,2,1,0:T(2,128)(2,1)S(1)}, u32[]{:S(2)}, u32[]{:S(2)}) collective-permute-start(bf16[2,16,2,512]{3,2,1,0:T(2,128)(2,1)S(1)} %convert_element_type.56), channel_id=1, source_target_pairs={{0,3},{1,4},{2,5},{3,6},{4,7},{5,8},{6,9},{7,10},{8,11},{9,12},{10... | collective-permute-start | bytes 196616 | tf_op jit(solution)/shard_map/ppermute | solution.py:16
  8.2 3.1 %collective-permute-start.2 = (bf16[2,16,2,512]{3,2,1,0:T(2,128)(2,1)S(1)}, bf16[2,16,2,512]{3,2,1,0:T(2,128)(2,1)S(1)}, u32[]{:S(2)}, u32[]{:S(2)}) collective-permute-start(bf16[2,16,2,512]{3,2,1,0:T(2,128)(2,1)S(1)} %convert_element_type.56), channel_id=1, source_target_pairs={{0,2},{1,3},{2,4},{3,5},{4,6},{5,7},{6,8},{7,9},{8,10},{9,11},{10,... | collective-permute-start | bytes 196616 | tf_op jit(solution)/shard_map/ppermute | solution.py:16
  11.4 2.8 %collective-permute-start.3 = (bf16[2,16,2,512]{3,2,1,0:T(2,128)(2,1)S(1)}, bf16[2,16,2,512]{3,2,1,0:T(2,128)(2,1)S(1)}, u32[]{:S(2)}, u32[]{:S(2)}) collective-permute-start(bf16[2,16,2,512]{3,2,1,0:T(2,128)(2,1)S(1)} %convert_element_type.56), channel_id=1, source_target_pairs={{0,1},{1,2},{2,3},{3,4},{4,5},{5,6},{6,7},{7,8},{8,9},{9,10},{10,1... | collective-permute-start | bytes 196616 | tf_op jit(solution)/shard_map/ppermute | solution.py:16
  14.2 1.9 %collective-permute-start.4 = (bf16[2,16,2,512]{3,2,1,0:T(2,128)(2,1)S(1)}, bf16[2,16,2,512]{3,2,1,0:T(2,128)(2,1)S(1)}, u32[]{:S(2)}, u32[]{:S(2)}) collective-permute-start(bf16[2,16,2,512]{3,2,1,0:T(2,128)(2,1)S(1)} %convert_element_type.56), channel_id=1, source_target_pairs={{1,0},{2,1},{3,2},{4,3},{5,4},{6,5},{7,6},{8,7},{9,8},{10,9},{11,1... | collective-permute-start | bytes 196616 | tf_op jit(solution)/shard_map/ppermute | solution.py:16
  16.1 0.7 fusion.42
  16.8 1.2 %fusion.13 = f32[32,2,511]{2,1,0:T(2,128)S(1)} fusion(f32[32,2,512]{2,1,0:T(2,128)} %bitcast.60), kind=kLoop, calls=%fused_computation.22 | loop fusion | flops 65408 | bytes 392448 | tf_op jit(solution)/shard_map/jit(clip)/min | solution.py:129
  18.1 3.6 %fusion.40 = (bf16[1,2,512,896]{3,2,1,0:T(8,128)(2,1)}, bf16[1,2,512,896]{3,2,1,0:T(8,128)(2,1)S(1)}) fusion(bf16[2,2,512,896]{3,2,1,0:T(8,128)(2,1)} %param.8), kind=kLoop, calls=%fused_computation.72 | loop fusion | bytes 7340032 | tf_op jit(solution)/shard_map/slice | solution.py:55
  22.2 5.7 %collective-permute-start.5 = (bf16[2,16,2,512]{3,2,1,0:T(2,128)(2,1)S(1)}, bf16[2,16,2,512]{3,2,1,0:T(2,128)(2,1)S(1)}, u32[]{:S(2)}, u32[]{:S(2)}) collective-permute-start(bf16[2,16,2,512]{3,2,1,0:T(2,128)(2,1)S(1)} %convert_element_type.56), channel_id=1, source_target_pairs={{2,0},{3,1},{4,2},{5,3},{6,4},{7,5},{8,6},{9,7},{10,8},{11,9},{12,... | collective-permute-start | bytes 196616 | tf_op jit(solution)/shard_map/ppermute | solution.py:16
  28.0 3.8 %collective-permute-start.6 = (bf16[2,16,2,512]{3,2,1,0:T(2,128)(2,1)S(1)}, bf16[2,16,2,512]{3,2,1,0:T(2,128)(2,1)S(1)}, u32[]{:S(2)}, u32[]{:S(2)}) collective-permute-start(bf16[2,16,2,512]{3,2,1,0:T(2,128)(2,1)S(1)} %convert_element_type.56), channel_id=1, source_target_pairs={{3,0},{4,1},{5,2},{6,3},{7,4},{8,5},{9,6},{10,7},{11,8},{12,9},{13... | collective-permute-start | bytes 196616 | tf_op jit(solution)/shard_map/ppermute | solution.py:16
  31.9 2.1 %collective-permute-start.7 = (bf16[2,16,2,512]{3,2,1,0:T(2,128)(2,1)S(1)}, bf16[2,16,2,512]{3,2,1,0:T(2,128)(2,1)S(1)}, u32[]{:S(2)}, u32[]{:S(2)}) collective-permute-start(bf16[2,16,2,512]{3,2,1,0:T(2,128)(2,1)S(1)} %convert_element_type.56), channel_id=1, source_target_pairs={{4,0},{5,1},{6,2},{7,3},{8,4},{9,5},{10,6},{11,7},{12,8},{13,9},{1... | collective-permute-start | bytes 196616 | tf_op jit(solution)/shard_map/ppermute | solution.py:16
  34.1 2.3 %collective-permute-start.16 = (f32[1,2,512]{2,1,0:T(2,128)S(1)}, f32[1,2,512]{2,1,0:T(2,128)S(1)}, u32[]{:S(2)}, u32[]{:S(2)}) collective-permute-start(f32[1,2,512]{2,1,0:T(2,128)S(1)} %get-tuple-element.20), channel_id=1, source_target_pairs={{0,1},{1,2},{2,3},{3,4},{4,5},{5,6},{6,7},{7,8},{8,9},{9,10},{10,1... | collective-permute-start | bytes 12296 | tf_op jit(solution)/shard_map/ppermute | solution.py:24
  36.6 2.0 %collective-permute-start.17 = (f32[1,2,512]{2,1,0:T(2,128)S(1)}, f32[1,2,512]{2,1,0:T(2,128)S(1)}, u32[]{:S(2)}, u32[]{:S(2)}) collective-permute-start(f32[1,2,512]{2,1,0:T(2,128)S(1)} %get-tuple-element.21), channel_id=1, source_target_pairs={{1,0},{2,1},{3,2},{4,3},{5,4},{6,5},{7,6},{8,7},{9,8},{10,9},{11,1... | collective-permute-start | bytes 12296 | tf_op jit(solution)/shard_map/ppermute | solution.py:27
  39.0 0.8 convolution_bitcast_fusion
  39.7 0.7 copy-done.3
  40.5 0.8 convolution_bitcast_fusion.1
  41.2 1.5 %pad_maximum_fusion = f32[2,288,896]{2,1,0:T(8,128)} fusion(f32[1,288,896]{2,1,0:T(8,128)S(1)} %convolution_bitcast_fusion, f32[1,288,896]{2,1,0:T(8,128)S(1)} %convolution_bitcast_fusion.1), kind=kLoop, calls=%fused_computation.5 | loop fusion | flops 516096 | bytes 4128768 | tf_op jit(solution)/shard_map/stack | solution.py:53
  42.7 1.7 %reshape.137 = f32[36,14336]{1,0:T(8,128)S(1)} reshape(f32[2,288,896]{2,1,0:T(8,128)} %pad_maximum_fusion) | data formatting | bytes 4128768 | tf_op jit(solution)/shard_map/reshape | solution.py:60
  44.5 0.4 copy.19
  45.0 1.8 %fusion = f32[8,4,16,896]{3,0,2,1:T(8,128)S(1)} fusion(f32[16,896,36,1]{1,0,2,3:T(8,128)S(1)} %slice_bitcast_fusion, s32[8,4]{0,1:T(4,128)S(1)} %get-tuple-element.5), kind=kOutput, calls=%fused_computation | convolution fusion | flops 198182016 | bytes 3899520 | tf_op jit(solution)/shard_map/dot_general | solution.py:68
  46.9 2.3 %fusion.9 = bf16[8,64,896,1]{2,1,3,0:T(8,128)(2,1)S(1)} fusion(f32[8,4,16,896]{3,0,2,1:T(8,128)S(1)} %fusion, bf16[8,64,896]{2,1,0:T(8,128)(2,1)S(1)} %copy-done.5, f32[8,4]{1,0:T(8,128)S(1)} %fusion.35, s32[8,4,16]{2,1,0:T(4,128)S(1)} %iota_add_fusion), kind=kOutput, calls=%fused_computation.15 | convolution fusion | flops 354680832 | bytes 3672192 | tf_op jit(solution)/shard_map/vkir,vkic->vrc/dot_general | solution.py:80
  49.2 0.5 broadcast_multiply_fusion
  49.7 1.0 %copy-done.4 = bf16[1,2,512,896]{3,2,1,0:T(8,128)(2,1)S(1)} copy-done((bf16[1,2,512,896]{3,2,1,0:T(8,128)(2,1)S(1)}, bf16[1,2,512,896]{3,2,1,0:T(8,128)(2,1)}, u32[]{:S(2)}) %copy-start.4) | copy-done | bytes 1835032
  50.7 1.3 %fusion.43 = f32[512,1024]{1,0:T(8,128)S(1)} fusion(bf16[512,896]{1,0:T(8,128)(2,1)S(1)} %bitcast.68, bf16[1024,896]{1,0:T(8,128)(2,1)S(1)} %bitcast.66), kind=kOutput, calls=%fused_computation.75 | convolution fusion | flops 939524096 | bytes 4849664 | tf_op jit(solution)/shard_map/dot_general | solution.py:97
  52.0 0.2 copy-done.2
  52.2 2.6 %convolution_add_fusion = f32[512,1024]{1,0:T(8,128)} fusion(f32[512,1024]{1,0:T(8,128)S(1)} %fusion.43, bf16[512,896]{1,0:T(8,128)(2,1)S(1)} %bitcast.67, bf16[1024,896]{1,0:T(8,128)(2,1)S(1)} %bitcast.64), kind=kOutput, calls=%fused_computation.11 | convolution fusion | flops 940048384 | bytes 6946816 | tf_op jit(solution)/shard_map/dot_general | solution.py:97
  54.8 1.7 %reshape.140 = f32[32,16384]{1,0:T(8,128)S(1)} reshape(f32[512,1024]{1,0:T(8,128)} %convolution_add_fusion) | data formatting | bytes 4194304 | tf_op jit(solution)/shard_map/reshape | solution.py:100
  56.6 1.6 %fusion.27 = f32[18,16384]{1,0:T(8,128)S(1)} fusion(f32[32,16384]{1,0:T(8,128)S(1)} %reshape.140, f32[32]{0:T(128)S(1)} %reshape.142, s32[32]{0:T(128)S(1)} %eq.65), kind=kOutput, calls=%fused_computation.52 | convolution fusion | flops 113247360 | bytes 3277056 | tf_op jit(solution)/shard_map/dot_general | solution.py:105
  58.2 0.4 fusion.41
  58.6 0.2 squeeze.45
  58.8 3.2 %collective-permute-start.15 = (f32[2,16,2,512]{3,2,1,0:T(2,128)S(1)}, f32[2,16,2,512]{3,2,1,0:T(2,128)S(1)}, u32[]{:S(2)}, u32[]{:S(2)}) collective-permute-start(f32[2,16,2,512]{3,2,1,0:T(2,128)S(1)} %squeeze.45), channel_id=1, source_target_pairs={{0,4},{1,5},{2,6},{3,7},{4,8},{5,9},{6,10},{7,11},{8,12},{9,13},{1... | collective-permute-start | bytes 393224 | tf_op jit(solution)/shard_map/ppermute | solution.py:16
  62.0 0.2 squeeze.44
  62.1 4.4 %collective-permute-start.14 = (f32[2,16,2,512]{3,2,1,0:T(2,128)S(1)}, f32[2,16,2,512]{3,2,1,0:T(2,128)S(1)}, u32[]{:S(2)}, u32[]{:S(2)}) collective-permute-start(f32[2,16,2,512]{3,2,1,0:T(2,128)S(1)} %squeeze.44), channel_id=1, source_target_pairs={{0,3},{1,4},{2,5},{3,6},{4,7},{5,8},{6,9},{7,10},{8,11},{9,12},{10... | collective-permute-start | bytes 393224 | tf_op jit(solution)/shard_map/ppermute | solution.py:16
  66.6 0.2 squeeze.43
  66.8 2.2 %collective-permute-start.13 = (f32[2,16,2,512]{3,2,1,0:T(2,128)S(1)}, f32[2,16,2,512]{3,2,1,0:T(2,128)S(1)}, u32[]{:S(2)}, u32[]{:S(2)}) collective-permute-start(f32[2,16,2,512]{3,2,1,0:T(2,128)S(1)} %squeeze.43), channel_id=1, source_target_pairs={{0,2},{1,3},{2,4},{3,5},{4,6},{5,7},{6,8},{7,9},{8,10},{9,11},{10,... | collective-permute-start | bytes 393224 | tf_op jit(solution)/shard_map/ppermute | solution.py:16
  69.1 0.2 squeeze.42
  69.3 0.2 squeeze.41
  69.4 0.2 squeeze.40
  69.6 0.2 squeeze.39
  69.9 3.1 %collective-permute-start.12 = (f32[2,16,2,512]{3,2,1,0:T(2,128)S(1)}, f32[2,16,2,512]{3,2,1,0:T(2,128)S(1)}, u32[]{:S(2)}, u32[]{:S(2)}) collective-permute-start(f32[2,16,2,512]{3,2,1,0:T(2,128)S(1)} %squeeze.42), channel_id=1, source_target_pairs={{0,1},{1,2},{2,3},{3,4},{4,5},{5,6},{6,7},{7,8},{8,9},{9,10},{10,1... | collective-permute-start | bytes 393224 | tf_op jit(solution)/shard_map/ppermute | solution.py:16
  73.0 1.9 %collective-permute-start.11 = (f32[2,16,2,512]{3,2,1,0:T(2,128)S(1)}, f32[2,16,2,512]{3,2,1,0:T(2,128)S(1)}, u32[]{:S(2)}, u32[]{:S(2)}) collective-permute-start(f32[2,16,2,512]{3,2,1,0:T(2,128)S(1)} %squeeze.41), channel_id=1, source_target_pairs={{1,0},{2,1},{3,2},{4,3},{5,4},{6,5},{7,6},{8,7},{9,8},{10,9},{11,1... | collective-permute-start | bytes 393224 | tf_op jit(solution)/shard_map/ppermute | solution.py:16
  75.0 6.1 %collective-permute-start.10 = (f32[2,16,2,512]{3,2,1,0:T(2,128)S(1)}, f32[2,16,2,512]{3,2,1,0:T(2,128)S(1)}, u32[]{:S(2)}, u32[]{:S(2)}) collective-permute-start(f32[2,16,2,512]{3,2,1,0:T(2,128)S(1)} %squeeze.40), channel_id=1, source_target_pairs={{2,0},{3,1},{4,2},{5,3},{6,4},{7,5},{8,6},{9,7},{10,8},{11,9},{12,... | collective-permute-start | bytes 393224 | tf_op jit(solution)/shard_map/ppermute | solution.py:16
  81.1 5.0 %collective-permute-start.9 = (f32[2,16,2,512]{3,2,1,0:T(2,128)S(1)}, f32[2,16,2,512]{3,2,1,0:T(2,128)S(1)}, u32[]{:S(2)}, u32[]{:S(2)}) collective-permute-start(f32[2,16,2,512]{3,2,1,0:T(2,128)S(1)} %squeeze.39), channel_id=1, source_target_pairs={{3,0},{4,1},{5,2},{6,3},{7,4},{8,5},{9,6},{10,7},{11,8},{12,9},{13... | collective-permute-start | bytes 393224 | tf_op jit(solution)/shard_map/ppermute | solution.py:16
  86.1 3.4 %collective-permute-start.8 = (f32[2,16,2,512]{3,2,1,0:T(2,128)S(1)}, f32[2,16,2,512]{3,2,1,0:T(2,128)S(1)}, u32[]{:S(2)}, u32[]{:S(2)}) collective-permute-start(f32[2,16,2,512]{3,2,1,0:T(2,128)S(1)} %squeeze.38), channel_id=1, source_target_pairs={{4,0},{5,1},{6,2},{7,3},{8,4},{9,5},{10,6},{11,7},{12,8},{13,9},{1... | collective-permute-start | bytes 393224 | tf_op jit(solution)/shard_map/ppermute | solution.py:16
  89.5 0.4 subtract_multiply_fusion
  90.1 2.7 %collective-permute-done.8 = f32[2,16,2,512]{3,2,1,0:T(2,128)S(1)} collective-permute-done((f32[2,16,2,512]{3,2,1,0:T(2,128)S(1)}, f32[2,16,2,512]{3,2,1,0:T(2,128)S(1)}, u32[]{:S(2)}, u32[]{:S(2)}) %collective-permute-start.8) | collective-permute-done | bytes 131104 | tf_op jit(solution)/shard_map/ppermute | solution.py:16
  92.7 0.8 add_add_fusion
  (58 shorter events, 1.7 us)
Async XLA Ops:
  1.0 21.3 %collective-permute-start = (bf16[2,16,2,512]{3,2,1,0:T(2,128)(2,1)S(1)}, bf16[2,16,2,512]{3,2,1,0:T(2,128)(2,1)S(1)}, u32[]{:S(2)}, u32[]{:S(2)}) collective-permute-start(bf16[2,16,2,512]{3,2,1,0:T(2,128)(2,1)S(1)} %convert_element_type.56), channel_id=1, source_target_pairs={{0,4},{1,5},{2,6},{3,7},{4,8},{5,9},{6,10},{7,11},{8,12},{9,13},{1... | collective-permute-start | bytes 196616 | tf_op jit(solution)/shard_map/ppermute | solution.py:16
  4.2 23.9 %collective-permute-start.1 = (bf16[2,16,2,512]{3,2,1,0:T(2,128)(2,1)S(1)}, bf16[2,16,2,512]{3,2,1,0:T(2,128)(2,1)S(1)}, u32[]{:S(2)}, u32[]{:S(2)}) collective-permute-start(bf16[2,16,2,512]{3,2,1,0:T(2,128)(2,1)S(1)} %convert_element_type.56), channel_id=1, source_target_pairs={{0,3},{1,4},{2,5},{3,6},{4,7},{5,8},{6,9},{7,10},{8,11},{9,12},{10... | collective-permute-start | bytes 196616 | tf_op jit(solution)/shard_map/ppermute | solution.py:16
  8.2 23.7 %collective-permute-start.2 = (bf16[2,16,2,512]{3,2,1,0:T(2,128)(2,1)S(1)}, bf16[2,16,2,512]{3,2,1,0:T(2,128)(2,1)S(1)}, u32[]{:S(2)}, u32[]{:S(2)}) collective-permute-start(bf16[2,16,2,512]{3,2,1,0:T(2,128)(2,1)S(1)} %convert_element_type.56), channel_id=1, source_target_pairs={{0,2},{1,3},{2,4},{3,5},{4,6},{5,7},{6,8},{7,9},{8,10},{9,11},{10,... | collective-permute-start | bytes 196616 | tf_op jit(solution)/shard_map/ppermute | solution.py:16
  11.4 22.7 %collective-permute-start.3 = (bf16[2,16,2,512]{3,2,1,0:T(2,128)(2,1)S(1)}, bf16[2,16,2,512]{3,2,1,0:T(2,128)(2,1)S(1)}, u32[]{:S(2)}, u32[]{:S(2)}) collective-permute-start(bf16[2,16,2,512]{3,2,1,0:T(2,128)(2,1)S(1)} %convert_element_type.56), channel_id=1, source_target_pairs={{0,1},{1,2},{2,3},{3,4},{4,5},{5,6},{6,7},{7,8},{8,9},{9,10},{10,1... | collective-permute-start | bytes 196616 | tf_op jit(solution)/shard_map/ppermute | solution.py:16
  14.2 22.4 %collective-permute-start.4 = (bf16[2,16,2,512]{3,2,1,0:T(2,128)(2,1)S(1)}, bf16[2,16,2,512]{3,2,1,0:T(2,128)(2,1)S(1)}, u32[]{:S(2)}, u32[]{:S(2)}) collective-permute-start(bf16[2,16,2,512]{3,2,1,0:T(2,128)(2,1)S(1)} %convert_element_type.56), channel_id=1, source_target_pairs={{1,0},{2,1},{3,2},{4,3},{5,4},{6,5},{7,6},{8,7},{9,8},{10,9},{11,1... | collective-permute-start | bytes 196616 | tf_op jit(solution)/shard_map/ppermute | solution.py:16
  18.0 3.7 %copy-start.9 = (s32[8]{0:T(128)S(1)}, s32[8]{0:T(128)}, u32[]{:S(2)}) copy-start(s32[8]{0:T(128)} %param.10) | copy-start | bytes 100
  18.0 3.7 %copy-start.6 = (s32[8,4]{0,1:T(4,128)S(1)}, s32[8,4]{0,1:T(4,128)}, u32[]{:S(2)}) copy-start(s32[8,4]{0,1:T(4,128)} %param.12) | copy-start | bytes 388
  18.0 3.9 %copy-start.8 = (s32[8]{0:T(128)S(1)}, s32[8]{0:T(128)}, u32[]{:S(2)}) copy-start(s32[8]{0:T(128)} %param.13) | copy-start | bytes 100
  18.1 3.9 %copy-start.7 = (s32[8,4]{0,1:T(4,128)S(1)}, s32[8,4]{0,1:T(4,128)}, u32[]{:S(2)}) copy-start(s32[8,4]{0,1:T(4,128)} %param.11) | copy-start | bytes 388
  18.1 18.4 %copy-start = (f32[2,16,2,512]{3,2,1,0:T(2,128)S(1)}, f32[2,16,2,512]{3,2,1,0:T(2,128)}, u32[]{:S(2)}) copy-start(f32[2,16,2,512]{3,2,1,0:T(2,128)} %param.7) | copy-start | bytes 393220
  21.7 18.0 %copy-start.1 = (bf16[1,2,512,896]{3,2,1,0:T(8,128)(2,1)}, bf16[1,2,512,896]{3,2,1,0:T(8,128)(2,1)S(1)}, u32[]{:S(2)}) copy-start(bf16[1,2,512,896]{3,2,1,0:T(8,128)(2,1)S(1)} %get-tuple-element.8) | copy-start | bytes 5505028
  22.2 16.4 %collective-permute-start.5 = (bf16[2,16,2,512]{3,2,1,0:T(2,128)(2,1)S(1)}, bf16[2,16,2,512]{3,2,1,0:T(2,128)(2,1)S(1)}, u32[]{:S(2)}, u32[]{:S(2)}) collective-permute-start(bf16[2,16,2,512]{3,2,1,0:T(2,128)(2,1)S(1)} %convert_element_type.56), channel_id=1, source_target_pairs={{2,0},{3,1},{4,2},{5,3},{6,4},{7,5},{8,6},{9,7},{10,8},{11,9},{12,... | collective-permute-start | bytes 196616 | tf_op jit(solution)/shard_map/ppermute | solution.py:16
  28.0 10.7 %collective-permute-start.6 = (bf16[2,16,2,512]{3,2,1,0:T(2,128)(2,1)S(1)}, bf16[2,16,2,512]{3,2,1,0:T(2,128)(2,1)S(1)}, u32[]{:S(2)}, u32[]{:S(2)}) collective-permute-start(bf16[2,16,2,512]{3,2,1,0:T(2,128)(2,1)S(1)} %convert_element_type.56), channel_id=1, source_target_pairs={{3,0},{4,1},{5,2},{6,3},{7,4},{8,5},{9,6},{10,7},{11,8},{12,9},{13... | collective-permute-start | bytes 196616 | tf_op jit(solution)/shard_map/ppermute | solution.py:16
  31.9 6.9 %collective-permute-start.7 = (bf16[2,16,2,512]{3,2,1,0:T(2,128)(2,1)S(1)}, bf16[2,16,2,512]{3,2,1,0:T(2,128)(2,1)S(1)}, u32[]{:S(2)}, u32[]{:S(2)}) collective-permute-start(bf16[2,16,2,512]{3,2,1,0:T(2,128)(2,1)S(1)} %convert_element_type.56), channel_id=1, source_target_pairs={{4,0},{5,1},{6,2},{7,3},{8,4},{9,5},{10,6},{11,7},{12,8},{13,9},{1... | collective-permute-start | bytes 196616 | tf_op jit(solution)/shard_map/ppermute | solution.py:16
  34.1 35.8 %collective-permute-start.16 = (f32[1,2,512]{2,1,0:T(2,128)S(1)}, f32[1,2,512]{2,1,0:T(2,128)S(1)}, u32[]{:S(2)}, u32[]{:S(2)}) collective-permute-start(f32[1,2,512]{2,1,0:T(2,128)S(1)} %get-tuple-element.20), channel_id=1, source_target_pairs={{0,1},{1,2},{2,3},{3,4},{4,5},{5,6},{6,7},{7,8},{8,9},{9,10},{10,1... | collective-permute-start | bytes 12296 | tf_op jit(solution)/shard_map/ppermute | solution.py:24
  36.6 36.5 %collective-permute-start.17 = (f32[1,2,512]{2,1,0:T(2,128)S(1)}, f32[1,2,512]{2,1,0:T(2,128)S(1)}, u32[]{:S(2)}, u32[]{:S(2)}) collective-permute-start(f32[1,2,512]{2,1,0:T(2,128)S(1)} %get-tuple-element.21), channel_id=1, source_target_pairs={{1,0},{2,1},{3,2},{4,3},{5,4},{6,5},{7,6},{8,7},{9,8},{10,9},{11,1... | collective-permute-start | bytes 12296 | tf_op jit(solution)/shard_map/ppermute | solution.py:27
  39.0 1.5 %copy-start.3 = (bf16[1,2,512,896]{3,2,1,0:T(8,128)(2,1)S(1)}, bf16[1,2,512,896]{3,2,1,0:T(8,128)(2,1)}, u32[]{:S(2)}) copy-start(bf16[1,2,512,896]{3,2,1,0:T(8,128)(2,1)} %get-tuple-element.7) | copy-start | bytes 5505028
  45.0 1.8 %copy-start.5 = (bf16[8,64,896]{2,1,0:T(8,128)(2,1)S(1)}, bf16[8,64,896]{2,1,0:T(8,128)(2,1)}, u32[]{:S(2)}) copy-start(bf16[8,64,896]{2,1,0:T(8,128)(2,1)} %param.9) | copy-start | bytes 2752516
  49.2 1.5 %copy-start.4 = (bf16[1,2,512,896]{3,2,1,0:T(8,128)(2,1)S(1)}, bf16[1,2,512,896]{3,2,1,0:T(8,128)(2,1)}, u32[]{:S(2)}) copy-start(bf16[1,2,512,896]{3,2,1,0:T(8,128)(2,1)} %get-tuple-element.7) | copy-start | bytes 5505028
  50.7 1.5 %copy-start.2 = (bf16[1,2,512,896]{3,2,1,0:T(8,128)(2,1)S(1)}, bf16[1,2,512,896]{3,2,1,0:T(8,128)(2,1)}, u32[]{:S(2)}) copy-start(bf16[1,2,512,896]{3,2,1,0:T(8,128)(2,1)} %copy-done.1) | copy-start | bytes 5505028
  58.8 16.2 %collective-permute-start.15 = (f32[2,16,2,512]{3,2,1,0:T(2,128)S(1)}, f32[2,16,2,512]{3,2,1,0:T(2,128)S(1)}, u32[]{:S(2)}, u32[]{:S(2)}) collective-permute-start(f32[2,16,2,512]{3,2,1,0:T(2,128)S(1)} %squeeze.45), channel_id=1, source_target_pairs={{0,4},{1,5},{2,6},{3,7},{4,8},{5,9},{6,10},{7,11},{8,12},{9,13},{1... | collective-permute-start | bytes 393224 | tf_op jit(solution)/shard_map/ppermute | solution.py:16
  62.1 18.9 %collective-permute-start.14 = (f32[2,16,2,512]{3,2,1,0:T(2,128)S(1)}, f32[2,16,2,512]{3,2,1,0:T(2,128)S(1)}, u32[]{:S(2)}, u32[]{:S(2)}) collective-permute-start(f32[2,16,2,512]{3,2,1,0:T(2,128)S(1)} %squeeze.44), channel_id=1, source_target_pairs={{0,3},{1,4},{2,5},{3,6},{4,7},{5,8},{6,9},{7,10},{8,11},{9,12},{10... | collective-permute-start | bytes 393224 | tf_op jit(solution)/shard_map/ppermute | solution.py:16
  66.8 19.3 %collective-permute-start.13 = (f32[2,16,2,512]{3,2,1,0:T(2,128)S(1)}, f32[2,16,2,512]{3,2,1,0:T(2,128)S(1)}, u32[]{:S(2)}, u32[]{:S(2)}) collective-permute-start(f32[2,16,2,512]{3,2,1,0:T(2,128)S(1)} %squeeze.43), channel_id=1, source_target_pairs={{0,2},{1,3},{2,4},{3,5},{4,6},{5,7},{6,8},{7,9},{8,10},{9,11},{10,... | collective-permute-start | bytes 393224 | tf_op jit(solution)/shard_map/ppermute | solution.py:16
  69.9 20.1 %collective-permute-start.12 = (f32[2,16,2,512]{3,2,1,0:T(2,128)S(1)}, f32[2,16,2,512]{3,2,1,0:T(2,128)S(1)}, u32[]{:S(2)}, u32[]{:S(2)}) collective-permute-start(f32[2,16,2,512]{3,2,1,0:T(2,128)S(1)} %squeeze.42), channel_id=1, source_target_pairs={{0,1},{1,2},{2,3},{3,4},{4,5},{5,6},{6,7},{7,8},{8,9},{9,10},{10,1... | collective-permute-start | bytes 393224 | tf_op jit(solution)/shard_map/ppermute | solution.py:16
  73.0 17.0 %collective-permute-start.11 = (f32[2,16,2,512]{3,2,1,0:T(2,128)S(1)}, f32[2,16,2,512]{3,2,1,0:T(2,128)S(1)}, u32[]{:S(2)}, u32[]{:S(2)}) collective-permute-start(f32[2,16,2,512]{3,2,1,0:T(2,128)S(1)} %squeeze.41), channel_id=1, source_target_pairs={{1,0},{2,1},{3,2},{4,3},{5,4},{6,5},{7,6},{8,7},{9,8},{10,9},{11,1... | collective-permute-start | bytes 393224 | tf_op jit(solution)/shard_map/ppermute | solution.py:16
  75.0 15.0 %collective-permute-start.10 = (f32[2,16,2,512]{3,2,1,0:T(2,128)S(1)}, f32[2,16,2,512]{3,2,1,0:T(2,128)S(1)}, u32[]{:S(2)}, u32[]{:S(2)}) collective-permute-start(f32[2,16,2,512]{3,2,1,0:T(2,128)S(1)} %squeeze.40), channel_id=1, source_target_pairs={{2,0},{3,1},{4,2},{5,3},{6,4},{7,5},{8,6},{9,7},{10,8},{11,9},{12,... | collective-permute-start | bytes 393224 | tf_op jit(solution)/shard_map/ppermute | solution.py:16
  81.1 9.0 %collective-permute-start.9 = (f32[2,16,2,512]{3,2,1,0:T(2,128)S(1)}, f32[2,16,2,512]{3,2,1,0:T(2,128)S(1)}, u32[]{:S(2)}, u32[]{:S(2)}) collective-permute-start(f32[2,16,2,512]{3,2,1,0:T(2,128)S(1)} %squeeze.39), channel_id=1, source_target_pairs={{3,0},{4,1},{5,2},{6,3},{7,4},{8,5},{9,6},{10,7},{11,8},{12,9},{13... | collective-permute-start | bytes 393224 | tf_op jit(solution)/shard_map/ppermute | solution.py:16
  86.1 6.6 %collective-permute-start.8 = (f32[2,16,2,512]{3,2,1,0:T(2,128)S(1)}, f32[2,16,2,512]{3,2,1,0:T(2,128)S(1)}, u32[]{:S(2)}, u32[]{:S(2)}) collective-permute-start(f32[2,16,2,512]{3,2,1,0:T(2,128)S(1)} %squeeze.38), channel_id=1, source_target_pairs={{4,0},{5,1},{6,2},{7,3},{8,4},{9,5},{10,6},{11,7},{12,8},{13,9},{1... | collective-permute-start | bytes 393224 | tf_op jit(solution)/shard_map/ppermute | solution.py:16
where the time goes:
time: 95.3 us; the launch traced here: 93.5 us
  starting transfers between devices  60.4 us (63%)
  local copies, waits for them, and re-layouts  13.1 us (14%)
  matrix products  11.7 us (12%)
  other arithmetic  5.06 us (5%)
  waiting for transfers between devices  2.71 us (3%)
    ppermute x16, starting transfers between devices, passed_along(): return lax.ppermute(shard, axis, pairs)  56 us
    dot_general x2, matrix products, shards(): lax.dot_general(masked, tables[table], (((1,), (1,)), ((), ())), preferre...  3.91 us
    slice x1, local copies, waits for them, and re-layouts, shards(): tables[table]  3.64 us
    unnamed x30, local copies, waits for them, and re-layouts  2.97 us
    ppermute x16, waiting for transfers between devices, passed_along(): return lax.ppermute(shard, axis, pairs)  2.7 us
    ppermute x1, starting transfers between devices, padded_2(): lax.ppermute(lax.slice_in_dim(block, block.shape[dim] - width, None, axis...  2.31 us
    dot_general x1, matrix products, shards(): jnp.einsum('vkir,vkic->vrc', placing, gathered, precision=highest, prefer...  2.29 us
    ppermute x1, starting transfers between devices, padded_2(): lax.ppermute(lax.slice_in_dim(block, 0, width, axis=dim), axis, backward)  2.01 us
  transfers between devices with their start and end apart: 18, of which 1 were waited for; matrix products, arithmetic and copies ran while one was open for 28% of the time, Pallas kernels for 0%

commit v1 on v0

v1 whole, which is shorter than its diff:
```python
import functools

import jax
import jax.numpy as jnp
from jax import lax
from jax.experimental import pallas as pl
from jax.experimental.pallas import tpu as pltpu
from jax.sharding import PartitionSpec as P

AXES = ("grp", "view")
DELTA = 0.5
PRIOR_WEIGHT = 2.0
CHUNK_PAIRS = 16


def both_ways(pairs):
    return pairs + [(b, a) for a, b in pairs]


def exchange_pairs(devices):
    chips = devices // 2
    swap = [(i, i ^ 1) for i in range(devices)]
    edge_y = [(i, i + 1) for i in range(0, chips, 2)]
    edge_d = [(i, i + 1) for i in range(1, chips - 1, 2)]
    edge_a = [(i + j, i + j + 2) for i in range(0, chips, 4) for j in (0, 1)]
    edge_b = [(i + j, i + j + 2) for i in range(2, chips - 2, 4) for j in (0, 1)]
    on_core = lambda edges, core: [(2 * a + core, 2 * b + core) for a, b in edges]
    last = devices - 1
    ends = [(0, 1), (1, 2), (2, 0), (last, last - 1), (last - 1, last - 3), (last - 3, last)]
    first = both_ways(on_core(edge_b, 0) + on_core(edge_d, 1)) + ends
    second = both_ways(on_core(edge_y, 0) + on_core(edge_a, 1))
    return swap, first, second


def pack_kernel(vol_ref, out_ref):
    slices = vol_ref.shape[0]
    row = vol_ref.shape[2]
    for y in range(vol_ref.shape[1]):
        cols = slice(y * row, (y + 1) * row)
        plane = vol_ref[:, y, :]
        high = plane.astype(jnp.bfloat16)
        rest = plane - high.astype(jnp.float32)
        mid = rest.astype(jnp.bfloat16)
        low = (rest - mid.astype(jnp.float32)).astype(jnp.bfloat16)
        out_ref[0:slices, cols] = high
        mid = mid.astype(jnp.float32)
        low = low.astype(jnp.float32)
        spare = jnp.concatenate(
            [
                mid[0:1],
                low[0:1],
                mid[slices - 1 : slices],
                low[slices - 1 : slices],
                jnp.zeros((4, row), jnp.float32),
            ],
            axis=0,
        )
        out_ref[slices : slices + 8, cols] = spare.astype(jnp.bfloat16)


def project_kernel(
    rows_ref,
    offset_ref,
    count_ref,
    angle_ref,
    own_ref,
    other_ref,
    near_ref,
    far_ref,
    table_ref,
    measured_ref,
    keep_ref,
    give_ref,
    window,
    table_proj,
    sino,
    picked,
    spread,
    grad,
    pos_ref,
):
    views, det_rows, channels = measured_ref.shape
    tables = table_ref.shape[0]
    slots = offset_ref.shape[1]
    slab = 16
    win_rows = window.shape[0]
    part = own_ref.shape[0] - 8
    piece = 2 * part
    window[0:piece, :] = near_ref[0:piece, :]
    window[piece : 2 * piece, :] = near_ref[piece + 8 : 2 * piece + 8, :]
    window[2 * piece : 3 * piece, :] = far_ref[0:piece, :]
    window[3 * piece : 4 * piece, :] = far_ref[piece + 8 : 2 * piece + 8, :]
    window[4 * piece : 4 * piece + part, :] = own_ref[0:part, :]
    window[4 * piece + part : 5 * piece, :] = other_ref[0:part, :]

    sino[...] = jnp.zeros_like(sino)
    grad[...] = jnp.zeros_like(grad)

    def count_table(view, total):
        return total + jnp.where(angle_ref[view] == 0, count_ref[view], 0)

    first_pairs = lax.fori_loop(0, views, count_table, 0)
    first_chunks = (first_pairs + CHUNK_PAIRS - 1) // CHUNK_PAIRS

    def forward(table, carry):
        table_proj[pl.ds(pl.multiple_of(table * win_rows, 16), win_rows), :] = jnp.dot(
            window[...], table_ref[table], preferred_element_type=jnp.float32
        )
        return carry

    lax.fori_loop(0, tables, forward, 0)

    def place(view, carry):
        base = angle_ref[view] * win_rows
        for slot in range(slots):

            @pl.when(slot < count_ref[view])
            def _():
                source = pl.multiple_of(base + rows_ref[view, slot], slab)
                target = view * det_rows + offset_ref[view, slot]
                for lane in range(0, channels, 128):
                    sino[lane // 128, pl.ds(target, slab), :] += table_proj[
                        pl.ds(source, slab), lane : lane + 128
                    ]

        return carry

    lax.fori_loop(0, views, place, 0)

    def weigh(view, carry):
        here = pl.ds(pl.multiple_of(view * det_rows, det_rows), det_rows)
        for lane in range(0, channels, 128):
            seen = measured_ref[view, :, lane : lane + 128].astype(jnp.float32)
            value = jnp.exp(-seen) * (sino[lane // 128, here, :] - seen)
            sino[lane // 128, here, :] = value.astype(jnp.bfloat16).astype(jnp.float32)
        return carry

    lax.fori_loop(0, views, weigh, 0)

    def pick(view, carry):
        zero_next, one_next = carry
        is_one = angle_ref[view] != 0
        start = jnp.where(is_one, one_next, zero_next)
        for slot in range(slots):

            @pl.when(slot < count_ref[view])
            def _():
                place_at = start + slot
                pos_ref[view * slots + slot] = place_at
                source = view * det_rows + offset_ref[view, slot]
                target = pl.multiple_of(place_at * slab, slab)
                for lane in range(0, channels, 128):
                    picked[pl.ds(target, slab), lane : lane + 128] = sino[
                        lane // 128, pl.ds(source, slab), :
                    ].astype(jnp.bfloat16)

        taken = count_ref[view]
        return (
            zero_next + jnp.where(is_one, 0, taken),
            one_next + jnp.where(is_one, taken, 0),
        )

    _, end = lax.fori_loop(0, views, pick, (jnp.int32(0), first_chunks * CHUNK_PAIRS))
    chunks = (end + CHUNK_PAIRS - 1) // CHUNK_PAIRS
    chunk_rows = CHUNK_PAIRS * slab

    def backward(chunk, carry):
        here = pl.ds(pl.multiple_of(chunk * chunk_rows, chunk_rows), chunk_rows)
        table = jnp.where(chunk < first_chunks, 0, 1)
        spread[here, :] = lax.dot_general(
            picked[here, :],
            table_ref[table],
            (((1,), (1,)), ((), ())),
            preferred_element_type=jnp.float32,
        )
        return carry

    lax.fori_loop(0, chunks, backward, 0)

    def collect(view, carry):
        for slot in range(slots):

            @pl.when(slot < count_ref[view])
            def _():
                source = pl.multiple_of(pos_ref[view * slots + slot] * slab, slab)
                target = pl.multiple_of(rows_ref[view, slot], slab)
                grad[pl.ds(target, slab), :] += spread[pl.ds(source, slab), :]

        return carry

    lax.fori_loop(0, views, collect, 0)
    keep_ref[0 : 2 * piece, :] = grad[0 : 2 * piece, :]
    keep_ref[2 * piece : 2 * piece + part, :] = grad[4 * piece : 4 * piece + part, :]
    give_ref[0 : 2 * piece, :] = grad[2 * piece : 4 * piece, :]
    give_ref[2 * piece : 2 * piece + part, :] = grad[4 * piece + part : 5 * piece, :]


def prior_kernel(scal_ref, vol_ref, own_ref, other_ref, near_ref, far_ref, out_ref):
    slices, strip, row = vol_ref.shape
    part = slices
    piece = 2 * part

    def halo(which, at):
        edge = 0 if which == 0 else part - 1

        def read(ref, base, tail):
            whole = ref[base + edge : base + edge + 1, :].astype(jnp.float32)
            more = ref[tail + 2 * which : tail + 2 * which + 2, :].astype(jnp.float32)
            return whole + more[0:1] + more[1:2]

        return read, at

    core = scal_ref[0]
    odd = scal_ref[1]
    has_low = scal_ref[2]
    has_high = scal_ref[3]
    step = piece + 8

    def piece_slice(which, exchange, via_me, via):
        qcore = 1 if which == 1 else 0
        sub = qcore ^ via
        ref = near_ref if via_me else far_ref
        base = exchange * step + sub * part
        tail = exchange * step + piece + 4 * sub
        read, _ = halo(which, None)
        return read(ref, base, tail)

    def other_slice(which):
        read, _ = halo(which, None)
        return read(other_ref, 0, part)

    def emit(low, high):
        for y in range(strip):
            cols = slice(y * row, (y + 1) * row)
            here = vol_ref[:, y, :]
            below = jnp.concatenate([low[:, cols], here[:-1]], axis=0)
            above = jnp.concatenate([here[1:], high[:, cols]], axis=0)
            iota = lax.broadcasted_iota(jnp.int32, here.shape, 0)
            down = jnp.clip(here - below, -DELTA, DELTA)
            down = jnp.where((iota > 0) | (has_low > 0), down, 0.0)
            up = jnp.clip(here - above, -DELTA, DELTA)
            up = jnp.where((iota < slices - 1) | (has_high > 0), up, 0.0)
            total = down + up
            if y > 0:
                total = total + jnp.clip(here - vol_ref[:, y - 1, :], -DELTA, DELTA)
            if y + 1 < strip:
                total = total + jnp.clip(here - vol_ref[:, y + 1, :], -DELTA, DELTA)
            lane = lax.broadcasted_iota(jnp.int32, here.shape, 1)
            left = jnp.clip(here - pltpu.roll(here, 1, 1), -DELTA, DELTA)
            total = total + jnp.where(lane > 0, left, 0.0)
            right = jnp.clip(here - pltpu.roll(here, row - 1, 1), -DELTA, DELTA)
            total = total + jnp.where(lane < row - 1, right, 0.0)
            out_ref[:, cols] = PRIOR_WEIGHT * total

    @pl.when((core == 0) & (odd == 0))
    def _():
        emit(piece_slice(1, 0, False, 1), other_slice(0))

    @pl.when((core == 0) & (odd == 1))
    def _():
        emit(piece_slice(1, 1, True, 0), other_slice(0))

    @pl.when((core == 1) & (odd == 0))
    def _():
        emit(other_slice(1), piece_slice(0, 1, False, 0))

    @pl.when((core == 1) & (odd == 1))
    def _():
        emit(other_slice(1), piece_slice(0, 0, True, 1))


def window_rows(cover, position, local_blocks, slab):
    core = position % 2
    chip = position // 2
    owner = cover // local_blocks
    owner_core = owner % 2
    delta = owner // 2 - chip
    nearer = jnp.abs(delta) == 1
    up = delta > 0
    is_y = up == (chip % 2 == 0)
    is_a = up == (chip % 4 < 2)
    second = jnp.where(nearer, is_y, is_a).astype(jnp.int32)
    via = jnp.where(nearer, jnp.where(is_y, 0, 1), jnp.where(is_a, 1, 0))
    part = local_blocks * slab
    away = ((via ^ core) * 2 + second) * 2 * part + (owner_core ^ via) * part
    here = 8 * part + (owner_core ^ core) * part
    return jnp.where(delta == 0, here, away) + (cover % local_blocks) * slab


def shards(volume, footprint, measured, angle_index, cover, offset, count):
    local_blocks, slab, strip, row = volume.shape
    views, det_rows, channels = measured.shape
    tables = footprint.shape[0]
    slots = cover.shape[1]
    plane = strip * row
    devices = lax.axis_size(AXES)
    position = lax.axis_index(AXES)
    core = position % 2
    swap, first, second = exchange_pairs(devices)
    send = lambda value, pairs: lax.ppermute(value, AXES, pairs)
    part = local_blocks * slab
    piece = 2 * part
    flat = volume.reshape(part, strip, row)
    vmem = pl.BlockSpec(memory_space=pltpu.VMEM)
    smem = pl.BlockSpec(memory_space=pltpu.SMEM)

    own = pl.pallas_call(
        pack_kernel,
        out_shape=jax.ShapeDtypeStruct((part + 8, plane), jnp.bfloat16),
        in_specs=[vmem],
        out_specs=vmem,
        name="pack",
    )(flat)
    other = send(own, swap)
    both = jnp.concatenate(
        [own[:part], other[:part], own[part : part + 4], other[part : part + 4]], axis=0
    )
    got_first = send(both, first)
    got_second = send(both, second)
    near = jnp.concatenate([got_first, got_second], axis=0)
    far = send(near, swap)

    rows = window_rows(cover, position, local_blocks, slab)
    keep, give = pl.pallas_call(
        project_kernel,
        out_shape=(
            jax.ShapeDtypeStruct((2 * piece + part, plane), jnp.float32),
            jax.ShapeDtypeStruct((2 * piece + part, plane), jnp.float32),
        ),
        in_specs=[smem] * 4 + [vmem] * 6,
        out_specs=(vmem, vmem),
        scratch_shapes=[
            pltpu.VMEM((5 * piece, plane), jnp.bfloat16),
            pltpu.VMEM((tables * 5 * piece, channels), jnp.float32),
            pltpu.VMEM((channels // 128, views * det_rows, 128), jnp.float32),
            pltpu.VMEM((views * slots * slab + CHUNK_PAIRS * slab, channels), jnp.bfloat16),
            pltpu.VMEM((views * slots * slab + CHUNK_PAIRS * slab, plane), jnp.float32),
            pltpu.VMEM((5 * piece, plane), jnp.float32),
            pltpu.SMEM((views * slots,), jnp.int32),
        ],
        compiler_params=pltpu.CompilerParams(vmem_limit_bytes=40 * 1024 * 1024),
        cost_estimate=pl.CostEstimate(flops=4_000_000_000, bytes_accessed=8_000_000, transcendentals=500_000),
        name="project",
    )(
        rows,
        offset,
        count,
        angle_index,
        own,
        other,
        near,
        far,
        footprint.reshape(tables, plane, channels),
        measured,
    )
    taken = send(give, swap)
    total = keep + taken
    wire = total[: 2 * piece].astype(jnp.bfloat16)
    back_first = send(wire[:piece], first)
    back_second = send(wire[piece:], second)

    scalars = jnp.stack(
        [
            core,
            (position // 2) % 2,
            (position > 0).astype(jnp.int32),
            (position < devices - 1).astype(jnp.int32),
        ]
    ).astype(jnp.int32)
    prior = pl.pallas_call(
        prior_kernel,
        out_shape=jax.ShapeDtypeStruct((part, plane), jnp.float32),
        in_specs=[smem] + [vmem] * 5,
        out_specs=vmem,
        name="prior",
        cost_estimate=pl.CostEstimate(flops=2_000_000, bytes_accessed=1_000_000, transcendentals=0),
    )(scalars, flat, own, other, near, far)

    arrived = back_first.astype(jnp.float32) + back_second.astype(jnp.float32)
    passed = send(arrived[part:], swap)
    data = total[2 * piece :] + arrived[:part] + passed
    return (data + prior).reshape(volume.shape)


def solution(mesh):
    in_specs = (
        P(AXES, None, None, None),
        P(AXES, None, None, None),
        P(AXES, None, None),
        P(AXES),
        P(AXES, None),
        P(AXES, None),
        P(AXES),
    )
    out_specs = P(AXES, None, None, None)
    return jax.shard_map(shards, mesh=mesh, in_specs=in_specs, out_specs=out_specs, check_vma=False)
```

time: 95.3 us -> 44 us (0.46); the launches traced: 93.5 us -> 43.9 us
  starting transfers between devices: 60.4 us -> 10.5 us
  matrix products: 11.7 us -> 0 us
  Pallas kernels: 0 us -> 9.94 us
  waiting for transfers between devices: 2.71 us -> 12.2 us
  local copies, waits for them, and re-layouts: 13.1 us -> 9.39 us
  other arithmetic: 5.06 us -> 1.69 us
    ppermute x18 -> x8, starting transfers between devices: 60.4 us -> 10.5 us  [shards(): send = lambda value, pairs: lax.ppermute(value, AXES, pairs)]
    dot_general x8 -> x0, matrix products: 11.7 us -> none  [the longest x2 3.91 us: shards(): lax.dot_general(masked, tables[table], (((1,), (1,)), ((), ())), preferre...]
    pallas_call x0 -> x3, Pallas kernels: none -> 9.94 us  [the longest x1 6.16 us: shards(): pl.pallas_call(project_kernel, out_shape=(jax.ShapeDtypeStruct((2 * piece...]
    ppermute x18 -> x8, waiting for transfers between devices: 2.71 us -> 12.2 us  [shards(): send = lambda value, pairs: lax.ppermute(value, AXES, pairs)]
    unnamed x30 -> x19, local copies, waits for them, and re-layouts: 2.97 us -> 7.01 us
    slice x3 -> x6, local copies, waits for them, and re-layouts: 4.74 us -> 1.61 us  [the longest x1 0.84 us: shards(): own[:part]]
    reshape x2 -> x1, local copies, waits for them, and re-layouts: 3.47 us -> 0.76 us  [shards(): return (data + prior).reshape(volume.shape)]
    squeeze x9 -> x0, local copies, waits for them, and re-layouts: 1.43 us -> none  [the longest x8 1.27 us: shards(): parts[REACH + step]]
  transfers between devices with their start and end apart: 18 -> 8, of which waited for: 1 -> 4; matrix products, arithmetic and copies ran while one was open for 28% -> 8% of each run, Pallas kernels for 0% -> 5%
where the time goes in v1:
time: 44 us; the launch traced here: 43.9 us
  waiting for transfers between devices  12.2 us (28%)
  starting transfers between devices  10.5 us (24%)
  Pallas kernels  9.94 us (23%)
  local copies, waits for them, and re-layouts  9.39 us (21%)
  other arithmetic  1.69 us (4%)
    ppermute x8, waiting for transfers between devices, shards(): send = lambda value, pairs: lax.ppermute(value, AXES, pairs)  12.2 us
    ppermute x8, starting transfers between devices, shards(): send = lambda value, pairs: lax.ppermute(value, AXES, pairs)  10.5 us
    unnamed x19, local copies, waits for them, and re-layouts  7.01 us
    pallas_call x1, Pallas kernels, shards(): pl.pallas_call(project_kernel, out_shape=(jax.ShapeDtypeStruct((2 * piece...  6.16 us
    pallas_call x1, Pallas kernels, shards(): pl.pallas_call(prior_kernel, out_shape=jax.ShapeDtypeStruct((part, plane)...  2.08 us
    pallas_call x1, Pallas kernels, shards(): pl.pallas_call(pack_kernel, out_shape=jax.ShapeDtypeStruct((part + 8, pla...  1.69 us
    add x1, other arithmetic, shards(): return (data + prior).reshape(volume.shape)  0.93 us
  transfers between devices with their start and end apart: 8, of which 4 were waited for; matrix products, arithmetic and copies ran while one was open for 8% of the time, Pallas kernels for 5%

profile of v1, /device:TPU:3, one launch (start us, length us, event | category | flops | bytes accessed | tf_op | source)
XLA Modules:
  0.0 43.9 jit_solution(14773793166299003504)
XLA Ops:
  0.0 1.7 %pack.1.own_ref = bf16[40,1024]{1,0:T(8,128)(2,1)} custom-call(f32[32,2,512]{2,1,0:T(2,128)} %bitcast.7), custom_call_target="tpu_custom_call" | custom-call | tf_op jit(solution)/shard_map/pack/pallas_call | solution.py:307
  1.7 0.7 %collective-permute-start = (bf16[40,1024]{1,0:T(8,128)(2,1)}, bf16[40,1024]{1,0:T(8,128)(2,1)S(1)}, u32[]{:S(2)}, u32[]{:S(2)}) collective-permute-start(bf16[40,1024]{1,0:T(8,128)(2,1)} %pack.1.own_ref), channel_id=1, source_target_pairs={{0,1},{1,0},{2,3},{3,2},{4,5},{5,4},{6,7},{7,6},{8,9},{9,8},{10,11... | collective-permute-start | bytes 245768 | tf_op jit(solution)/shard_map/ppermute | solution.py:300
  2.4 0.7 %slice.42 = bf16[4,1024]{1,0:T(4,128)(2,1)S(1)} slice(bf16[40,1024]{1,0:T(8,128)(2,1)} %pack.1.own_ref), slice={[32:36], [0:1024]} | slice | bytes 16384 | tf_op jit(solution)/shard_map/slice | solution.py:316
  3.1 0.8 %slice.40 = bf16[32,1024]{1,0:T(8,128)(2,1)S(1)} slice(bf16[40,1024]{1,0:T(8,128)(2,1)} %pack.1.own_ref), slice={[0:32], [0:1024]} | slice | bytes 131072 | tf_op jit(solution)/shard_map/slice | solution.py:316
  3.9 0.0 collective-permute-done.other_ref
  3.9 0.0 copy-start.2
  4.0 4.3 %collective-permute-start.1 = (bf16[72,1024]{1,0:T(8,128)(2,1)S(1)}, bf16[72,1024]{1,0:T(8,128)(2,1)S(1)}, u32[]{:S(2)}, u32[]{:S(2)}) collective-permute-start(bf16[72,1024]{1,0:T(8,128)(2,1)S(1)} %pad_maximum_fusion), channel_id=1, source_target_pairs={{4,8},{6,10},{12,16},{14,18},{20,24},{22,26},{3,5},{7,9},{11,13},{... | collective-permute-start | bytes 442376 | tf_op jit(solution)/shard_map/ppermute | solution.py:300
  8.3 0.0 collective-permute-start.2
  8.3 4.6 %collective-permute-done.1 = bf16[72,1024]{1,0:T(8,128)(2,1)S(1)} collective-permute-done((bf16[72,1024]{1,0:T(8,128)(2,1)S(1)}, bf16[72,1024]{1,0:T(8,128)(2,1)S(1)}, u32[]{:S(2)}, u32[]{:S(2)}) %collective-permute-start.1) | collective-permute-done | bytes 147488 | tf_op jit(solution)/shard_map/ppermute | solution.py:300
  12.9 0.1 collective-permute-done.2
  13.1 0.0 copy-start.1
  13.1 1.1 %collective-permute-start.3 = (bf16[144,1024]{1,0:T(8,128)(2,1)S(1)}, bf16[144,1024]{1,0:T(8,128)(2,1)S(1)}, u32[]{:S(2)}, u32[]{:S(2)}) collective-permute-start(bf16[144,1024]{1,0:T(8,128)(2,1)S(1)} %constant_dynamic-update-slice_fusion.near_ref), channel_id=1, source_target_pairs={{0,1},{1,0},{2,3},{3,2},{4,5},{5,4},{6,7},{7,6},{8,9},{9,8},{10,11... | collective-permute-start | bytes 884744 | tf_op jit(solution)/shard_map/ppermute | solution.py:300
  14.1 0.8 %copy.8 = s32[8,4]{1,0:T(8,128)S(1)} copy(s32[8,4]{0,1:T(4,128)} %param.11) | data formatting | bytes 256 | tf_op args[4]
  14.9 0.8 %copy.12.offset_ref = s32[8,4]{1,0:T(8,128)S(1)} copy(s32[8,4]{0,1:T(4,128)} %param.12) | data formatting | bytes 256 | tf_op args[5]
  15.7 0.0 collective-permute-done.3.far_ref
  15.7 0.0 copy-start.3
  15.7 0.0 copy-start
  15.7 0.9 %copy-done = bf16[40,1024]{1,0:T(8,128)(2,1)S(1)} copy-done((bf16[40,1024]{1,0:T(8,128)(2,1)S(1)}, bf16[40,1024]{1,0:T(8,128)(2,1)}, u32[]{:S(2)}) %copy-start) | copy-done | bytes 81944
  16.7 0.0 copy-start.4
  16.7 2.0 %copy-done.4 = bf16[2,2,512,896]{3,2,1,0:T(8,128)(2,1)S(1)} copy-done((bf16[2,2,512,896]{3,2,1,0:T(8,128)(2,1)S(1)}, bf16[2,2,512,896]{3,2,1,0:T(8,128)(2,1)}, u32[]{:S(2)}) %copy-start.4) | copy-done | bytes 3670040
  18.7 0.0 copy-start.5
  18.7 1.2 %copy-done.5 = bf16[8,64,896]{2,1,0:T(8,128)(2,1)S(1)} copy-done((bf16[8,64,896]{2,1,0:T(8,128)(2,1)S(1)}, bf16[8,64,896]{2,1,0:T(8,128)(2,1)}, u32[]{:S(2)}) %copy-start.5) | copy-done | bytes 917528
  19.9 0.0 copy-start.6
  19.9 0.7 %copy-done.6 = s32[8]{0:T(128)S(1)} copy-done((s32[8]{0:T(128)S(1)}, s32[8]{0:T(128)}, u32[]{:S(2)}) %copy-start.6) | copy-done | bytes 56
  20.5 0.0 copy-start.7
  20.5 0.7 %copy-done.7 = s32[8]{0:T(128)S(1)} copy-done((s32[8]{0:T(128)S(1)}, s32[8]{0:T(128)}, u32[]{:S(2)}) %copy-start.7) | copy-done | bytes 56
  21.2 6.2 %project.1 = (f32[160,1024]{1,0:T(8,128)S(1)}, f32[160,1024]{1,0:T(8,128)S(1)}) custom-call(s32[8,4]{1,0:T(8,128)S(1)} %fusion.4.rows_ref, s32[8,4]{1,0:T(8,128)S(1)} %copy.12.offset_ref, s32[8]{0:T(128)S(1)} %copy-done.6, s32[8]{0:T(128)S(1)} %copy-done.7, bf16[40,1024]{1,0:T(8,128)(2,1)S(1)} %copy-done, ...), custom_call_target="tpu_custom_call" | custom-call | flops 4000000000 | bytes 8000000 | tf_op jit(solution)/shard_map/project/pallas_call | solution.py:324
  27.4 0.0 copy-done.2
  27.4 0.0 copy-done.1
  27.4 0.0 copy-done.3
  27.4 0.1 collective-permute-start.4
  27.5 2.1 %collective-permute-done.4 = f32[160,1024]{1,0:T(8,128)S(1)} collective-permute-done((f32[160,1024]{1,0:T(8,128)S(1)}, f32[160,1024]{1,0:T(8,128)S(1)}, u32[]{:S(2)}, u32[]{:S(2)}) %collective-permute-start.4) | collective-permute-done | bytes 655392 | tf_op jit(solution)/shard_map/ppermute | solution.py:300
  29.6 0.1 fusion.7
  29.7 3.3 %collective-permute-start.5 = (bf16[64,1024]{1,0:T(8,128)(2,1)S(1)}, bf16[64,1024]{1,0:T(8,128)(2,1)S(1)}, u32[]{:S(2)}, u32[]{:S(2)}) collective-permute-start(bf16[64,1024]{1,0:T(8,128)(2,1)S(1)} %get-tuple-element.11), channel_id=1, source_target_pairs={{4,8},{6,10},{12,16},{14,18},{20,24},{22,26},{3,5},{7,9},{11,13},{... | collective-permute-start | bytes 393224 | tf_op jit(solution)/shard_map/ppermute | solution.py:300
  33.0 0.0 collective-permute-start.6
  33.0 5.4 %collective-permute-done.5 = bf16[64,1024]{1,0:T(8,128)(2,1)S(1)} collective-permute-done((bf16[64,1024]{1,0:T(8,128)(2,1)S(1)}, bf16[64,1024]{1,0:T(8,128)(2,1)S(1)}, u32[]{:S(2)}, u32[]{:S(2)}) %collective-permute-start.5) | collective-permute-done | bytes 131104 | tf_op jit(solution)/shard_map/ppermute | solution.py:300
  38.4 0.0 collective-permute-done.6
  38.5 1.0 %collective-permute-start.7 = (f32[32,1024]{1,0:T(8,128)S(1)}, f32[32,1024]{1,0:T(8,128)S(1)}, u32[]{:S(2)}, u32[]{:S(2)}) collective-permute-start(f32[32,1024]{1,0:T(8,128)S(1)} %slice.48), channel_id=1, source_target_pairs={{0,1},{1,0},{2,3},{3,2},{4,5},{5,4},{6,7},{7,6},{8,9},{9,8},{10,11... | collective-permute-start | bytes 393224 | tf_op jit(solution)/shard_map/ppermute | solution.py:300
  39.5 0.6 %pad_add_fusion.scal_ref = s32[4]{0:T(128)} fusion(s32[1]{0:T(128)} %bitcast.5, s32[1]{0:T(128)} %bitcast.4, s32[1]{0:T(128)} %bitcast.3, s32[1]{0:T(128)} %bitcast.2), kind=kLoop, calls=%fused_computation.25 | loop fusion | flops 12 | bytes 32 | tf_op jit(solution)/shard_map/stack | solution.py:362
  40.1 2.1 %prior.1 = f32[32,1024]{1,0:T(8,128)} custom-call(s32[4]{0:T(128)} %pad_add_fusion.scal_ref, f32[32,2,512]{2,1,0:T(2,128)} %bitcast.8, bf16[40,1024]{1,0:T(8,128)(2,1)} %pack.1.own_ref, bf16[40,1024]{1,0:T(8,128)(2,1)} %copy-done.2, bf16[144,1024]{1,0:T(8,128)(2,1)} %copy-done.1, bf16[144,1024]{1,0:T(8,128)(2,1)} %copy-done.3), custom_call_target="tpu_custom_call" | custom-call | flops 2000000 | bytes 1000000 | tf_op jit(solution)/shard_map/prior/pallas_call | solution.py:370
  42.2 0.0 collective-permute-done.7
  42.2 0.9 %fusion.1 = f32[32,1024]{1,0:T(8,128)S(1)} fusion(f32[32,1024]{1,0:T(8,128)} %prior.1, f32[32,1024]{1,0:T(8,128)S(1)} %collective-permute-done.7, f32[64,1024]{1,0:T(8,128)S(1)} %convert_add_fusion, f32[160,1024]{1,0:T(8,128)S(1)} %get-tuple-element.10), kind=kLoop, calls=%fused_computation.4 | loop fusion | flops 98304 | bytes 655360 | tf_op jit(solution)/shard_map/add | solution.py:382
  43.1 0.8 %reshape.11 = f32[2,16,2,512]{3,2,1,0:T(2,128)} reshape(f32[32,1024]{1,0:T(8,128)S(1)} %fusion.1) | data formatting | bytes 262144 | tf_op jit(solution)/shard_map/reshape | solution.py:382
  (9 shorter events, 0.1 us)
Async XLA Ops:
  1.7 2.2 %collective-permute-start = (bf16[40,1024]{1,0:T(8,128)(2,1)}, bf16[40,1024]{1,0:T(8,128)(2,1)S(1)}, u32[]{:S(2)}, u32[]{:S(2)}) collective-permute-start(bf16[40,1024]{1,0:T(8,128)(2,1)} %pack.1.own_ref), channel_id=1, source_target_pairs={{0,1},{1,0},{2,3},{3,2},{4,5},{5,4},{6,7},{7,6},{8,9},{9,8},{10,11... | collective-permute-start | bytes 245768 | tf_op jit(solution)/shard_map/ppermute | solution.py:300
  3.9 23.4 %copy-start.2 = (bf16[40,1024]{1,0:T(8,128)(2,1)}, bf16[40,1024]{1,0:T(8,128)(2,1)S(1)}, u32[]{:S(2)}) copy-start(bf16[40,1024]{1,0:T(8,128)(2,1)S(1)} %collective-permute-done.other_ref) | copy-start | bytes 245764
  4.0 8.9 %collective-permute-start.1 = (bf16[72,1024]{1,0:T(8,128)(2,1)S(1)}, bf16[72,1024]{1,0:T(8,128)(2,1)S(1)}, u32[]{:S(2)}, u32[]{:S(2)}) collective-permute-start(bf16[72,1024]{1,0:T(8,128)(2,1)S(1)} %pad_maximum_fusion), channel_id=1, source_target_pairs={{4,8},{6,10},{12,16},{14,18},{20,24},{22,26},{3,5},{7,9},{11,13},{... | collective-permute-start | bytes 442376 | tf_op jit(solution)/shard_map/ppermute | solution.py:300
  8.3 4.8 %collective-permute-start.2 = (bf16[72,1024]{1,0:T(8,128)(2,1)S(1)}, bf16[72,1024]{1,0:T(8,128)(2,1)S(1)}, u32[]{:S(2)}, u32[]{:S(2)}) collective-permute-start(bf16[72,1024]{1,0:T(8,128)(2,1)S(1)} %pad_maximum_fusion), channel_id=1, source_target_pairs={{0,2},{4,6},{8,10},{12,14},{16,18},{20,22},{24,26},{28,30},{1,5},{... | collective-permute-start | bytes 442376 | tf_op jit(solution)/shard_map/ppermute | solution.py:300
  13.1 14.3 %copy-start.1 = (bf16[144,1024]{1,0:T(8,128)(2,1)}, bf16[144,1024]{1,0:T(8,128)(2,1)S(1)}, u32[]{:S(2)}) copy-start(bf16[144,1024]{1,0:T(8,128)(2,1)S(1)} %constant_dynamic-update-slice_fusion.near_ref) | copy-start | bytes 884740
  13.1 2.6 %collective-permute-start.3 = (bf16[144,1024]{1,0:T(8,128)(2,1)S(1)}, bf16[144,1024]{1,0:T(8,128)(2,1)S(1)}, u32[]{:S(2)}, u32[]{:S(2)}) collective-permute-start(bf16[144,1024]{1,0:T(8,128)(2,1)S(1)} %constant_dynamic-update-slice_fusion.near_ref), channel_id=1, source_target_pairs={{0,1},{1,0},{2,3},{3,2},{4,5},{5,4},{6,7},{7,6},{8,9},{9,8},{10,11... | collective-permute-start | bytes 884744 | tf_op jit(solution)/shard_map/ppermute | solution.py:300
  15.7 11.7 %copy-start.3 = (bf16[144,1024]{1,0:T(8,128)(2,1)}, bf16[144,1024]{1,0:T(8,128)(2,1)S(1)}, u32[]{:S(2)}) copy-start(bf16[144,1024]{1,0:T(8,128)(2,1)S(1)} %collective-permute-done.3.far_ref) | copy-start | bytes 884740
  15.7 1.0 %copy-start = (bf16[40,1024]{1,0:T(8,128)(2,1)S(1)}, bf16[40,1024]{1,0:T(8,128)(2,1)}, u32[]{:S(2)}) copy-start(bf16[40,1024]{1,0:T(8,128)(2,1)} %pack.1.own_ref) | copy-start | bytes 245764
  16.7 2.0 %copy-start.4 = (bf16[2,2,512,896]{3,2,1,0:T(8,128)(2,1)S(1)}, bf16[2,2,512,896]{3,2,1,0:T(8,128)(2,1)}, u32[]{:S(2)}) copy-start(bf16[2,2,512,896]{3,2,1,0:T(8,128)(2,1)} %param.8) | copy-start | bytes 11010052
  18.7 1.2 %copy-start.5 = (bf16[8,64,896]{2,1,0:T(8,128)(2,1)S(1)}, bf16[8,64,896]{2,1,0:T(8,128)(2,1)}, u32[]{:S(2)}) copy-start(bf16[8,64,896]{2,1,0:T(8,128)(2,1)} %measured_ref.1) | copy-start | bytes 2752516
  19.9 0.7 %copy-start.6 = (s32[8]{0:T(128)S(1)}, s32[8]{0:T(128)}, u32[]{:S(2)}) copy-start(s32[8]{0:T(128)} %count_ref.1) | copy-start | bytes 100
  20.5 0.7 %copy-start.7 = (s32[8]{0:T(128)S(1)}, s32[8]{0:T(128)}, u32[]{:S(2)}) copy-start(s32[8]{0:T(128)} %angle_ref.1) | copy-start | bytes 100
  27.4 2.2 %collective-permute-start.4 = (f32[160,1024]{1,0:T(8,128)S(1)}, f32[160,1024]{1,0:T(8,128)S(1)}, u32[]{:S(2)}, u32[]{:S(2)}) collective-permute-start(f32[160,1024]{1,0:T(8,128)S(1)} %get-tuple-element.8), channel_id=1, source_target_pairs={{0,1},{1,0},{2,3},{3,2},{4,5},{5,4},{6,7},{7,6},{8,9},{9,8},{10,11... | collective-permute-start | bytes 1966088 | tf_op jit(solution)/shard_map/ppermute | solution.py:300
  29.7 8.8 %collective-permute-start.5 = (bf16[64,1024]{1,0:T(8,128)(2,1)S(1)}, bf16[64,1024]{1,0:T(8,128)(2,1)S(1)}, u32[]{:S(2)}, u32[]{:S(2)}) collective-permute-start(bf16[64,1024]{1,0:T(8,128)(2,1)S(1)} %get-tuple-element.11), channel_id=1, source_target_pairs={{4,8},{6,10},{12,16},{14,18},{20,24},{22,26},{3,5},{7,9},{11,13},{... | collective-permute-start | bytes 393224 | tf_op jit(solution)/shard_map/ppermute | solution.py:300
  33.0 5.4 %collective-permute-start.6 = (bf16[64,1024]{1,0:T(8,128)(2,1)S(1)}, bf16[64,1024]{1,0:T(8,128)(2,1)S(1)}, u32[]{:S(2)}, u32[]{:S(2)}) collective-permute-start(bf16[64,1024]{1,0:T(8,128)(2,1)S(1)} %get-tuple-element.12), channel_id=1, source_target_pairs={{0,2},{4,6},{8,10},{12,14},{16,18},{20,22},{24,26},{28,30},{1,5},{... | collective-permute-start | bytes 393224 | tf_op jit(solution)/shard_map/ppermute | solution.py:300
  38.5 3.7 %collective-permute-start.7 = (f32[32,1024]{1,0:T(8,128)S(1)}, f32[32,1024]{1,0:T(8,128)S(1)}, u32[]{:S(2)}, u32[]{:S(2)}) collective-permute-start(f32[32,1024]{1,0:T(8,128)S(1)} %slice.48), channel_id=1, source_target_pairs={{0,1},{1,0},{2,3},{3,2},{4,5},{5,4},{6,7},{7,6},{8,9},{9,8},{10,11... | collective-permute-start | bytes 393224 | tf_op jit(solution)/shard_map/ppermute | solution.py:300

commit v2 on v1

v2 whole, which is shorter than its diff:
```python
import functools

import jax
import jax.numpy as jnp
from jax import lax
from jax.experimental import pallas as pl
from jax.experimental.pallas import tpu as pltpu
from jax.sharding import PartitionSpec as P

AXES = ("grp", "view")
DELTA = 0.5
PRIOR_WEIGHT = 2.0
CHUNK_PAIRS = 16


def both_ways(pairs):
    return pairs + [(b, a) for a, b in pairs]


def exchange_pairs(devices):
    chips = devices // 2
    swap = [(i, i ^ 1) for i in range(devices)]
    edge_y = [(i, i + 1) for i in range(0, chips, 2)]
    edge_d = [(i, i + 1) for i in range(1, chips - 1, 2)]
    edge_a = [(i + j, i + j + 2) for i in range(0, chips, 4) for j in (0, 1)]
    edge_b = [(i + j, i + j + 2) for i in range(2, chips - 2, 4) for j in (0, 1)]
    on_core = lambda edges, core: [(2 * a + core, 2 * b + core) for a, b in edges]
    last = devices - 1
    ends = [(0, 1), (1, 2), (2, 0), (last, last - 1), (last - 1, last - 3), (last - 3, last)]
    first = both_ways(on_core(edge_b, 0) + on_core(edge_d, 1)) + ends
    second = both_ways(on_core(edge_y, 0) + on_core(edge_a, 1))
    return swap, first, second


def pack_kernel(vol_ref, out_ref):
    slices, strip, row = vol_ref.shape
    for y in range(strip):
        cols = slice(y * row, (y + 1) * row)
        plane = vol_ref[:, y, :]
        high = plane.astype(jnp.bfloat16)
        rest = plane - high.astype(jnp.float32)
        mid = rest.astype(jnp.bfloat16).astype(jnp.float32)
        low = rest - mid
        out_ref[0:slices, cols] = high
        spare = jnp.concatenate(
            [
                mid[0:1],
                low[0:1],
                mid[slices - 1 : slices],
                low[slices - 1 : slices],
                jnp.zeros((4, row), jnp.float32),
            ],
            axis=0,
        )
        out_ref[slices : slices + 8, cols] = spare.astype(jnp.bfloat16)


def join_kernel(own_ref, other_ref, out_ref):
    part = own_ref.shape[0] - 8
    out_ref[0:part, :] = own_ref[0:part, :]
    out_ref[part : 2 * part, :] = other_ref[0:part, :]
    mine = own_ref[part : part + 8, :].astype(jnp.float32)
    theirs = other_ref[part : part + 8, :].astype(jnp.float32)
    spare = jnp.concatenate([mine[0:4], theirs[0:4]], axis=0)
    out_ref[2 * part : 2 * part + 8, :] = spare.astype(jnp.bfloat16)


def early_kernel(own_ref, other_ref, table_ref, measured_ref, proj_ref, decay_ref, window):
    views, det_rows, channels = measured_ref.shape
    tables = table_ref.shape[0]
    part = own_ref.shape[0] - 8
    window[0:part, :] = own_ref[0:part, :]
    window[part : 2 * part, :] = other_ref[0:part, :]

    def forward(table, carry):
        here = pl.ds(pl.multiple_of(table * 2 * part, 16), 2 * part)
        proj_ref[here, :] = jnp.dot(
            window[...], table_ref[table], preferred_element_type=jnp.float32
        )
        return carry

    lax.fori_loop(0, tables, forward, 0)

    def fade(view, carry):
        here = pl.ds(pl.multiple_of(view * det_rows, det_rows), det_rows)
        for lane in range(0, channels, 128):
            seen = measured_ref[view, :, lane : lane + 128].astype(jnp.float32)
            decay_ref[lane // 128, here, :] = jnp.exp(-seen)
        return carry

    lax.fori_loop(0, views, fade, 0)


def project_kernel(
    scal_ref,
    near_ref,
    far_ref,
    table_ref,
    measured_ref,
    own_proj_ref,
    decay_ref,
    keep_ref,
    give_ref,
    window,
    table_proj,
    sino,
    picked,
    spread,
    row_ref,
    *,
    local_blocks,
    slots,
):
    views, det_rows, channels = measured_ref.shape
    tables = table_ref.shape[0]
    slab = 16
    part = local_blocks * slab
    piece = 2 * part
    win_rows = 5 * piece
    away_rows = 4 * piece
    position = scal_ref[2 * slots + 2, 0]
    core = lax.rem(position, 2)
    chip = position // 2

    angle_of = lambda view: scal_ref[2 * slots + 1, view]
    count_of = lambda view: scal_ref[2 * slots, view]
    offset_of = lambda view, slot: scal_ref[slots + slot, view]

    def window_row(block):
        owner = block // local_blocks
        owner_core = lax.rem(owner, 2)
        delta = owner // 2 - chip
        up = delta > 0
        nearer = jnp.abs(delta) == 1
        is_y = up == (lax.rem(chip, 2) == 0)
        is_a = up == (lax.rem(chip, 4) < 2)
        second = jnp.where(nearer, is_y, is_a).astype(jnp.int32)
        via = jnp.where(nearer, 1 - is_y.astype(jnp.int32), is_a.astype(jnp.int32))
        differ = lambda one, two: jnp.where(one == two, 0, 1)
        away = (differ(via, core) * 2 + second) * piece + differ(owner_core, via) * part
        here = away_rows + differ(owner_core, core) * part
        return jnp.where(delta == 0, here, away) + lax.rem(block, local_blocks) * slab

    window[0:piece, :] = near_ref[0:piece, :]
    window[piece : 2 * piece, :] = near_ref[piece + 8 : 2 * piece + 8, :]
    window[2 * piece : 3 * piece, :] = far_ref[0:piece, :]
    window[3 * piece : 4 * piece, :] = far_ref[piece + 8 : 2 * piece + 8, :]
    sino[...] = jnp.zeros_like(sino)
    keep_ref[...] = jnp.zeros_like(keep_ref)
    give_ref[...] = jnp.zeros_like(give_ref)

    def count_table(view, total):
        return total + jnp.where(angle_of(view) == 0, count_of(view), 0)

    first_pairs = lax.fori_loop(0, views, count_table, 0)
    first_chunks = (first_pairs + CHUNK_PAIRS - 1) // CHUNK_PAIRS

    def forward(table, carry):
        start = pl.multiple_of(table * win_rows, 16)
        table_proj[pl.ds(start, away_rows), :] = jnp.dot(
            window[...], table_ref[table], preferred_element_type=jnp.float32
        )
        table_proj[pl.ds(pl.multiple_of(start + away_rows, 16), piece), :] = own_proj_ref[
            pl.ds(pl.multiple_of(table * piece, 16), piece), :
        ]
        return carry

    lax.fori_loop(0, tables, forward, 0)

    def place(view, carry):
        base = angle_of(view) * win_rows
        for slot in range(slots):

            @pl.when(slot < count_of(view))
            def _():
                row = window_row(scal_ref[slot, view])
                row_ref[view * slots + slot] = row
                source = pl.multiple_of(base + row, slab)
                target = view * det_rows + offset_of(view, slot)
                for lane in range(0, channels, 128):
                    sino[lane // 128, pl.ds(target, slab), :] += table_proj[
                        pl.ds(source, slab), lane : lane + 128
                    ]

        return carry

    lax.fori_loop(0, views, place, 0)

    def weigh(view, carry):
        here = pl.ds(pl.multiple_of(view * det_rows, det_rows), det_rows)
        for lane in range(0, channels, 128):
            seen = measured_ref[view, :, lane : lane + 128].astype(jnp.float32)
            value = decay_ref[lane // 128, here, :] * (sino[lane // 128, here, :] - seen)
            sino[lane // 128, here, :] = value.astype(jnp.bfloat16).astype(jnp.float32)
        return carry

    lax.fori_loop(0, views, weigh, 0)

    def starts(view, carry):
        zero_next, one_next = carry
        is_one = angle_of(view) != 0
        taken = count_of(view)
        after = (
            zero_next + jnp.where(is_one, 0, taken),
            one_next + jnp.where(is_one, taken, 0),
        )
        return jnp.where(is_one, one_next, zero_next), after

    def pick(view, carry):
        start, after = starts(view, carry)
        for slot in range(slots):

            @pl.when(slot < count_of(view))
            def _():
                source = view * det_rows + offset_of(view, slot)
                target = pl.multiple_of((start + slot) * slab, slab)
                for lane in range(0, channels, 128):
                    picked[pl.ds(target, slab), lane : lane + 128] = sino[
                        lane // 128, pl.ds(source, slab), :
                    ].astype(jnp.bfloat16)

        return after

    first = (jnp.int32(0), first_chunks * CHUNK_PAIRS)
    _, end = lax.fori_loop(0, views, pick, first)
    chunks = (end + CHUNK_PAIRS - 1) // CHUNK_PAIRS
    chunk_rows = CHUNK_PAIRS * slab

    def backward(chunk, carry):
        here = pl.ds(pl.multiple_of(chunk * chunk_rows, chunk_rows), chunk_rows)
        table = jnp.where(chunk < first_chunks, 0, 1)
        spread[here, :] = lax.dot_general(
            picked[here, :],
            table_ref[table],
            (((1,), (1,)), ((), ())),
            preferred_element_type=jnp.float32,
        )
        return carry

    lax.fori_loop(0, chunks, backward, 0)

    def collect(view, carry):
        start, after = starts(view, carry)
        for slot in range(slots):

            @pl.when(slot < count_of(view))
            def _():
                source = pl.multiple_of((start + slot) * slab, slab)
                row = row_ref[view * slots + slot]
                at_home = row >= away_rows
                local = row - jnp.where(at_home, 2 * piece, 0)
                own_side = jnp.where(at_home, row < away_rows + part, row < 2 * piece)
                kept = pl.multiple_of(local, slab)
                given = pl.multiple_of(local - jnp.where(at_home, part, 2 * piece), slab)

                @pl.when(own_side)
                def _():
                    keep_ref[pl.ds(kept, slab), :] += spread[pl.ds(source, slab), :]

                @pl.when(jnp.logical_not(own_side))
                def _():
                    give_ref[pl.ds(given, slab), :] += spread[pl.ds(source, slab), :]

        return after

    lax.fori_loop(0, views, collect, first)


def prior_kernel(scal_ref, vol_ref, other_ref, near_ref, far_ref, out_ref, *, devices, scal_row):
    slices, strip, row = vol_ref.shape
    part = slices
    piece = 2 * part
    step = piece + 8
    position = scal_ref[scal_row, 0]
    core = lax.rem(position, 2)
    odd = lax.rem(position // 2, 2)

    def edge_slice(ref, which, base, tail):
        at = base + (part - 1) * which
        whole = ref[at : at + 1, :].astype(jnp.float32)
        more = ref[tail + 2 * which : tail + 2 * which + 2, :].astype(jnp.float32)
        return whole + (more[0:1] + more[1:2])

    def chip_slice(ref, which, exchange, via):
        sub = which ^ via
        return edge_slice(ref, which, exchange * step + sub * part, exchange * step + piece + 4 * sub)

    def emit(low, high):
        for y in range(strip):
            cols = slice(y * row, (y + 1) * row)
            here = vol_ref[:, y, :]
            below = jnp.concatenate([low[:, cols], here[:-1]], axis=0)
            above = jnp.concatenate([here[1:], high[:, cols]], axis=0)
            level = lax.broadcasted_iota(jnp.int32, here.shape, 0)
            down = jnp.clip(here - below, -DELTA, DELTA)
            total = jnp.where((level > 0) | (position > 0), down, 0.0)
            up = jnp.clip(here - above, -DELTA, DELTA)
            total += jnp.where((level < slices - 1) | (position < devices - 1), up, 0.0)
            if y > 0:
                total += jnp.clip(here - vol_ref[:, y - 1, :], -DELTA, DELTA)
            if y + 1 < strip:
                total += jnp.clip(here - vol_ref[:, y + 1, :], -DELTA, DELTA)
            lane = lax.broadcasted_iota(jnp.int32, here.shape, 1)
            left = jnp.clip(here - pltpu.roll(here, 1, 1), -DELTA, DELTA)
            total += jnp.where(lane > 0, left, 0.0)
            right = jnp.clip(here - pltpu.roll(here, row - 1, 1), -DELTA, DELTA)
            total += jnp.where(lane < row - 1, right, 0.0)
            out_ref[:, cols] = PRIOR_WEIGHT * total

    @pl.when((core == 0) & (odd == 0))
    def _():
        emit(chip_slice(far_ref, 1, 0, 1), edge_slice(other_ref, 0, 0, part))

    @pl.when((core == 0) & (odd == 1))
    def _():
        emit(chip_slice(near_ref, 1, 1, 0), edge_slice(other_ref, 0, 0, part))

    @pl.when((core == 1) & (odd == 0))
    def _():
        emit(edge_slice(other_ref, 1, 0, part), chip_slice(far_ref, 0, 1, 0))

    @pl.when((core == 1) & (odd == 1))
    def _():
        emit(edge_slice(other_ref, 1, 0, part), chip_slice(near_ref, 0, 0, 1))


def last_kernel(total_ref, arrived_ref, passed_ref, prior_ref, out_ref):
    part, strip, row = out_ref.shape
    for y in range(strip):
        cols = slice(y * row, (y + 1) * row)
        out_ref[:, y, :] = (
            (total_ref[:, cols] + arrived_ref[:, cols]) + passed_ref[:, cols]
        ) + prior_ref[:, cols]


def shards(volume, footprint, measured, angle_index, cover, offset, count):
    local_blocks, slab, strip, row = volume.shape
    views, det_rows, channels = measured.shape
    tables = footprint.shape[0]
    slots = cover.shape[1]
    plane = strip * row
    devices = lax.axis_size(AXES)
    position = lax.axis_index(AXES)
    swap, first, second = exchange_pairs(devices)
    send = lambda value, pairs: lax.ppermute(value, AXES, pairs)
    part = local_blocks * slab
    piece = 2 * part
    flat = volume.reshape(part, strip, row)
    table = footprint.reshape(tables, plane, channels)
    vmem = pl.BlockSpec(memory_space=pltpu.VMEM)
    smem = pl.BlockSpec(memory_space=pltpu.SMEM)
    shape = jax.ShapeDtypeStruct
    room = lambda mib: pltpu.CompilerParams(vmem_limit_bytes=mib * 1024 * 1024)
    cost = lambda flops, size: pl.CostEstimate(flops=flops, bytes_accessed=size, transcendentals=0)

    own = pl.pallas_call(
        pack_kernel,
        out_shape=shape((part + 8, plane), jnp.bfloat16),
        in_specs=[vmem],
        out_specs=vmem,
        compiler_params=room(4),
        name="pack",
    )(flat)
    other = send(own, swap)
    both = pl.pallas_call(
        join_kernel,
        out_shape=shape((piece + 8, plane), jnp.bfloat16),
        in_specs=[vmem] * 2,
        out_specs=vmem,
        compiler_params=room(4),
        name="join",
    )(own, other)
    got_first = send(both, first)
    got_second = send(both, second)

    scalars = jnp.concatenate(
        [
            cover.T,
            offset.T,
            count[None],
            angle_index[None],
            jnp.broadcast_to(position.astype(jnp.int32), (1, views)),
        ],
        axis=0,
    )
    own_proj, decay = pl.pallas_call(
        early_kernel,
        out_shape=(
            shape((tables * piece, channels), jnp.float32),
            shape((channels // 128, views * det_rows, 128), jnp.float32),
        ),
        in_specs=[vmem] * 4,
        out_specs=(vmem, vmem),
        scratch_shapes=[pltpu.VMEM((piece, plane), jnp.bfloat16)],
        compiler_params=room(16),
        cost_estimate=cost(1_000_000_000, 8_000_000),
        name="early",
    )(own, other, table, measured)
    got_first, got_second, own_proj, decay, scalars = lax.optimization_barrier(
        (got_first, got_second, own_proj, decay, scalars)
    )
    near = jnp.concatenate([got_first, got_second], axis=0)
    far = send(near, swap)

    pair_rows = views * slots * slab + CHUNK_PAIRS * slab
    keep, give = pl.pallas_call(
        functools.partial(project_kernel, local_blocks=local_blocks, slots=slots),
        out_shape=(
            shape((2 * piece + part, plane), jnp.float32),
            shape((2 * piece + part, plane), jnp.float32),
        ),
        in_specs=[smem] + [vmem] * 6,
        out_specs=(vmem, vmem),
        scratch_shapes=[
            pltpu.VMEM((4 * piece, plane), jnp.bfloat16),
            pltpu.VMEM((tables * 5 * piece, channels), jnp.float32),
            pltpu.VMEM((channels // 128, views * det_rows, 128), jnp.float32),
            pltpu.VMEM((pair_rows, channels), jnp.bfloat16),
            pltpu.VMEM((pair_rows, plane), jnp.float32),
            pltpu.SMEM((views * slots,), jnp.int32),
        ],
        compiler_params=room(32),
        cost_estimate=cost(4_000_000_000, 8_000_000),
        name="project",
    )(scalars, near, far, table, measured, own_proj, decay)
    taken = send(give, swap)
    total = keep + taken
    wire = total[: 2 * piece].astype(jnp.bfloat16)
    back_first = send(wire[:piece], first)
    back_second = send(wire[piece:], second)

    prior = pl.pallas_call(
        functools.partial(prior_kernel, devices=devices, scal_row=2 * slots + 2),
        out_shape=shape((part, plane), jnp.float32),
        in_specs=[smem] + [vmem] * 4,
        out_specs=vmem,
        compiler_params=room(8),
        cost_estimate=cost(10_000_000, 1_000_000),
        name="prior",
    )(scalars, flat, other, near, far)
    back_first, back_second, prior = lax.optimization_barrier((back_first, back_second, prior))

    arrived = back_first.astype(jnp.float32) + back_second.astype(jnp.float32)
    passed = send(arrived[part:], swap)
    out = pl.pallas_call(
        last_kernel,
        out_shape=shape((part, strip, row), jnp.float32),
        in_specs=[vmem] * 4,
        out_specs=vmem,
        compiler_params=room(4),
        name="last",
    )(total[2 * piece :], arrived[:part], passed, prior)
    return out.reshape(volume.shape)


def solution(mesh):
    in_specs = (
        P(AXES, None, None, None),
        P(AXES, None, None, None),
        P(AXES, None, None),
        P(AXES),
        P(AXES, None),
        P(AXES, None),
        P(AXES),
    )
    out_specs = P(AXES, None, None, None)
    return jax.shard_map(shards, mesh=mesh, in_specs=in_specs, out_specs=out_specs, check_vma=False)
```

time: 44 us -> 35.6 us (0.81)
  local copies, waits for them, and re-layouts: 9.39 us -> 5.6 us
  waiting for transfers between devices: 12.2 us -> 10.6 us
  other arithmetic: 1.69 us -> 0.14 us
  starting transfers between devices: 10.5 us -> 9.62 us
    unnamed x19 -> x13, local copies, waits for them, and re-layouts: 7.01 us -> 4.14 us
    ppermute x8, waiting for transfers between devices: 12.2 us -> 10.6 us  [shards(): send = lambda value, pairs: lax.ppermute(value, AXES, pairs)]
    slice x5 -> x2, local copies, waits for them, and re-layouts: 1.6 us -> 0.03 us  [the longest x1 0.02 us: shards(): back_second = send(wire[piece:], second)]
    concatenate x0 -> x1, local copies, waits for them, and re-layouts: none -> 1.4 us  [shards(): jnp.concatenate([cover.T, offset.T, count[None], angle_index[None], jnp.b...]
    add x2 -> x0, other arithmetic: 0.96 us -> none  [the longest x1 0.93 us: shards(): return (data + prior).reshape(volume.shape)]
    ppermute x8, starting transfers between devices: 10.5 us -> 9.62 us  [shards(): send = lambda value, pairs: lax.ppermute(value, AXES, pairs)]
    reshape x1 -> x0, local copies, waits for them, and re-layouts: 0.76 us -> none  [shards(): return (data + prior).reshape(volume.shape)]
    another operation x2 -> x1, other arithmetic: 0.68 us -> 0.11 us  [the longest x1 0.59 us: shards(): jnp.stack([core, position // 2 % 2, (position > 0).astype(jnp.int32), (po...]
  transfers between devices with their start and end apart: 8 -> 8, of which waited for: 4 -> 7; matrix products, arithmetic and copies ran while one was open for 8% -> 4% of each run, Pallas kernels for 5% -> 6%
where the time goes in v2:
time: 35.6 us; the launch traced here: 35.9 us
  waiting for transfers between devices  10.6 us (30%)
  Pallas kernels  9.77 us (27%)
  starting transfers between devices  9.62 us (27%)
  local copies, waits for them, and re-layouts  5.6 us (16%)
    ppermute x8, waiting for transfers between devices, shards(): send = lambda value, pairs: lax.ppermute(value, AXES, pairs)  10.6 us
    ppermute x8, starting transfers between devices, shards(): send = lambda value, pairs: lax.ppermute(value, AXES, pairs)  9.62 us
    pallas_call x1, Pallas kernels, shards(): pl.pallas_call(functools.partial(project_kernel, local_blocks=local_block...  6.82 us
    unnamed x13, local copies, waits for them, and re-layouts  4.14 us
    concatenate x1, local copies, waits for them, and re-layouts, shards(): jnp.concatenate([cover.T, offset.T, count[None], angle_index[None], jnp.b...  1.4 us
    pallas_call x1, Pallas kernels, shards(): pl.pallas_call(early_kernel, out_shape=(shape((tables * piece, channels),...  1.19 us
    pallas_call x1, Pallas kernels, shards(): pl.pallas_call(functools.partial(prior_kernel, devices=devices, scal_row=...  0.89 us
  transfers between devices with their start and end apart: 8, of which 7 were waited for; matrix products, arithmetic and copies ran while one was open for 4% of the time, Pallas kernels for 6%

profile of v2, /device:TPU:3, one launch (start us, length us, event | category | flops | bytes accessed | tf_op | source)
XLA Modules:
  0.0 35.9 jit_solution(12047566428273905854)
XLA Ops:
  0.0 0.0 copy-start.4
  0.0 0.9 %copy-done.4 = f32[2,16,2,512]{3,2,1,0:T(2,128)S(1)} copy-done((f32[2,16,2,512]{3,2,1,0:T(2,128)S(1)}, f32[2,16,2,512]{3,2,1,0:T(2,128)}, u32[]{:S(2)}) %copy-start.4) | copy-done | bytes 131096
  0.9 0.2 pack.1.own_ref
  1.1 0.7 %collective-permute-start = (bf16[40,1024]{1,0:T(8,128)(2,1)S(1)}, bf16[40,1024]{1,0:T(8,128)(2,1)S(1)}, u32[]{:S(2)}, u32[]{:S(2)}) collective-permute-start(bf16[40,1024]{1,0:T(8,128)(2,1)S(1)} %pack.1.own_ref), channel_id=1, source_target_pairs={{0,1},{1,0},{2,3},{3,2},{4,5},{5,4},{6,7},{7,6},{8,9},{9,8},{10,11... | collective-permute-start | bytes 245768 | tf_op jit(solution)/shard_map/ppermute | solution.py:345
  1.8 0.9 %collective-permute-done.other_ref = bf16[40,1024]{1,0:T(8,128)(2,1)S(1)} collective-permute-done((bf16[40,1024]{1,0:T(8,128)(2,1)S(1)}, bf16[40,1024]{1,0:T(8,128)(2,1)S(1)}, u32[]{:S(2)}, u32[]{:S(2)}) %collective-permute-start) | collective-permute-done | bytes 81952 | tf_op jit(solution)/shard_map/ppermute | solution.py:345
  2.8 1.4 %collective-permute-start.2 = (bf16[72,1024]{1,0:T(8,128)(2,1)S(1)}, bf16[72,1024]{1,0:T(8,128)(2,1)S(1)}, u32[]{:S(2)}, u32[]{:S(2)}) collective-permute-start(bf16[72,1024]{1,0:T(8,128)(2,1)S(1)} %join.1), channel_id=1, source_target_pairs={{0,2},{4,6},{8,10},{12,14},{16,18},{20,22},{24,26},{28,30},{1,5},{... | collective-permute-start | bytes 442376 | tf_op jit(solution)/shard_map/ppermute | solution.py:345
  4.1 3.1 %collective-permute-start.1 = (bf16[72,1024]{1,0:T(8,128)(2,1)S(1)}, bf16[72,1024]{1,0:T(8,128)(2,1)S(1)}, u32[]{:S(2)}, u32[]{:S(2)}) collective-permute-start(bf16[72,1024]{1,0:T(8,128)(2,1)S(1)} %join.1), channel_id=1, source_target_pairs={{4,8},{6,10},{12,16},{14,18},{20,24},{22,26},{3,5},{7,9},{11,13},{... | collective-permute-start | bytes 442376 | tf_op jit(solution)/shard_map/ppermute | solution.py:345
  7.2 1.4 %concatenate.6.scal_ref = s32[11,8]{1,0:T(8,128)S(1)} concatenate(s32[4,8]{1,0:T(4,128)} %bitcast.11, s32[4,8]{1,0:T(4,128)} %bitcast.12, s32[1,8]{1,0:T(1,128)} %bitcast.13, s32[1,8]{1,0:T(1,128)} %bitcast.14, s32[1,8]{1,0:T(1,128)S(1)} %broadcast_in_dim.11), dimensions={0} | concatenate | bytes 704 | tf_op jit(solution)/shard_map/concatenate | solution.py:376
  8.6 0.0 copy-start
  8.6 2.0 %copy-done = bf16[2,2,512,896]{3,2,1,0:T(8,128)(2,1)S(1)} copy-done((bf16[2,2,512,896]{3,2,1,0:T(8,128)(2,1)S(1)}, bf16[2,2,512,896]{3,2,1,0:T(8,128)(2,1)}, u32[]{:S(2)}) %copy-start) | copy-done | bytes 3670040
  10.7 0.0 copy-start.2
  10.7 1.2 %copy-done.2 = bf16[8,64,896]{2,1,0:T(8,128)(2,1)S(1)} copy-done((bf16[8,64,896]{2,1,0:T(8,128)(2,1)S(1)}, bf16[8,64,896]{2,1,0:T(8,128)(2,1)}, u32[]{:S(2)}) %copy-start.2) | copy-done | bytes 917528
  11.9 0.0 copy-start.1
  11.9 0.0 copy-start.3
  11.9 1.2 %early.1 = (f32[128,896]{1,0:T(8,128)S(1)}, f32[7,512,128]{2,1,0:T(8,128)S(1)}) custom-call(bf16[40,1024]{1,0:T(8,128)(2,1)S(1)} %pack.1.own_ref, bf16[40,1024]{1,0:T(8,128)(2,1)S(1)} %collective-permute-done.other_ref, bf16[2,1024,896]{2,1,0:T(8,128)(2,1)S(1)} %bitcast.7, bf16[8,64,896]{2,1,0:T(8,128)(2,1)S(1)} %copy-done.2), custom_call_target="tpu_custom_call" | custom-call | flops 1000000000 | bytes 8000000 | tf_op jit(solution)/shard_map/early/pallas_call | solution.py:386
  13.1 0.0 collective-permute-done.2
  13.1 0.1 collective-permute-done.1
  13.2 0.0 copy-start.5
  13.3 1.0 %collective-permute-start.3 = (bf16[144,1024]{1,0:T(8,128)(2,1)S(1)}, bf16[144,1024]{1,0:T(8,128)(2,1)S(1)}, u32[]{:S(2)}, u32[]{:S(2)}) collective-permute-start(bf16[144,1024]{1,0:T(8,128)(2,1)S(1)} %constant_dynamic-update-slice_fusion.near_ref), channel_id=1, source_target_pairs={{0,1},{1,0},{2,3},{3,2},{4,5},{5,4},{6,7},{7,6},{8,9},{9,8},{10,11... | collective-permute-start | bytes 884744 | tf_op jit(solution)/shard_map/ppermute | solution.py:345
  14.2 1.2 %collective-permute-done.3.far_ref = bf16[144,1024]{1,0:T(8,128)(2,1)S(1)} collective-permute-done((bf16[144,1024]{1,0:T(8,128)(2,1)S(1)}, bf16[144,1024]{1,0:T(8,128)(2,1)S(1)}, u32[]{:S(2)}, u32[]{:S(2)}) %collective-permute-start.3) | collective-permute-done | bytes 294944 | tf_op jit(solution)/shard_map/ppermute | solution.py:345
  15.4 0.0 copy-done.1
  15.4 0.0 copy-done.3
  15.4 6.8 %project.1 = (f32[160,1024]{1,0:T(8,128)S(1)}, f32[160,1024]{1,0:T(8,128)S(1)}) custom-call(s32[11,8]{1,0:T(8,128)S(1)} %concatenate.6.scal_ref, bf16[144,1024]{1,0:T(8,128)(2,1)S(1)} %constant_dynamic-update-slice_fusion.near_ref, bf16[144,1024]{1,0:T(8,128)(2,1)S(1)} %collective-permute-done.3.far_ref, bf16[2,1024,896]{2,1,0:T(8,128)(2,1)S(1)} %bitcast.8, ...), custom_call_target="tpu_custom_call" | custom-call | flops 4000000000 | bytes 8000000 | tf_op jit(solution)/shard_map/project/pallas_call | solution.py:406
  22.3 0.1 collective-permute-start.4
  22.3 2.1 %collective-permute-done.4 = f32[160,1024]{1,0:T(8,128)S(1)} collective-permute-done((f32[160,1024]{1,0:T(8,128)S(1)}, f32[160,1024]{1,0:T(8,128)S(1)}, u32[]{:S(2)}, u32[]{:S(2)}) %collective-permute-start.4) | collective-permute-done | bytes 655392 | tf_op jit(solution)/shard_map/ppermute | solution.py:345
  24.4 0.1 fusion
  24.6 0.1 collective-permute-start.6
  24.6 1.6 %collective-permute-start.5 = (bf16[64,1024]{1,0:T(8,128)(2,1)S(1)}, bf16[64,1024]{1,0:T(8,128)(2,1)S(1)}, u32[]{:S(2)}, u32[]{:S(2)}) collective-permute-start(bf16[64,1024]{1,0:T(8,128)(2,1)S(1)} %get-tuple-element.32), channel_id=1, source_target_pairs={{4,8},{6,10},{12,16},{14,18},{20,24},{22,26},{3,5},{7,9},{11,13},{... | collective-permute-start | bytes 393224 | tf_op jit(solution)/shard_map/ppermute | solution.py:345
  26.2 0.0 copy-done.5
  26.2 0.9 %prior.1.prior_ref = f32[32,1024]{1,0:T(8,128)S(1)} custom-call(s32[11,8]{1,0:T(8,128)S(1)} %concatenate.6.scal_ref, f32[32,2,512]{2,1,0:T(2,128)S(1)} %bitcast.10, bf16[40,1024]{1,0:T(8,128)(2,1)S(1)} %collective-permute-done.other_ref, bf16[144,1024]{1,0:T(8,128)(2,1)S(1)} %constant_dynamic-update-slice_fusion.near_ref, ...), custom_call_target="tpu_custom_call" | custom-call | flops 10000000 | bytes 1000000 | tf_op jit(solution)/shard_map/prior/pallas_call | solution.py:432
  27.1 1.6 %collective-permute-done.6 = bf16[64,1024]{1,0:T(8,128)(2,1)S(1)} collective-permute-done((bf16[64,1024]{1,0:T(8,128)(2,1)S(1)}, bf16[64,1024]{1,0:T(8,128)(2,1)S(1)}, u32[]{:S(2)}, u32[]{:S(2)}) %collective-permute-start.6) | collective-permute-done | bytes 131104 | tf_op jit(solution)/shard_map/ppermute | solution.py:345
  28.8 3.7 %collective-permute-done.5 = bf16[64,1024]{1,0:T(8,128)(2,1)S(1)} collective-permute-done((bf16[64,1024]{1,0:T(8,128)(2,1)S(1)}, bf16[64,1024]{1,0:T(8,128)(2,1)S(1)}, u32[]{:S(2)}, u32[]{:S(2)}) %collective-permute-start.5) | collective-permute-done | bytes 131104 | tf_op jit(solution)/shard_map/ppermute | solution.py:345
  32.5 1.7 %collective-permute-start.7 = (f32[32,1024]{1,0:T(8,128)S(1)}, f32[32,1024]{1,0:T(8,128)S(1)}, u32[]{:S(2)}, u32[]{:S(2)}) collective-permute-start(f32[32,1024]{1,0:T(8,128)S(1)} %get-tuple-element.33), channel_id=1, source_target_pairs={{0,1},{1,0},{2,3},{3,2},{4,5},{5,4},{6,7},{7,6},{8,9},{9,8},{10,11... | collective-permute-start | bytes 393224 | tf_op jit(solution)/shard_map/ppermute | solution.py:345
  34.2 1.0 %collective-permute-done.7.passed_ref = f32[32,1024]{1,0:T(8,128)S(1)} collective-permute-done((f32[32,1024]{1,0:T(8,128)S(1)}, f32[32,1024]{1,0:T(8,128)S(1)}, u32[]{:S(2)}, u32[]{:S(2)}) %collective-permute-start.7) | collective-permute-done | bytes 131104 | tf_op jit(solution)/shard_map/ppermute | solution.py:345
  35.2 0.7 %last.1 = f32[32,2,512]{2,1,0:T(2,128)} custom-call(f32[32,1024]{1,0:T(8,128)S(1)} %slice.24.total_ref, f32[32,1024]{1,0:T(8,128)S(1)} %get-tuple-element.34.arrived_ref, f32[32,1024]{1,0:T(8,128)S(1)} %collective-permute-done.7.passed_ref, f32[32,1024]{1,0:T(8,128)S(1)} %prior.1.prior_ref), custom_call_target="tpu_custom_call" | custom-call | tf_op jit(solution)/shard_map/last/pallas_call | solution.py:445
  (8 shorter events, 0.1 us)
Async XLA Ops:
  0.0 0.9 %copy-start.4 = (f32[2,16,2,512]{3,2,1,0:T(2,128)S(1)}, f32[2,16,2,512]{3,2,1,0:T(2,128)}, u32[]{:S(2)}) copy-start(f32[2,16,2,512]{3,2,1,0:T(2,128)} %param.7) | copy-start | bytes 393220
  1.1 1.7 %collective-permute-start = (bf16[40,1024]{1,0:T(8,128)(2,1)S(1)}, bf16[40,1024]{1,0:T(8,128)(2,1)S(1)}, u32[]{:S(2)}, u32[]{:S(2)}) collective-permute-start(bf16[40,1024]{1,0:T(8,128)(2,1)S(1)} %pack.1.own_ref), channel_id=1, source_target_pairs={{0,1},{1,0},{2,3},{3,2},{4,5},{5,4},{6,7},{7,6},{8,9},{9,8},{10,11... | collective-permute-start | bytes 245768 | tf_op jit(solution)/shard_map/ppermute | solution.py:345
  2.8 10.3 %collective-permute-start.2 = (bf16[72,1024]{1,0:T(8,128)(2,1)S(1)}, bf16[72,1024]{1,0:T(8,128)(2,1)S(1)}, u32[]{:S(2)}, u32[]{:S(2)}) collective-permute-start(bf16[72,1024]{1,0:T(8,128)(2,1)S(1)} %join.1), channel_id=1, source_target_pairs={{0,2},{4,6},{8,10},{12,14},{16,18},{20,22},{24,26},{28,30},{1,5},{... | collective-permute-start | bytes 442376 | tf_op jit(solution)/shard_map/ppermute | solution.py:345
  4.1 9.1 %collective-permute-start.1 = (bf16[72,1024]{1,0:T(8,128)(2,1)S(1)}, bf16[72,1024]{1,0:T(8,128)(2,1)S(1)}, u32[]{:S(2)}, u32[]{:S(2)}) collective-permute-start(bf16[72,1024]{1,0:T(8,128)(2,1)S(1)} %join.1), channel_id=1, source_target_pairs={{4,8},{6,10},{12,16},{14,18},{20,24},{22,26},{3,5},{7,9},{11,13},{... | collective-permute-start | bytes 442376 | tf_op jit(solution)/shard_map/ppermute | solution.py:345
  8.6 2.0 %copy-start = (bf16[2,2,512,896]{3,2,1,0:T(8,128)(2,1)S(1)}, bf16[2,2,512,896]{3,2,1,0:T(8,128)(2,1)}, u32[]{:S(2)}) copy-start(bf16[2,2,512,896]{3,2,1,0:T(8,128)(2,1)} %param.8) | copy-start | bytes 11010052
  10.7 1.2 %copy-start.2 = (bf16[8,64,896]{2,1,0:T(8,128)(2,1)S(1)}, bf16[8,64,896]{2,1,0:T(8,128)(2,1)}, u32[]{:S(2)}) copy-start(bf16[8,64,896]{2,1,0:T(8,128)(2,1)} %measured_ref.3) | copy-start | bytes 2752516
  11.9 3.6 %copy-start.1 = (bf16[2,2,512,896]{3,2,1,0:T(8,128)(2,1)S(1)}, bf16[2,2,512,896]{3,2,1,0:T(8,128)(2,1)}, u32[]{:S(2)}) copy-start(bf16[2,2,512,896]{3,2,1,0:T(8,128)(2,1)} %param.8) | copy-start | bytes 11010052
  11.9 3.6 %copy-start.3 = (bf16[8,64,896]{2,1,0:T(8,128)(2,1)S(1)}, bf16[8,64,896]{2,1,0:T(8,128)(2,1)}, u32[]{:S(2)}) copy-start(bf16[8,64,896]{2,1,0:T(8,128)(2,1)} %measured_ref.3) | copy-start | bytes 2752516
  13.2 13.0 %copy-start.5 = (f32[2,16,2,512]{3,2,1,0:T(2,128)S(1)}, f32[2,16,2,512]{3,2,1,0:T(2,128)}, u32[]{:S(2)}) copy-start(f32[2,16,2,512]{3,2,1,0:T(2,128)} %param.7) | copy-start | bytes 393220
  13.3 2.2 %collective-permute-start.3 = (bf16[144,1024]{1,0:T(8,128)(2,1)S(1)}, bf16[144,1024]{1,0:T(8,128)(2,1)S(1)}, u32[]{:S(2)}, u32[]{:S(2)}) collective-permute-start(bf16[144,1024]{1,0:T(8,128)(2,1)S(1)} %constant_dynamic-update-slice_fusion.near_ref), channel_id=1, source_target_pairs={{0,1},{1,0},{2,3},{3,2},{4,5},{5,4},{6,7},{7,6},{8,9},{9,8},{10,11... | collective-permute-start | bytes 884744 | tf_op jit(solution)/shard_map/ppermute | solution.py:345
  22.3 2.2 %collective-permute-start.4 = (f32[160,1024]{1,0:T(8,128)S(1)}, f32[160,1024]{1,0:T(8,128)S(1)}, u32[]{:S(2)}, u32[]{:S(2)}) collective-permute-start(f32[160,1024]{1,0:T(8,128)S(1)} %get-tuple-element.25), channel_id=1, source_target_pairs={{0,1},{1,0},{2,3},{3,2},{4,5},{5,4},{6,7},{7,6},{8,9},{9,8},{10,11... | collective-permute-start | bytes 1966088 | tf_op jit(solution)/shard_map/ppermute | solution.py:345
  24.6 4.2 %collective-permute-start.6 = (bf16[64,1024]{1,0:T(8,128)(2,1)S(1)}, bf16[64,1024]{1,0:T(8,128)(2,1)S(1)}, u32[]{:S(2)}, u32[]{:S(2)}) collective-permute-start(bf16[64,1024]{1,0:T(8,128)(2,1)S(1)} %get-tuple-element.31), channel_id=1, source_target_pairs={{0,2},{4,6},{8,10},{12,14},{16,18},{20,22},{24,26},{28,30},{1,5},{... | collective-permute-start | bytes 393224 | tf_op jit(solution)/shard_map/ppermute | solution.py:345
  24.6 7.8 %collective-permute-start.5 = (bf16[64,1024]{1,0:T(8,128)(2,1)S(1)}, bf16[64,1024]{1,0:T(8,128)(2,1)S(1)}, u32[]{:S(2)}, u32[]{:S(2)}) collective-permute-start(bf16[64,1024]{1,0:T(8,128)(2,1)S(1)} %get-tuple-element.32), channel_id=1, source_target_pairs={{4,8},{6,10},{12,16},{14,18},{20,24},{22,26},{3,5},{7,9},{11,13},{... | collective-permute-start | bytes 393224 | tf_op jit(solution)/shard_map/ppermute | solution.py:345
  32.5 2.7 %collective-permute-start.7 = (f32[32,1024]{1,0:T(8,128)S(1)}, f32[32,1024]{1,0:T(8,128)S(1)}, u32[]{:S(2)}, u32[]{:S(2)}) collective-permute-start(f32[32,1024]{1,0:T(8,128)S(1)} %get-tuple-element.33), channel_id=1, source_target_pairs={{0,1},{1,0},{2,3},{3,2},{4,5},{5,4},{6,7},{7,6},{8,9},{9,8},{10,11... | collective-permute-start | bytes 393224 | tf_op jit(solution)/shard_map/ppermute | solution.py:345

commit v3 on v0

v3 whole, which is shorter than its diff:
```python
import functools

import jax
import jax.numpy as jnp
from jax import lax
from jax.experimental import pallas as pl
from jax.experimental.pallas import tpu as pltpu
from jax.sharding import PartitionSpec as P

AXES = ("grp", "view")
DELTA = 0.5
PRIOR_WEIGHT = 2.0


def both_ways(pairs):
    return pairs + [(b, a) for a, b in pairs]


def exchange_pairs(devices):
    chips = devices // 2
    swap = [(i, i ^ 1) for i in range(devices)]
    edge_y = [(i, i + 1) for i in range(0, chips, 2)]
    edge_d = [(i, i + 1) for i in range(1, chips - 1, 2)]
    edge_a = [(i + j, i + j + 2) for i in range(0, chips, 4) for j in (0, 1)]
    edge_b = [(i + j, i + j + 2) for i in range(2, chips - 2, 4) for j in (0, 1)]
    on_core = lambda edges, core: [(2 * a + core, 2 * b + core) for a, b in edges]
    last = devices - 1
    ends = [(0, 1), (1, 2), (2, 0), (last, last - 1), (last - 1, last - 3), (last - 3, last)]
    long = both_ways(on_core(edge_b, 0) + on_core(edge_d, 1)) + ends
    short = both_ways(on_core(edge_y, 0) + on_core(edge_a, 1))
    return swap, long, short


def load_kernel(source, target, sem):
    copy = pltpu.make_async_copy(source, target, sem)
    copy.start()
    copy.wait()


def join_kernel(own_ref, other_ref, out_ref):
    slices, strip, row = own_ref.shape
    for y in range(strip):
        cols = slice(y * row, (y + 1) * row)
        spare = []
        for k, ref in enumerate((own_ref, other_ref)):
            plane = ref[:, y, :]
            high = plane.astype(jnp.bfloat16)
            out_ref[k * slices : (k + 1) * slices, cols] = high
            rest = plane - high.astype(jnp.float32)
            mid = rest.astype(jnp.bfloat16).astype(jnp.float32)
            low = rest - mid
            for at in (0, slices - 1):
                spare += [mid[at : at + 1], low[at : at + 1]]
        spare = jnp.concatenate(spare, axis=0).astype(jnp.bfloat16)
        out_ref[2 * slices : 2 * slices + 8, cols] = spare


def window_rows(block, position, local_blocks, slab):
    part = local_blocks * slab
    piece = 2 * part
    core = lax.rem(position, 2)
    chip = position // 2
    owner = block // local_blocks
    owner_core = lax.rem(owner, 2)
    delta = owner // 2 - chip
    flag = lambda what: jnp.where(what, 1, 0)
    up = flag(delta > 0)
    nearer = jnp.abs(delta) == 1
    is_y = flag(up == 1 - lax.rem(chip, 2))
    is_a = flag(up == flag(lax.rem(chip, 4) < 2))
    short = jnp.where(nearer, is_y, is_a)
    via = jnp.where(nearer, 1 - is_y, is_a)
    away = (2 * jnp.abs(via - core) + short) * piece + jnp.abs(owner_core - via) * part
    here = 4 * piece + jnp.abs(owner_core - core) * part
    return jnp.where(delta == 0, here, away) + lax.rem(block, local_blocks) * slab


class Scalars:
    def __init__(self, ref):
        self.ref = ref
        self.slots = (ref.shape[0] - 2) // 2
        self.views = ref.shape[1]

    def each_pair(self, first_row, rows, do):
        def body(view, carry):
            count = self.ref[2 * self.slots, view]
            angle = self.ref[2 * self.slots + 1, view]
            for slot in range(self.slots):
                row = self.ref[slot, view]

                @pl.when((slot < count) & (row >= first_row) & (row < first_row + rows))
                def _():
                    do(view, angle, self.ref[self.slots + slot, view], row - first_row)

            return carry

        lax.fori_loop(0, self.views, body, 0)


def place(scal, sino, proj, first_row, rows, slab):
    det_rows = sino.shape[1] // scal.views

    def add(view, angle, offset, local):
        source = pl.multiple_of(angle * rows + local, slab)
        target = pl.ds(view * det_rows + offset, slab)
        for tile in range(sino.shape[0]):
            cols = slice(tile * 128, (tile + 1) * 128)
            sino[tile, target, :] += proj[pl.ds(source, slab), cols]

    scal.each_pair(first_row, rows, add)


def gather(scal, sino, decay, sums, first_row, rows, slab):
    det_rows = sino.shape[1] // scal.views

    def add(view, angle, offset, local):
        source = pl.ds(view * det_rows + offset, slab)
        target = pl.ds(pl.multiple_of(angle * rows + local, slab), slab)
        for tile in range(sino.shape[0]):
            cols = slice(tile * 128, (tile + 1) * 128)
            value = (decay[tile, source, :] * sino[tile, source, :]).astype(jnp.bfloat16)
            sums[target, cols] += value.astype(jnp.float32)

    scal.each_pair(first_row, rows, add)


def back_project(sums, turned_ref, group):
    total = None
    for table in range(turned_ref.shape[0]):
        value = sums[table * group : (table + 1) * group, :]
        high = value.astype(jnp.bfloat16)
        low = (value - high.astype(jnp.float32)).astype(jnp.bfloat16)
        both = jnp.concatenate([high, low], axis=0)
        got = jnp.dot(both, turned_ref[table], preferred_element_type=jnp.float32)
        got = got[:group] + got[group:]
        total = got if total is None else total + got
    return total


def early_kernel(
    both_ref,
    table_hbm,
    measured_hbm,
    cover_hbm,
    offset_hbm,
    count_hbm,
    angle_hbm,
    table_ref,
    turned_ref,
    scal_ref,
    sino_ref,
    decay_ref,
    measured,
    cover,
    offset,
    count,
    angle,
    scal,
    proj,
    sems,
    *,
    local_blocks,
    slab,
    here,
):
    views, det_rows, channels = measured.shape
    slots = cover.shape[0]
    piece = both_ref.shape[0] - 8
    small = [(cover_hbm, cover), (offset_hbm, offset), (count_hbm, count), (angle_hbm, angle)]
    copies = [pltpu.make_async_copy(a, b, sems.at[i]) for i, (a, b) in enumerate(small)]
    copies.append(pltpu.make_async_copy(measured_hbm, measured, sems.at[4]))
    for table in range(table_ref.shape[0]):
        copies.append(
            pltpu.make_async_copy(table_hbm.at[table], table_ref.at[table], sems.at[5 + table])
        )
    for copy in copies:
        copy.start()
    for copy in copies[:4]:
        copy.wait()
    scal_ref[0:slots, :] = window_rows(cover[...], here(), local_blocks, slab)
    scal_ref[slots : 2 * slots, :] = offset[...]
    scal_ref[2 * slots : 2 * slots + 1, :] = count[...]
    scal_ref[2 * slots + 1 : 2 * slots + 2, :] = angle[...]
    load = fetch(scal_ref, scal, sems.at[0])
    copies[4].wait()

    def fade(view, carry):
        rows = pl.ds(pl.multiple_of(view * det_rows, det_rows), det_rows)
        for tile in range(sino_ref.shape[0]):
            seen = measured[view, :, tile * 128 : (tile + 1) * 128].astype(jnp.float32)
            decay_ref[tile, rows, :] = jnp.exp(-seen)
            sino_ref[tile, rows, :] = -seen
        return carry

    lax.fori_loop(0, views, fade, 0)
    for table in range(table_ref.shape[0]):
        copies[5 + table].wait()
        turned_ref[table] = table_ref[table].T
        proj[table * piece : (table + 1) * piece, :] = jnp.dot(
            both_ref[0:piece, :], table_ref[table], preferred_element_type=jnp.float32
        )
    load.wait()
    place(Scalars(scal), sino_ref, proj, 4 * piece, piece, slab)


def project_into(sino_ref, begun_ref, scal, load, proj, pieces, table_ref, first_row, slab):
    rows = sum(piece.shape[0] for piece in pieces)
    sino_ref[...] = begun_ref[...]
    window = pieces[0] if len(pieces) == 1 else jnp.concatenate(pieces, axis=0)
    for table in range(table_ref.shape[0]):
        proj[table * rows : (table + 1) * rows, :] = jnp.dot(
            window, table_ref[table], preferred_element_type=jnp.float32
        )
    load.wait()
    place(scal, sino_ref, proj, first_row, rows, slab)


def fetch(scal_ref, scal, sem):
    load = pltpu.make_async_copy(scal_ref, scal, sem)
    load.start()
    return load


def middle_kernel(
    scal_ref, long_ref, short_ref, table_ref, begun_ref, sino_ref, scal, proj, sem, *, slab
):
    load = fetch(scal_ref, scal, sem)
    piece = long_ref.shape[0] - 8
    pieces = [long_ref[0:piece, :], short_ref[0:piece, :]]
    project_into(sino_ref, begun_ref, Scalars(scal), load, proj, pieces, table_ref, 0, slab)


def main_kernel(
    scal_ref,
    long_ref,
    short_ref,
    table_ref,
    turned_ref,
    begun_ref,
    decay_ref,
    sino_ref,
    give_ref,
    scal,
    proj,
    sums,
    sem,
    *,
    slab,
):
    load = fetch(scal_ref, scal, sem)
    piece = long_ref.shape[0] - 8
    sums[...] = jnp.zeros_like(sums)
    index = Scalars(scal)
    pieces = [long_ref[0:piece, :], short_ref[0:piece, :]]
    project_into(sino_ref, begun_ref, index, load, proj, pieces, table_ref, 2 * piece, slab)
    gather(index, sino_ref, decay_ref, sums, 2 * piece, 2 * piece, slab)
    give_ref[...] = back_project(sums, turned_ref, 2 * piece)


def rest_kernel(
    scal_ref, turned_ref, sino_ref, decay_ref, out_ref, scal, sums, sem, *, first_row, slab
):
    load = fetch(scal_ref, scal, sem)
    sums[...] = jnp.zeros_like(sums)
    rows = out_ref.shape[0]
    load.wait()
    gather(Scalars(scal), sino_ref, decay_ref, sums, first_row, rows, slab)
    out_ref[...] = back_project(sums, turned_ref, rows)


def prior_kernel(
    vol_ref, other_ref, long_ref, far_long_ref, short_ref, far_short_ref, out_ref, *, devices, here
):
    slices, strip, row = vol_ref.shape
    part = slices
    piece = 2 * part
    position = here()
    core = lax.rem(position, 2)
    odd = lax.rem(position // 2, 2)

    def chip_slice(ref, which, via):
        sub = which ^ via
        at = sub * part + (part - 1) * which
        tail = piece + 4 * sub + 2 * which
        whole = ref[at : at + 1, :].astype(jnp.float32)
        more = ref[tail : tail + 2, :].astype(jnp.float32)
        whole = whole + (more[0:1] + more[1:2])
        return lambda y: whole[:, y * row : (y + 1) * row]

    def core_slice(which):
        at = (part - 1) * which
        return lambda y: other_ref[at : at + 1, y, :]

    def emit(low, high):
        for y in range(strip):
            cols = slice(y * row, (y + 1) * row)
            here = vol_ref[:, y, :]
            below = jnp.concatenate([low(y), here[:-1]], axis=0)
            above = jnp.concatenate([here[1:], high(y)], axis=0)
            level = lax.broadcasted_iota(jnp.int32, here.shape, 0)
            down = jnp.clip(here - below, -DELTA, DELTA)
            total = jnp.where((level > 0) | (position > 0), down, 0.0)
            up = jnp.clip(here - above, -DELTA, DELTA)
            total += jnp.where((level < slices - 1) | (position < devices - 1), up, 0.0)
            if y > 0:
                total += jnp.clip(here - vol_ref[:, y - 1, :], -DELTA, DELTA)
            if y + 1 < strip:
                total += jnp.clip(here - vol_ref[:, y + 1, :], -DELTA, DELTA)
            lane = lax.broadcasted_iota(jnp.int32, here.shape, 1)
            left = jnp.clip(here - pltpu.roll(here, 1, 1), -DELTA, DELTA)
            total += jnp.where(lane > 0, left, 0.0)
            right = jnp.clip(here - pltpu.roll(here, row - 1, 1), -DELTA, DELTA)
            total += jnp.where(lane < row - 1, right, 0.0)
            out_ref[:, cols] = PRIOR_WEIGHT * total

    @pl.when((core == 0) & (odd == 0))
    def _():
        emit(chip_slice(far_long_ref, 1, 1), core_slice(0))

    @pl.when((core == 0) & (odd == 1))
    def _():
        emit(chip_slice(short_ref, 1, 0), core_slice(0))

    @pl.when((core == 1) & (odd == 0))
    def _():
        emit(core_slice(1), chip_slice(far_short_ref, 0, 0))

    @pl.when((core == 1) & (odd == 1))
    def _():
        emit(core_slice(1), chip_slice(long_ref, 0, 1))


def last_kernel(arrived_ref, passed_ref, prior_ref, out_ref):
    part, strip, row = out_ref.shape
    for y in range(strip):
        cols = slice(y * row, (y + 1) * row)
        out_ref[:, y, :] = (arrived_ref[:, cols] + passed_ref[:, cols]) + prior_ref[:, cols]


def shards(volume, footprint, measured, angle_index, cover, offset, count):
    local_blocks, slab, strip, row = volume.shape
    views, det_rows, channels = measured.shape
    tables = footprint.shape[0]
    slots = cover.shape[1]
    plane = strip * row
    devices = lax.axis_size(AXES)
    position = lax.axis_index(AXES)
    swap, long, short = exchange_pairs(devices)
    send = lambda value, pairs: lax.ppermute(value, AXES, pairs)
    part = local_blocks * slab
    piece = 2 * part
    flat = volume.reshape(part, strip, row)
    table = footprint.reshape(tables, plane, channels)
    vmem = pl.BlockSpec(memory_space=pltpu.VMEM)
    smem = pl.BlockSpec(memory_space=pltpu.SMEM)
    shape = jax.ShapeDtypeStruct
    room = lambda mib: pltpu.CompilerParams(vmem_limit_bytes=mib * 1024 * 1024)
    cost = lambda flops, size: pl.CostEstimate(flops=flops, bytes_accessed=size, transcendentals=0)

    here = lambda: lax.axis_index("grp") * lax.axis_size("view") + lax.axis_index("view")
    hbm = pl.BlockSpec(memory_space=pltpu.HBM)
    stay = lambda value: pltpu.with_memory_space_constraint(value, pltpu.HBM)

    other = send(flat, swap)
    mine = pl.pallas_call(
        load_kernel,
        out_shape=shape(flat.shape, flat.dtype),
        in_specs=[hbm],
        out_specs=vmem,
        scratch_shapes=[pltpu.SemaphoreType.DMA],
        compiler_params=room(4),
        cost_estimate=cost(1, 1),
        name="load",
    )(stay(flat))
    other, mine = lax.optimization_barrier((other, mine))
    both = pl.pallas_call(
        join_kernel,
        out_shape=shape((piece + 8, plane), jnp.bfloat16),
        in_specs=[vmem] * 2,
        out_specs=vmem,
        compiler_params=room(4),
        name="join",
    )(mine, other)
    got_short = send(both, short)
    got_long = send(both, long)

    sino_shape = shape((channels // 128, views * det_rows, 128), jnp.float32)
    scal_shape = (2 * slots + 2, views)
    table_vmem, turned, scalars, sino, decay = pl.pallas_call(
        functools.partial(early_kernel, local_blocks=local_blocks, slab=slab, here=here),
        out_shape=(
            shape(table.shape, table.dtype),
            shape((tables, channels, plane), table.dtype),
            shape(scal_shape, jnp.int32),
            sino_shape,
            sino_shape,
        ),
        in_specs=[vmem] + [hbm] * 6,
        out_specs=(vmem,) * 5,
        scratch_shapes=[
            pltpu.VMEM(measured.shape, measured.dtype),
            pltpu.VMEM((slots, views), jnp.int32),
            pltpu.VMEM((slots, views), jnp.int32),
            pltpu.VMEM((1, views), jnp.int32),
            pltpu.VMEM((1, views), jnp.int32),
            pltpu.SMEM(scal_shape, jnp.int32),
            pltpu.VMEM((tables * piece, channels), jnp.float32),
            pltpu.SemaphoreType.DMA((5 + tables,)),
        ],
        compiler_params=room(16),
        cost_estimate=cost(1, 1),
        name="early",
    )(
        both,
        stay(table),
        stay(measured),
        stay(cover.T),
        stay(offset.T),
        stay(count.reshape(1, views)),
        stay(angle_index.reshape(1, views)),
    )
    got_short, got_long, table_vmem, turned, scalars, sino, decay = lax.optimization_barrier(
        (got_short, got_long, table_vmem, turned, scalars, sino, decay)
    )
    index = [pltpu.SMEM(scal_shape, jnp.int32)]
    waits = [pltpu.SemaphoreType.DMA]
    proj = lambda rows: [pltpu.VMEM((tables * rows, channels), jnp.float32)]
    sums = lambda rows: [pltpu.VMEM((tables * rows, channels), jnp.float32)]

    far_short = send(got_short, swap)
    far_long = send(got_long, swap)
    sino = pl.pallas_call(
        functools.partial(middle_kernel, slab=slab),
        out_shape=sino_shape,
        in_specs=[vmem] * 5,
        out_specs=vmem,
        scratch_shapes=index + proj(2 * piece) + waits,
        compiler_params=room(16),
        cost_estimate=cost(1, 1),
        name="middle",
    )(scalars, got_long, got_short, table_vmem, sino)
    far_short, far_long, sino = lax.optimization_barrier((far_short, far_long, sino))
    sino, give = pl.pallas_call(
        functools.partial(main_kernel, slab=slab),
        out_shape=(sino_shape, shape((2 * piece, plane), jnp.float32)),
        in_specs=[vmem] * 7,
        out_specs=(vmem, vmem),
        scratch_shapes=index + proj(2 * piece) + sums(2 * piece) + waits,
        compiler_params=room(16),
        cost_estimate=cost(1, 1),
        name="main",
    )(scalars, far_long, far_short, table_vmem, turned, sino, decay)
    taken = send(give, swap)
    keep = pl.pallas_call(
        functools.partial(rest_kernel, first_row=0, slab=slab),
        out_shape=shape((2 * piece, plane), jnp.float32),
        in_specs=[vmem] * 4,
        out_specs=vmem,
        scratch_shapes=index + sums(2 * piece) + waits,
        compiler_params=room(16),
        cost_estimate=cost(1, 1),
        name="rest",
    )(scalars, turned, sino, decay)
    taken, keep = lax.optimization_barrier((taken, keep))
    wire = (keep + taken).astype(jnp.bfloat16)
    back_short = send(wire[piece:], short)
    back_long = send(wire[:piece], long)

    home = pl.pallas_call(
        functools.partial(rest_kernel, first_row=4 * piece, slab=slab),
        out_shape=shape((piece, plane), jnp.float32),
        in_specs=[vmem] * 4,
        out_specs=vmem,
        scratch_shapes=index + sums(piece) + waits,
        compiler_params=room(16),
        cost_estimate=cost(1, 1),
        name="home",
    )(scalars, turned, sino, decay)
    prior = pl.pallas_call(
        functools.partial(prior_kernel, devices=devices, here=here),
        out_shape=shape((part, plane), jnp.float32),
        in_specs=[vmem] * 6,
        out_specs=vmem,
        compiler_params=room(8),
        cost_estimate=cost(1, 1),
        name="prior",
    )(mine, other, got_long, far_long, got_short, far_short)
    back_short, back_long, home, prior = lax.optimization_barrier(
        (back_short, back_long, home, prior)
    )

    arrived = (back_short.astype(jnp.float32) + back_long.astype(jnp.float32)) + home
    passed = send(arrived[part:], swap)
    out = pl.pallas_call(
        last_kernel,
        out_shape=shape((part, strip, row), jnp.float32),
        in_specs=[vmem] * 3,
        out_specs=vmem,
        compiler_params=room(4),
        name="last",
    )(arrived[:part], passed, prior)
    return out.reshape(volume.shape)


def solution(mesh):
    in_specs = (
        P(AXES, None, None, None),
        P(AXES, None, None, None),
        P(AXES, None, None),
        P(AXES),
        P(AXES, None),
        P(AXES, None),
        P(AXES),
    )
    out_specs = P(AXES, None, None, None)
    return jax.shard_map(shards, mesh=mesh, in_specs=in_specs, out_specs=out_specs, check_vma=False)
```

time: 95.3 us -> 31.3 us (0.33); the launches traced: 93.5 us -> 31.1 us
  starting transfers between devices: 60.4 us -> 10.8 us
  Pallas kernels: 0 us -> 14.2 us
  local copies, waits for them, and re-layouts: 13.1 us -> 0.04 us
  matrix products: 11.7 us -> 0 us
  other arithmetic: 5.06 us -> 0.1 us
  waiting for transfers between devices: 2.71 us -> 5.85 us
    ppermute x18 -> x9, starting transfers between devices: 60.4 us -> 10.8 us  [shards(): send = lambda value, pairs: lax.ppermute(value, AXES, pairs)]
    pallas_call x0 -> x9, Pallas kernels: none -> 14.2 us  [the longest x1 3.55 us: shards(): pl.pallas_call(functools.partial(early_kernel, local_blocks=local_blocks,...]
    dot_general x8 -> x0, matrix products: 11.7 us -> none  [the longest x2 3.91 us: shards(): lax.dot_general(masked, tables[table], (((1,), (1,)), ((), ())), preferre...]
    slice x3 -> x2, local copies, waits for them, and re-layouts: 4.74 us -> 0.04 us  [the longest x1 0.02 us: shards(): back_long = send(wire[:piece], long)]
    reshape x2 -> x0, local copies, waits for them, and re-layouts: 3.47 us -> none  [the longest x1 1.75 us: shards(): back = back.reshape(view_count * slot_count, slab_rows * plane)]
    ppermute x18 -> x9, waiting for transfers between devices: 2.71 us -> 5.85 us  [shards(): send = lambda value, pairs: lax.ppermute(value, AXES, pairs)]
    unnamed x30 -> x0, local copies, waits for them, and re-layouts: 2.97 us -> none
    another operation x1 -> x0, other arithmetic: 1.49 us -> none  [shards(): jnp.stack([jnp.dot(win_rows, tables[table], preferred_element_type=jnp.fl...]
  transfers between devices with their start and end apart: 18 -> 9, of which waited for: 1 -> 6; matrix products, arithmetic and copies ran while one was open for 28% -> 0% of each run, Pallas kernels for 0% -> 33%
where the time goes in v3:
time: 31.3 us; the launch traced here: 31.1 us
  Pallas kernels  14.2 us (45%)
  starting transfers between devices  10.8 us (35%)
  waiting for transfers between devices  5.85 us (19%)
    ppermute x9, starting transfers between devices, shards(): send = lambda value, pairs: lax.ppermute(value, AXES, pairs)  10.8 us
    ppermute x9, waiting for transfers between devices, shards(): send = lambda value, pairs: lax.ppermute(value, AXES, pairs)  5.85 us
    pallas_call x1, Pallas kernels, shards(): pl.pallas_call(functools.partial(early_kernel, local_blocks=local_blocks,...  3.55 us
    pallas_call x1, Pallas kernels, shards(): pl.pallas_call(functools.partial(main_kernel, slab=slab), out_shape=(sino...  3.04 us
    pallas_call x1, Pallas kernels, shards(): pl.pallas_call(functools.partial(rest_kernel, first_row=0, slab=slab), ou...  2.41 us
    pallas_call x1, Pallas kernels, shards(): pl.pallas_call(functools.partial(rest_kernel, first_row=4 * piece, slab=s...  1.8 us
    pallas_call x1, Pallas kernels, shards(): pl.pallas_call(functools.partial(middle_kernel, slab=slab), out_shape=sin...  1.25 us
    pallas_call x1, Pallas kernels, shards(): pl.pallas_call(load_kernel, out_shape=shape(flat.shape, flat.dtype), in_s...  0.91 us
  transfers between devices with their start and end apart: 9, of which 6 were waited for; matrix products, arithmetic and copies ran while one was open for 0% of the time, Pallas kernels for 33%

profile of v3, /device:TPU:3, one launch (start us, length us, event | category | flops | bytes accessed | tf_op | source)
XLA Modules:
  0.0 31.1 jit_solution(10132501101711922613)
XLA Ops:
  0.0 0.7 %collective-permute-start = (f32[32,2,512]{2,1,0:T(2,128)}, f32[32,2,512]{2,1,0:T(2,128)S(1)}, u32[]{:S(2)}, u32[]{:S(2)}) collective-permute-start(f32[32,2,512]{2,1,0:T(2,128)} %bitcast.8), channel_id=1, source_target_pairs={{0,1},{1,0},{2,3},{3,2},{4,5},{5,4},{6,7},{7,6},{8,9},{9,8},{10,11... | collective-permute-start | bytes 393224 | tf_op jit(solution)/shard_map/ppermute | solution.py:349
  0.7 0.9 %load.1.own_ref.vol_ref = f32[32,2,512]{2,1,0:T(2,128)S(1)} custom-call(f32[32,2,512]{2,1,0:T(2,128)} %bitcast.9), custom_call_target="tpu_custom_call" | custom-call | flops 1 | bytes 1 | tf_op jit(solution)/shard_map/load/pallas_call | solution.py:365
  1.6 0.3 collective-permute-done.other_ref
  1.9 0.3 join.1.both_ref
  2.2 4.3 %collective-permute-start.2 = (bf16[72,1024]{1,0:T(8,128)(2,1)S(1)}, bf16[72,1024]{1,0:T(8,128)(2,1)S(1)}, u32[]{:S(2)}, u32[]{:S(2)}) collective-permute-start(bf16[72,1024]{1,0:T(8,128)(2,1)S(1)} %join.1.both_ref), channel_id=1, source_target_pairs={{4,8},{6,10},{12,16},{14,18},{20,24},{22,26},{3,5},{7,9},{11,13},{... | collective-permute-start | bytes 442376 | tf_op jit(solution)/shard_map/ppermute | solution.py:349
  6.5 0.0 collective-permute-start.1
  6.5 3.6 %early.1 = (bf16[2,1024,896]{2,1,0:T(8,128)(2,1)S(1)}, bf16[2,896,1024]{2,1,0:T(8,128)(2,1)S(1)}, s32[10,8]{1,0:T(8,128)S(1)}, f32[7,512,128]{2,1,0:T(8,128)S(1)}, f32[7,512,128]{2,1,0:T(8,128)S(1)}) custom-call(bf16[72,1024]{1,0:T(8,128)(2,1)S(1)} %join.1.both_ref, bf16[2,1024,896]{2,1,0:T(8,128)(2,1)} %bitcast.7, bf16[8,64,896]{2,1,0:T(8,128)(2,1)} %measured_hbm.1, ...), custom_call_target="tpu_custom_call" | custom-call | flops 1 | bytes 1 | tf_op jit(solution)/shard_map/early/pallas_call | solution.py:389
  10.0 0.6 %collective-permute-done.2.long_ref = bf16[72,1024]{1,0:T(8,128)(2,1)S(1)} collective-permute-done((bf16[72,1024]{1,0:T(8,128)(2,1)S(1)}, bf16[72,1024]{1,0:T(8,128)(2,1)S(1)}, u32[]{:S(2)}, u32[]{:S(2)}) %collective-permute-start.2) | collective-permute-done | bytes 147488 | tf_op jit(solution)/shard_map/ppermute | solution.py:349
  10.7 0.9 %collective-permute-done.1.short_ref = bf16[72,1024]{1,0:T(8,128)(2,1)S(1)} collective-permute-done((bf16[72,1024]{1,0:T(8,128)(2,1)S(1)}, bf16[72,1024]{1,0:T(8,128)(2,1)S(1)}, u32[]{:S(2)}, u32[]{:S(2)}) %collective-permute-start.1) | collective-permute-done | bytes 147488 | tf_op jit(solution)/shard_map/ppermute | solution.py:349
  11.6 0.7 %collective-permute-start.3 = (bf16[72,1024]{1,0:T(8,128)(2,1)S(1)}, bf16[72,1024]{1,0:T(8,128)(2,1)S(1)}, u32[]{:S(2)}, u32[]{:S(2)}) collective-permute-start(bf16[72,1024]{1,0:T(8,128)(2,1)S(1)} %collective-permute-done.1.short_ref), channel_id=1, source_target_pairs={{0,1},{1,0},{2,3},{3,2},{4,5},{5,4},{6,7},{7,6},{8,9},{9,8},{10,11... | collective-permute-start | bytes 442376 | tf_op jit(solution)/shard_map/ppermute | solution.py:349
  12.2 0.0 collective-permute-start.4
  12.3 1.2 %middle.1.begun_ref = f32[7,512,128]{2,1,0:T(8,128)S(1)} custom-call(s32[10,8]{1,0:T(8,128)S(1)} %get-tuple-element.37.scal_ref, bf16[72,1024]{1,0:T(8,128)(2,1)S(1)} %collective-permute-done.2.long_ref, bf16[72,1024]{1,0:T(8,128)(2,1)S(1)} %collective-permute-done.1.short_ref, bf16[2,1024,896]{2,1,0:T(8,128)(2,1)S(1)} %get-tuple-element.40.table_ref, ...), custom_call_target="tpu_custom_call" | custom-call | flops 1 | bytes 1 | tf_op jit(solution)/shard_map/middle/pallas_call | solution.py:432
  13.5 0.0 collective-permute-done.3.short_ref.far_short_ref
  13.5 0.1 collective-permute-done.4.long_ref.far_long_ref
  13.6 3.0 %main.1 = (f32[7,512,128]{2,1,0:T(8,128)S(1)}, f32[128,1024]{1,0:T(8,128)S(1)}) custom-call(s32[10,8]{1,0:T(8,128)S(1)} %get-tuple-element.37.scal_ref, bf16[72,1024]{1,0:T(8,128)(2,1)S(1)} %collective-permute-done.4.long_ref.far_long_ref, bf16[72,1024]{1,0:T(8,128)(2,1)S(1)} %collective-permute-done.3.short_ref.far_short_ref, ...), custom_call_target="tpu_custom_call" | custom-call | flops 1 | bytes 1 | tf_op jit(solution)/shard_map/main/pallas_call | solution.py:443
  16.7 0.5 %collective-permute-start.5 = (f32[128,1024]{1,0:T(8,128)S(1)}, f32[128,1024]{1,0:T(8,128)S(1)}, u32[]{:S(2)}, u32[]{:S(2)}) collective-permute-start(f32[128,1024]{1,0:T(8,128)S(1)} %get-tuple-element.47), channel_id=1, source_target_pairs={{0,1},{1,0},{2,3},{3,2},{4,5},{5,4},{6,7},{7,6},{8,9},{9,8},{10,11... | collective-permute-start | bytes 1572872 | tf_op jit(solution)/shard_map/ppermute | solution.py:349
  17.2 2.4 %rest.1 = f32[128,1024]{1,0:T(8,128)S(1)} custom-call(s32[10,8]{1,0:T(8,128)S(1)} %get-tuple-element.37.scal_ref, bf16[2,896,1024]{2,1,0:T(8,128)(2,1)S(1)} %get-tuple-element.44.turned_ref, f32[7,512,128]{2,1,0:T(8,128)S(1)} %get-tuple-element.48.sino_ref, f32[7,512,128]{2,1,0:T(8,128)S(1)} %get-tuple-element.46.decay_ref), custom_call_target="tpu_custom_call" | custom-call | flops 1 | bytes 1 | tf_op jit(solution)/shard_map/rest/pallas_call | solution.py:454
  19.6 0.0 collective-permute-done.5
  19.6 0.1 add_convert_fusion
  19.7 3.6 %collective-permute-start.7 = (bf16[64,1024]{1,0:T(8,128)(2,1)S(1)}, bf16[64,1024]{1,0:T(8,128)(2,1)S(1)}, u32[]{:S(2)}, u32[]{:S(2)}) collective-permute-start(bf16[64,1024]{1,0:T(8,128)(2,1)S(1)} %get-tuple-element.57), channel_id=1, source_target_pairs={{4,8},{6,10},{12,16},{14,18},{20,24},{22,26},{3,5},{7,9},{11,13},{... | collective-permute-start | bytes 393224 | tf_op jit(solution)/shard_map/ppermute | solution.py:349
  23.3 0.0 collective-permute-start.6
  23.3 0.2 prior.1.prior_ref
  23.5 1.8 %home.1 = f32[64,1024]{1,0:T(8,128)S(1)} custom-call(s32[10,8]{1,0:T(8,128)S(1)} %get-tuple-element.37.scal_ref, bf16[2,896,1024]{2,1,0:T(8,128)(2,1)S(1)} %get-tuple-element.44.turned_ref, f32[7,512,128]{2,1,0:T(8,128)S(1)} %get-tuple-element.48.sino_ref, f32[7,512,128]{2,1,0:T(8,128)S(1)} %get-tuple-element.46.decay_ref), custom_call_target="tpu_custom_call" | custom-call | flops 1 | bytes 1 | tf_op jit(solution)/shard_map/home/pallas_call | solution.py:469
  25.3 2.9 %collective-permute-done.7 = bf16[64,1024]{1,0:T(8,128)(2,1)S(1)} collective-permute-done((bf16[64,1024]{1,0:T(8,128)(2,1)S(1)}, bf16[64,1024]{1,0:T(8,128)(2,1)S(1)}, u32[]{:S(2)}, u32[]{:S(2)}) %collective-permute-start.7) | collective-permute-done | bytes 131104 | tf_op jit(solution)/shard_map/ppermute | solution.py:349
  28.2 0.0 collective-permute-done.6
  28.3 1.1 %collective-permute-start.8 = (f32[32,1024]{1,0:T(8,128)S(1)}, f32[32,1024]{1,0:T(8,128)S(1)}, u32[]{:S(2)}, u32[]{:S(2)}) collective-permute-start(f32[32,1024]{1,0:T(8,128)S(1)} %get-tuple-element.55), channel_id=1, source_target_pairs={{0,1},{1,0},{2,3},{3,2},{4,5},{5,4},{6,7},{7,6},{8,9},{9,8},{10,11... | collective-permute-start | bytes 393224 | tf_op jit(solution)/shard_map/ppermute | solution.py:349
  29.4 1.0 %collective-permute-done.8.passed_ref = f32[32,1024]{1,0:T(8,128)S(1)} collective-permute-done((f32[32,1024]{1,0:T(8,128)S(1)}, f32[32,1024]{1,0:T(8,128)S(1)}, u32[]{:S(2)}, u32[]{:S(2)}) %collective-permute-start.8) | collective-permute-done | bytes 131104 | tf_op jit(solution)/shard_map/ppermute | solution.py:349
  30.4 0.7 %last.1 = f32[32,2,512]{2,1,0:T(2,128)} custom-call(f32[32,1024]{1,0:T(8,128)S(1)} %get-tuple-element.56.arrived_ref, f32[32,1024]{1,0:T(8,128)S(1)} %collective-permute-done.8.passed_ref, f32[32,1024]{1,0:T(8,128)S(1)} %prior.1.prior_ref), custom_call_target="tpu_custom_call" | custom-call | tf_op jit(solution)/shard_map/last/pallas_call | solution.py:494
  (3 shorter events, 0.1 us)
Async XLA Ops:
  0.0 1.9 %collective-permute-start = (f32[32,2,512]{2,1,0:T(2,128)}, f32[32,2,512]{2,1,0:T(2,128)S(1)}, u32[]{:S(2)}, u32[]{:S(2)}) collective-permute-start(f32[32,2,512]{2,1,0:T(2,128)} %bitcast.8), channel_id=1, source_target_pairs={{0,1},{1,0},{2,3},{3,2},{4,5},{5,4},{6,7},{7,6},{8,9},{9,8},{10,11... | collective-permute-start | bytes 393224 | tf_op jit(solution)/shard_map/ppermute | solution.py:349
  2.2 8.5 %collective-permute-start.2 = (bf16[72,1024]{1,0:T(8,128)(2,1)S(1)}, bf16[72,1024]{1,0:T(8,128)(2,1)S(1)}, u32[]{:S(2)}, u32[]{:S(2)}) collective-permute-start(bf16[72,1024]{1,0:T(8,128)(2,1)S(1)} %join.1.both_ref), channel_id=1, source_target_pairs={{4,8},{6,10},{12,16},{14,18},{20,24},{22,26},{3,5},{7,9},{11,13},{... | collective-permute-start | bytes 442376 | tf_op jit(solution)/shard_map/ppermute | solution.py:349
  6.5 5.1 %collective-permute-start.1 = (bf16[72,1024]{1,0:T(8,128)(2,1)S(1)}, bf16[72,1024]{1,0:T(8,128)(2,1)S(1)}, u32[]{:S(2)}, u32[]{:S(2)}) collective-permute-start(bf16[72,1024]{1,0:T(8,128)(2,1)S(1)} %join.1.both_ref), channel_id=1, source_target_pairs={{0,2},{4,6},{8,10},{12,14},{16,18},{20,22},{24,26},{28,30},{1,5},{... | collective-permute-start | bytes 442376 | tf_op jit(solution)/shard_map/ppermute | solution.py:349
  11.6 1.9 %collective-permute-start.3 = (bf16[72,1024]{1,0:T(8,128)(2,1)S(1)}, bf16[72,1024]{1,0:T(8,128)(2,1)S(1)}, u32[]{:S(2)}, u32[]{:S(2)}) collective-permute-start(bf16[72,1024]{1,0:T(8,128)(2,1)S(1)} %collective-permute-done.1.short_ref), channel_id=1, source_target_pairs={{0,1},{1,0},{2,3},{3,2},{4,5},{5,4},{6,7},{7,6},{8,9},{9,8},{10,11... | collective-permute-start | bytes 442376 | tf_op jit(solution)/shard_map/ppermute | solution.py:349
  12.2 1.4 %collective-permute-start.4 = (bf16[72,1024]{1,0:T(8,128)(2,1)S(1)}, bf16[72,1024]{1,0:T(8,128)(2,1)S(1)}, u32[]{:S(2)}, u32[]{:S(2)}) collective-permute-start(bf16[72,1024]{1,0:T(8,128)(2,1)S(1)} %collective-permute-done.2.long_ref), channel_id=1, source_target_pairs={{0,1},{1,0},{2,3},{3,2},{4,5},{5,4},{6,7},{7,6},{8,9},{9,8},{10,11... | collective-permute-start | bytes 442376 | tf_op jit(solution)/shard_map/ppermute | solution.py:349
  16.7 2.9 %collective-permute-start.5 = (f32[128,1024]{1,0:T(8,128)S(1)}, f32[128,1024]{1,0:T(8,128)S(1)}, u32[]{:S(2)}, u32[]{:S(2)}) collective-permute-start(f32[128,1024]{1,0:T(8,128)S(1)} %get-tuple-element.47), channel_id=1, source_target_pairs={{0,1},{1,0},{2,3},{3,2},{4,5},{5,4},{6,7},{7,6},{8,9},{9,8},{10,11... | collective-permute-start | bytes 1572872 | tf_op jit(solution)/shard_map/ppermute | solution.py:349
  19.7 8.5 %collective-permute-start.7 = (bf16[64,1024]{1,0:T(8,128)(2,1)S(1)}, bf16[64,1024]{1,0:T(8,128)(2,1)S(1)}, u32[]{:S(2)}, u32[]{:S(2)}) collective-permute-start(bf16[64,1024]{1,0:T(8,128)(2,1)S(1)} %get-tuple-element.57), channel_id=1, source_target_pairs={{4,8},{6,10},{12,16},{14,18},{20,24},{22,26},{3,5},{7,9},{11,13},{... | collective-permute-start | bytes 393224 | tf_op jit(solution)/shard_map/ppermute | solution.py:349
  23.3 5.0 %collective-permute-start.6 = (bf16[64,1024]{1,0:T(8,128)(2,1)S(1)}, bf16[64,1024]{1,0:T(8,128)(2,1)S(1)}, u32[]{:S(2)}, u32[]{:S(2)}) collective-permute-start(bf16[64,1024]{1,0:T(8,128)(2,1)S(1)} %get-tuple-element.58), channel_id=1, source_target_pairs={{0,2},{4,6},{8,10},{12,14},{16,18},{20,22},{24,26},{28,30},{1,5},{... | collective-permute-start | bytes 393224 | tf_op jit(solution)/shard_map/ppermute | solution.py:349
  28.3 2.1 %collective-permute-start.8 = (f32[32,1024]{1,0:T(8,128)S(1)}, f32[32,1024]{1,0:T(8,128)S(1)}, u32[]{:S(2)}, u32[]{:S(2)}) collective-permute-start(f32[32,1024]{1,0:T(8,128)S(1)} %get-tuple-element.55), channel_id=1, source_target_pairs={{0,1},{1,0},{2,3},{3,2},{4,5},{5,4},{6,7},{7,6},{8,9},{9,8},{10,11... | collective-permute-start | bytes 393224 | tf_op jit(solution)/shard_map/ppermute | solution.py:349

commit v4 on v3

--- a/solution.py
+++ b/solution.py
@@ -75,66 +75,80 @@
     return jnp.where(delta == 0, here, away) + lax.rem(block, local_blocks) * slab
 
 
-class Scalars:
+class Pairs:
     def __init__(self, ref):
         self.ref = ref
-        self.slots = (ref.shape[0] - 2) // 2
-        self.views = ref.shape[1]
-
-    def each_pair(self, first_row, rows, do):
-        def body(view, carry):
-            count = self.ref[2 * self.slots, view]
-            angle = self.ref[2 * self.slots + 1, view]
-            for slot in range(self.slots):
-                row = self.ref[slot, view]
-
-                @pl.when((slot < count) & (row >= first_row) & (row < first_row + rows))
-                def _():
-                    do(view, angle, self.ref[self.slots + slot, view], row - first_row)
-
+
+    def each(self, group, do):
+        def body(i, carry):
+            do(*(self.ref[3 * group + k, i] for k in range(3)))
             return carry
 
-        lax.fori_loop(0, self.views, body, 0)
-
-
-def place(scal, sino, proj, first_row, rows, slab):
-    det_rows = sino.shape[1] // scal.views
-
-    def add(view, angle, offset, local):
-        source = pl.multiple_of(angle * rows + local, slab)
-        target = pl.ds(view * det_rows + offset, slab)
+        lax.fori_loop(0, self.ref[9, group], body, 0)
+
+
+def list_pairs(scal, lists, near_rows, det_rows):
+    slots = (scal.shape[0] - 2) // 2
+
+    def body(view, used):
+        count = scal[2 * slots, view]
+        table = scal[2 * slots + 1, view]
+        for slot in range(slots):
+            row = scal[slot, view]
+            group = jnp.minimum(row // near_rows, 2)
+            at = jnp.where(group == 0, used[0], jnp.where(group == 1, used[1], used[2]))
+
+            @pl.when(slot < count)
+            def _():
+                lists[3 * group, at] = view * det_rows + scal[slots + slot, view]
+                lists[3 * group + 1, at] = table
+                lists[3 * group + 2, at] = row
+
+            used = tuple(
+                n + jnp.where((group == k) & (slot < count), 1, 0) for k, n in enumerate(used)
+            )
+        return used
+
+    zero = jnp.int32(0)
+    used = lax.fori_loop(0, scal.shape[1], body, (zero, zero, zero))
+    for k, n in enumerate(used):
+        lists[9, k] = n
+
+
+def place(pairs, group, sino, proj, first_row, slab):
+    width = sino.shape[0] * 128
+
+    def add(target, table, row):
+        source = pl.ds(pl.multiple_of(row - first_row, slab), slab)
         for tile in range(sino.shape[0]):
-            cols = slice(tile * 128, (tile + 1) * 128)
-            sino[tile, target, :] += proj[pl.ds(source, slab), cols]
-
-    scal.each_pair(first_row, rows, add)
-
-
-def gather(scal, sino, decay, sums, first_row, rows, slab):
-    det_rows = sino.shape[1] // scal.views
-
-    def add(view, angle, offset, local):
-        source = pl.ds(view * det_rows + offset, slab)
-        target = pl.ds(pl.multiple_of(angle * rows + local, slab), slab)
+            cols = pl.ds(pl.multiple_of(table * width + tile * 128, 128), 128)
+            sino[tile, pl.ds(target, slab), :] += proj[source, cols]
+
+    pairs.each(group, add)
+
+
+def gather(pairs, group, sino, decay, sums, first_row, slab):
+    width = sino.shape[0] * 128
+
+    def add(source, table, row):
+        target = pl.ds(pl.multiple_of(row - first_row, slab), slab)
+        here = pl.ds(source, slab)
         for tile in range(sino.shape[0]):
-            cols = slice(tile * 128, (tile + 1) * 128)
-            value = (decay[tile, source, :] * sino[tile, source, :]).astype(jnp.bfloat16)
+            cols = pl.ds(pl.multiple_of(table * width + tile * 128, 128), 128)
+            value = (decay[tile, here, :] * sino[tile, here, :]).astype(jnp.bfloat16)
             sums[target, cols] += value.astype(jnp.float32)
 
-    scal.each_pair(first_row, rows, add)
-
-
-def back_project(sums, turned_ref, group):
-    total = None
-    for table in range(turned_ref.shape[0]):
-        value = sums[table * group : (table + 1) * group, :]
-        high = value.astype(jnp.bfloat16)
-        low = (value - high.astype(jnp.float32)).astype(jnp.bfloat16)
-        both = jnp.concatenate([high, low], axis=0)
-        got = jnp.dot(both, turned_ref[table], preferred_element_type=jnp.float32)
-        got = got[:group] + got[group:]
-        total = got if total is None else total + got
-    return total
+    pairs.each(group, add)
+
+
+def back_project(sums, turned_ref):
+    rows = sums.shape[0]
+    value = sums[...]
+    high = value.astype(jnp.bfloat16)
+    low = (value - high.astype(jnp.float32)).astype(jnp.bfloat16)
+    both = jnp.concatenate([high, low], axis=0)
+    got = jnp.dot(both, turned_ref[...], preferred_element_type=jnp.float32)
+    return got[:rows] + got[rows:]
 
 
 def early_kernel(
@@ -147,7 +161,7 @@
     angle_hbm,
     table_ref,
     turned_ref,
-    scal_ref,
+    lists_ref,
     sino_ref,
     decay_ref,
     measured,
@@ -155,7 +169,9 @@
     offset,
     count,
     angle,
+    index,
     scal,
+    lists,
     proj,
     sems,
     *,
@@ -165,23 +181,23 @@
 ):
     views, det_rows, channels = measured.shape
     slots = cover.shape[0]
+    tables = table_hbm.shape[0]
     piece = both_ref.shape[0] - 8
     small = [(cover_hbm, cover), (offset_hbm, offset), (count_hbm, count), (angle_hbm, angle)]
     copies = [pltpu.make_async_copy(a, b, sems.at[i]) for i, (a, b) in enumerate(small)]
     copies.append(pltpu.make_async_copy(measured_hbm, measured, sems.at[4]))
-    for table in range(table_ref.shape[0]):
-        copies.append(
-            pltpu.make_async_copy(table_hbm.at[table], table_ref.at[table], sems.at[5 + table])
-        )
+    for table in range(tables):
+        to = table_ref.at[:, table * channels : (table + 1) * channels]
+        copies.append(pltpu.make_async_copy(table_hbm.at[table], to, sems.at[5 + table]))
     for copy in copies:
         copy.start()
     for copy in copies[:4]:
         copy.wait()
-    scal_ref[0:slots, :] = window_rows(cover[...], here(), local_blocks, slab)
-    scal_ref[slots : 2 * slots, :] = offset[...]
-    scal_ref[2 * slots : 2 * slots + 1, :] = count[...]
-    scal_ref[2 * slots + 1 : 2 * slots + 2, :] = angle[...]
-    load = fetch(scal_ref, scal, sems.at[0])
+    index[0:slots, :] = window_rows(cover[...], here(), local_blocks, slab)
+    index[slots : 2 * slots, :] = offset[...]
+    index[2 * slots : 2 * slots + 1, :] = count[...]
+    index[2 * slots + 1 : 2 * slots + 2, :] = angle[...]
+    load = fetch(index, scal, sems.at[0])
     copies[4].wait()
 
     def fade(view, carry):
@@ -193,45 +209,42 @@
         return carry
 
     lax.fori_loop(0, views, fade, 0)
-    for table in range(table_ref.shape[0]):
+    load.wait()
+    list_pairs(scal, lists, 2 * piece, det_rows)
+    save = fetch(lists, lists_ref, sems.at[0])
+    for table in range(tables):
         copies[5 + table].wait()
-        turned_ref[table] = table_ref[table].T
-        proj[table * piece : (table + 1) * piece, :] = jnp.dot(
-            both_ref[0:piece, :], table_ref[table], preferred_element_type=jnp.float32
-        )
-    load.wait()
-    place(Scalars(scal), sino_ref, proj, 4 * piece, piece, slab)
-
-
-def project_into(sino_ref, begun_ref, scal, load, proj, pieces, table_ref, first_row, slab):
-    rows = sum(piece.shape[0] for piece in pieces)
-    sino_ref[...] = begun_ref[...]
-    window = pieces[0] if len(pieces) == 1 else jnp.concatenate(pieces, axis=0)
-    for table in range(table_ref.shape[0]):
-        proj[table * rows : (table + 1) * rows, :] = jnp.dot(
-            window, table_ref[table], preferred_element_type=jnp.float32
-        )
-    load.wait()
-    place(scal, sino_ref, proj, first_row, rows, slab)
-
-
-def fetch(scal_ref, scal, sem):
-    load = pltpu.make_async_copy(scal_ref, scal, sem)
+        cols = slice(table * channels, (table + 1) * channels)
+        turned_ref[cols, :] = table_ref[:, cols].T
+    proj[...] = jnp.dot(both_ref[0:piece, :], table_ref[...], preferred_element_type=jnp.float32)
+    place(Pairs(lists), 2, sino_ref, proj, 4 * piece, slab)
+    save.wait()
+
+
+def fetch(source, target, sem):
+    load = pltpu.make_async_copy(source, target, sem)
     load.start()
     return load
 
 
+def project(load, lists, group, long_ref, short_ref, table_ref, begun_ref, sino_ref, proj, slab):
+    piece = long_ref.shape[0] - 8
+    sino_ref[...] = begun_ref[...]
+    window = jnp.concatenate([long_ref[0:piece, :], short_ref[0:piece, :]], axis=0)
+    proj[...] = jnp.dot(window, table_ref[...], preferred_element_type=jnp.float32)
+    load.wait()
+    place(Pairs(lists), group, sino_ref, proj, group * 2 * piece, slab)
+
+
 def middle_kernel(
-    scal_ref, long_ref, short_ref, table_ref, begun_ref, sino_ref, scal, proj, sem, *, slab
+    lists_ref, long_ref, short_ref, table_ref, begun_ref, sino_ref, lists, proj, sem, *, slab
 ):
-    load = fetch(scal_ref, scal, sem)
-    piece = long_ref.shape[0] - 8
-    pieces = [long_ref[0:piece, :], short_ref[0:piece, :]]
-    project_into(sino_ref, begun_ref, Scalars(scal), load, proj, pieces, table_ref, 0, slab)
+    load = fetch(lists_ref, lists, sem)
+    project(load, lists, 0, long_ref, short_ref, table_ref, begun_ref, sino_ref, proj, slab)
 
 
 def main_kernel(
-    scal_ref,
+    lists_ref,
     long_ref,
     short_ref,
     table_ref,
@@ -240,32 +253,28 @@
     decay_ref,
     sino_ref,
     give_ref,
-    scal,
+    lists,
     proj,
     sums,
     sem,
     *,
     slab,
 ):
-    load = fetch(scal_ref, scal, sem)
-    piece = long_ref.shape[0] - 8
+    load = fetch(lists_ref, lists, sem)
     sums[...] = jnp.zeros_like(sums)
-    index = Scalars(scal)
-    pieces = [long_ref[0:piece, :], short_ref[0:piece, :]]
-    project_into(sino_ref, begun_ref, index, load, proj, pieces, table_ref, 2 * piece, slab)
-    gather(index, sino_ref, decay_ref, sums, 2 * piece, 2 * piece, slab)
-    give_ref[...] = back_project(sums, turned_ref, 2 * piece)
+    project(load, lists, 1, long_ref, short_ref, table_ref, begun_ref, sino_ref, proj, slab)
+    gather(Pairs(lists), 1, sino_ref, decay_ref, sums, sums.shape[0], slab)
+    give_ref[...] = back_project(sums, turned_ref)
 
 
 def rest_kernel(
-    scal_ref, turned_ref, sino_ref, decay_ref, out_ref, scal, sums, sem, *, first_row, slab
+    lists_ref, turned_ref, sino_ref, decay_ref, out_ref, lists, sums, sem, *, group, first_row, slab
 ):
-    load = fetch(scal_ref, scal, sem)
+    load = fetch(lists_ref, lists, sem)
     sums[...] = jnp.zeros_like(sums)
-    rows = out_ref.shape[0]
     load.wait()
-    gather(Scalars(scal), sino_ref, decay_ref, sums, first_row, rows, slab)
-    out_ref[...] = back_project(sums, turned_ref, rows)
+    gather(Pairs(lists), group, sino_ref, decay_ref, sums, first_row, slab)
+    out_ref[...] = back_project(sums, turned_ref)
 
 
 def prior_kernel(
@@ -385,13 +394,13 @@
     got_long = send(both, long)
 
     sino_shape = shape((channels // 128, views * det_rows, 128), jnp.float32)
-    scal_shape = (2 * slots + 2, views)
-    table_vmem, turned, scalars, sino, decay = pl.pallas_call(
+    lists_shape = (10, views * slots)
+    table_vmem, turned, lists, sino, decay = pl.pallas_call(
         functools.partial(early_kernel, local_blocks=local_blocks, slab=slab, here=here),
         out_shape=(
-            shape(table.shape, table.dtype),
-            shape((tables, channels, plane), table.dtype),
-            shape(scal_shape, jnp.int32),
+            shape((plane, tables * channels), table.dtype),
+            shape((tables * channels, plane), table.dtype),
+            shape(lists_shape, jnp.int32),
             sino_shape,
             sino_shape,
         ),
@@ -403,8 +412,10 @@
             pltpu.VMEM((slots, views), jnp.int32),
             pltpu.VMEM((1, views), jnp.int32),
             pltpu.VMEM((1, views), jnp.int32),
-            pltpu.SMEM(scal_shape, jnp.int32),
-            pltpu.VMEM((tables * piece, channels), jnp.float32),
+            pltpu.VMEM((2 * slots + 2, views), jnp.int32),
+            pltpu.SMEM((2 * slots + 2, views), jnp.int32),
+            pltpu.SMEM(lists_shape, jnp.int32),
+            pltpu.VMEM((piece, tables * channels), jnp.float32),
             pltpu.SemaphoreType.DMA((5 + tables,)),
         ],
         compiler_params=room(16),
@@ -419,63 +430,62 @@
         stay(count.reshape(1, views)),
         stay(angle_index.reshape(1, views)),
     )
-    got_short, got_long, table_vmem, turned, scalars, sino, decay = lax.optimization_barrier(
-        (got_short, got_long, table_vmem, turned, scalars, sino, decay)
+    got_short, got_long, table_vmem, turned, lists, sino, decay = lax.optimization_barrier(
+        (got_short, got_long, table_vmem, turned, lists, sino, decay)
     )
-    index = [pltpu.SMEM(scal_shape, jnp.int32)]
+    index = [pltpu.SMEM(lists_shape, jnp.int32)]
     waits = [pltpu.SemaphoreType.DMA]
-    proj = lambda rows: [pltpu.VMEM((tables * rows, channels), jnp.float32)]
-    sums = lambda rows: [pltpu.VMEM((tables * rows, channels), jnp.float32)]
-
-    far_short = send(got_short, swap)
-    far_long = send(got_long, swap)
+    rows_of = lambda rows: [pltpu.VMEM((rows, tables * channels), jnp.float32)]
+
+    far = send(jnp.concatenate([got_long, got_short], axis=0), swap)
+    far_long, far_short = far[: piece + 8], far[piece + 8 :]
     sino = pl.pallas_call(
         functools.partial(middle_kernel, slab=slab),
         out_shape=sino_shape,
         in_specs=[vmem] * 5,
         out_specs=vmem,
-        scratch_shapes=index + proj(2 * piece) + waits,
+        scratch_shapes=index + rows_of(2 * piece) + waits,
         compiler_params=room(16),
         cost_estimate=cost(1, 1),
         name="middle",
-    )(scalars, got_long, got_short, table_vmem, sino)
+    )(lists, got_long, got_short, table_vmem, sino)
     far_short, far_long, sino = lax.optimization_barrier((far_short, far_long, sino))
     sino, give = pl.pallas_call(
         functools.partial(main_kernel, slab=slab),
         out_shape=(sino_shape, shape((2 * piece, plane), jnp.float32)),
         in_specs=[vmem] * 7,
         out_specs=(vmem, vmem),
-        scratch_shapes=index + proj(2 * piece) + sums(2 * piece) + waits,
+        scratch_shapes=index + rows_of(2 * piece) + rows_of(2 * piece) + waits,
         compiler_params=room(16),
         cost_estimate=cost(1, 1),
         name="main",
-    )(scalars, far_long, far_short, table_vmem, turned, sino, decay)
+    )(lists, far_long, far_short, table_vmem, turned, sino, decay)
     taken = send(give, swap)
     keep = pl.pallas_call(
-        functools.partial(rest_kernel, first_row=0, slab=slab),
+        functools.partial(rest_kernel, group=0, first_row=0, slab=slab),
         out_shape=shape((2 * piece, plane), jnp.float32),
         in_specs=[vmem] * 4,
         out_specs=vmem,
-        scratch_shapes=index + sums(2 * piece) + waits,
+        scratch_shapes=index + rows_of(2 * piece) + waits,
         compiler_params=room(16),
         cost_estimate=cost(1, 1),
         name="rest",
-    )(scalars, turned, sino, decay)
+    )(lists, turned, sino, decay)
     taken, keep = lax.optimization_barrier((taken, keep))
     wire = (keep + taken).astype(jnp.bfloat16)
     back_short = send(wire[piece:], short)
     back_long = send(wire[:piece], long)
 
     home = pl.pallas_call(
-        functools.partial(rest_kernel, first_row=4 * piece, slab=slab),
+        functools.partial(rest_kernel, group=2, first_row=4 * piece, slab=slab),
         out_shape=shape((piece, plane), jnp.float32),
         in_specs=[vmem] * 4,
         out_specs=vmem,
-        scratch_shapes=index + sums(piece) + waits,
+        scratch_shapes=index + rows_of(piece) + waits,
         compiler_params=room(16),
         cost_estimate=cost(1, 1),
         name="home",
-    )(scalars, turned, sino, decay)
+    )(lists, turned, sino, decay)
     prior = pl.pallas_call(
         functools.partial(prior_kernel, devices=devices, here=here),
         out_shape=shape((part, plane), jnp.float32),

time: 31.3 us -> 30.2 us (0.965)
  Pallas kernels: 14.2 us -> 12.5 us
  waiting for transfers between devices: 5.85 us -> 6.92 us
  starting transfers between devices: 10.8 us -> 10.4 us
    ppermute x9 -> x8, waiting for transfers between devices: 5.85 us -> 6.92 us  [shards(): send = lambda value, pairs: lax.ppermute(value, AXES, pairs)]
    pallas_call x2, Pallas kernels: 4.21 us -> 3.45 us  [the longest x1 2 us: shards(): pl.pallas_call(functools.partial(rest_kernel, group=0, first_row=0, slab=...]
    pallas_call x1, Pallas kernels: 3.04 us -> 2.48 us  [shards(): pl.pallas_call(functools.partial(main_kernel, slab=slab), out_shape=(sino...]
    pallas_call x1, Pallas kernels: 1.25 us -> 0.83 us  [shards(): pl.pallas_call(functools.partial(middle_kernel, slab=slab), out_shape=sin...]
    ppermute x9 -> x8, starting transfers between devices: 10.8 us -> 10.4 us  [shards(): send = lambda value, pairs: lax.ppermute(value, AXES, pairs)]
  transfers between devices with their start and end apart: 9 -> 8, of which waited for: 6 -> 6; matrix products, arithmetic and copies ran while one was open for 0% -> 0% of each run, Pallas kernels for 33% -> 30%
where the time goes in v4:
time: 30.2 us; the launch traced here: 30.1 us
  Pallas kernels  12.5 us (41%)
  starting transfers between devices  10.4 us (34%)
  waiting for transfers between devices  6.92 us (23%)
    ppermute x8, starting transfers between devices, shards(): send = lambda value, pairs: lax.ppermute(value, AXES, pairs)  10.4 us
    ppermute x8, waiting for transfers between devices, shards(): send = lambda value, pairs: lax.ppermute(value, AXES, pairs)  6.92 us
    pallas_call x1, Pallas kernels, shards(): pl.pallas_call(functools.partial(early_kernel, local_blocks=local_blocks,...  3.62 us
    pallas_call x1, Pallas kernels, shards(): pl.pallas_call(functools.partial(main_kernel, slab=slab), out_shape=(sino...  2.48 us
    pallas_call x1, Pallas kernels, shards(): pl.pallas_call(functools.partial(rest_kernel, group=0, first_row=0, slab=...  2 us
    pallas_call x1, Pallas kernels, shards(): pl.pallas_call(functools.partial(rest_kernel, group=2, first_row=4 * piec...  1.44 us
    pallas_call x1, Pallas kernels, shards(): pl.pallas_call(load_kernel, out_shape=shape(flat.shape, flat.dtype), in_s...  0.91 us
    pallas_call x1, Pallas kernels, shards(): pl.pallas_call(functools.partial(middle_kernel, slab=slab), out_shape=sin...  0.83 us
  transfers between devices with their start and end apart: 8, of which 6 were waited for; matrix products, arithmetic and copies ran while one was open for 0% of the time, Pallas kernels for 30%

profile of v4, /device:TPU:3, one launch (start us, length us, event | category | flops | bytes accessed | tf_op | source)
XLA Modules:
  0.0 30.1 jit_solution(12606686914961368680)
XLA Ops:
  0.0 0.7 %collective-permute-start = (f32[32,2,512]{2,1,0:T(2,128)}, f32[32,2,512]{2,1,0:T(2,128)S(1)}, u32[]{:S(2)}, u32[]{:S(2)}) collective-permute-start(f32[32,2,512]{2,1,0:T(2,128)} %bitcast.8), channel_id=1, source_target_pairs={{0,1},{1,0},{2,3},{3,2},{4,5},{5,4},{6,7},{7,6},{8,9},{9,8},{10,11... | collective-permute-start | bytes 393224 | tf_op jit(solution)/shard_map/ppermute | solution.py:358
  0.7 0.9 %load.1.own_ref.vol_ref = f32[32,2,512]{2,1,0:T(2,128)S(1)} custom-call(f32[32,2,512]{2,1,0:T(2,128)} %bitcast.9), custom_call_target="tpu_custom_call" | custom-call | flops 1 | bytes 1 | tf_op jit(solution)/shard_map/load/pallas_call | solution.py:374
  1.6 0.3 collective-permute-done.other_ref
  1.9 0.3 %join.1.both_ref = bf16[72,1024]{1,0:T(8,128)(2,1)S(1)} custom-call(f32[32,2,512]{2,1,0:T(2,128)S(1)} %load.1.own_ref.vol_ref, f32[32,2,512]{2,1,0:T(2,128)S(1)} %collective-permute-done.other_ref), custom_call_target="tpu_custom_call" | custom-call | tf_op jit(solution)/shard_map/join/pallas_call | solution.py:385
  2.2 4.3 %collective-permute-start.2 = (bf16[72,1024]{1,0:T(8,128)(2,1)S(1)}, bf16[72,1024]{1,0:T(8,128)(2,1)S(1)}, u32[]{:S(2)}, u32[]{:S(2)}) collective-permute-start(bf16[72,1024]{1,0:T(8,128)(2,1)S(1)} %join.1.both_ref), channel_id=1, source_target_pairs={{4,8},{6,10},{12,16},{14,18},{20,24},{22,26},{3,5},{7,9},{11,13},{... | collective-permute-start | bytes 442376 | tf_op jit(solution)/shard_map/ppermute | solution.py:358
  6.5 0.0 collective-permute-start.1
  6.5 3.6 %early.1 = (bf16[1024,1792]{1,0:T(8,128)(2,1)S(1)}, bf16[1792,1024]{1,0:T(8,128)(2,1)S(1)}, s32[10,32]{1,0:T(8,128)S(1)}, f32[7,512,128]{2,1,0:T(8,128)S(1)}, f32[7,512,128]{2,1,0:T(8,128)S(1)}) custom-call(bf16[72,1024]{1,0:T(8,128)(2,1)S(1)} %join.1.both_ref, bf16[2,1024,896]{2,1,0:T(8,128)(2,1)} %bitcast.7, bf16[8,64,896]{2,1,0:T(8,128)(2,1)} %measured_hbm.1, ...), custom_call_target="tpu_custom_call" | custom-call | flops 1 | bytes 1 | tf_op jit(solution)/shard_map/early/pallas_call | solution.py:398
  10.1 0.6 %collective-permute-done.2.long_ref = bf16[72,1024]{1,0:T(8,128)(2,1)S(1)} collective-permute-done((bf16[72,1024]{1,0:T(8,128)(2,1)S(1)}, bf16[72,1024]{1,0:T(8,128)(2,1)S(1)}, u32[]{:S(2)}, u32[]{:S(2)}) %collective-permute-start.2) | collective-permute-done | bytes 147488 | tf_op jit(solution)/shard_map/ppermute | solution.py:358
  10.7 0.9 %collective-permute-done.1.short_ref = bf16[72,1024]{1,0:T(8,128)(2,1)S(1)} collective-permute-done((bf16[72,1024]{1,0:T(8,128)(2,1)S(1)}, bf16[72,1024]{1,0:T(8,128)(2,1)S(1)}, u32[]{:S(2)}, u32[]{:S(2)}) %collective-permute-start.1) | collective-permute-done | bytes 147488 | tf_op jit(solution)/shard_map/ppermute | solution.py:358
  11.6 0.7 %collective-permute-start.3 = (bf16[144,1024]{1,0:T(8,128)(2,1)S(1)}, bf16[144,1024]{1,0:T(8,128)(2,1)S(1)}, u32[]{:S(2)}, u32[]{:S(2)}) collective-permute-start(bf16[144,1024]{1,0:T(8,128)(2,1)S(1)} %pad_maximum_fusion), channel_id=1, source_target_pairs={{0,1},{1,0},{2,3},{3,2},{4,5},{5,4},{6,7},{7,6},{8,9},{9,8},{10,11... | collective-permute-start | bytes 884744 | tf_op jit(solution)/shard_map/ppermute | solution.py:358
  12.3 0.8 %middle.1.begun_ref = f32[7,512,128]{2,1,0:T(8,128)S(1)} custom-call(s32[10,32]{1,0:T(8,128)S(1)} %get-tuple-element.37.lists_ref, bf16[72,1024]{1,0:T(8,128)(2,1)S(1)} %collective-permute-done.2.long_ref, bf16[72,1024]{1,0:T(8,128)(2,1)S(1)} %collective-permute-done.1.short_ref, bf16[1024,1792]{1,0:T(8,128)(2,1)S(1)} %get-tuple-element.40.table_ref, ...), custom_call_target="tpu_custom_call" | custom-call | flops 1 | bytes 1 | tf_op jit(solution)/shard_map/middle/pallas_call | solution.py:442
  13.2 0.4 %collective-permute-done.3 = bf16[144,1024]{1,0:T(8,128)(2,1)S(1)} collective-permute-done((bf16[144,1024]{1,0:T(8,128)(2,1)S(1)}, bf16[144,1024]{1,0:T(8,128)(2,1)S(1)}, u32[]{:S(2)}, u32[]{:S(2)}) %collective-permute-start.3) | collective-permute-done | bytes 294944 | tf_op jit(solution)/shard_map/ppermute | solution.py:358
  13.6 2.5 %main.1 = (f32[7,512,128]{2,1,0:T(8,128)S(1)}, f32[128,1024]{1,0:T(8,128)S(1)}) custom-call(s32[10,32]{1,0:T(8,128)S(1)} %get-tuple-element.37.lists_ref, bf16[72,1024]{1,0:T(8,128)(2,1)S(1)} %get-tuple-element.42.long_ref.far_long_ref, bf16[72,1024]{1,0:T(8,128)(2,1)S(1)} %get-tuple-element.43.short_ref.far_short_ref, ...), custom_call_target="tpu_custom_call" | custom-call | flops 1 | bytes 1 | tf_op jit(solution)/shard_map/main/pallas_call | solution.py:453
  16.1 0.5 %collective-permute-start.4 = (f32[128,1024]{1,0:T(8,128)S(1)}, f32[128,1024]{1,0:T(8,128)S(1)}, u32[]{:S(2)}, u32[]{:S(2)}) collective-permute-start(f32[128,1024]{1,0:T(8,128)S(1)} %get-tuple-element.47), channel_id=1, source_target_pairs={{0,1},{1,0},{2,3},{3,2},{4,5},{5,4},{6,7},{7,6},{8,9},{9,8},{10,11... | collective-permute-start | bytes 1572872 | tf_op jit(solution)/shard_map/ppermute | solution.py:358
  16.6 2.0 %rest.1 = f32[128,1024]{1,0:T(8,128)S(1)} custom-call(s32[10,32]{1,0:T(8,128)S(1)} %get-tuple-element.37.lists_ref, bf16[1792,1024]{1,0:T(8,128)(2,1)S(1)} %get-tuple-element.44.turned_ref, f32[7,512,128]{2,1,0:T(8,128)S(1)} %get-tuple-element.48.sino_ref, f32[7,512,128]{2,1,0:T(8,128)S(1)} %get-tuple-element.46.decay_ref), custom_call_target="tpu_custom_call" | custom-call | flops 1 | bytes 1 | tf_op jit(solution)/shard_map/rest/pallas_call | solution.py:464
  18.6 0.0 collective-permute-done.4
  18.6 0.1 add_convert_fusion
  18.7 3.3 %collective-permute-start.6 = (bf16[64,1024]{1,0:T(8,128)(2,1)S(1)}, bf16[64,1024]{1,0:T(8,128)(2,1)S(1)}, u32[]{:S(2)}, u32[]{:S(2)}) collective-permute-start(bf16[64,1024]{1,0:T(8,128)(2,1)S(1)} %get-tuple-element.59), channel_id=1, source_target_pairs={{4,8},{6,10},{12,16},{14,18},{20,24},{22,26},{3,5},{7,9},{11,13},{... | collective-permute-start | bytes 393224 | tf_op jit(solution)/shard_map/ppermute | solution.py:358
  22.0 0.0 collective-permute-start.5
  22.0 0.2 prior.1.prior_ref
  22.2 1.4 %home.1 = f32[64,1024]{1,0:T(8,128)S(1)} custom-call(s32[10,32]{1,0:T(8,128)S(1)} %get-tuple-element.37.lists_ref, bf16[1792,1024]{1,0:T(8,128)(2,1)S(1)} %get-tuple-element.44.turned_ref, f32[7,512,128]{2,1,0:T(8,128)S(1)} %get-tuple-element.48.sino_ref, f32[7,512,128]{2,1,0:T(8,128)S(1)} %get-tuple-element.46.decay_ref), custom_call_target="tpu_custom_call" | custom-call | flops 1 | bytes 1 | tf_op jit(solution)/shard_map/home/pallas_call | solution.py:479
  23.6 3.8 %collective-permute-done.6 = bf16[64,1024]{1,0:T(8,128)(2,1)S(1)} collective-permute-done((bf16[64,1024]{1,0:T(8,128)(2,1)S(1)}, bf16[64,1024]{1,0:T(8,128)(2,1)S(1)}, u32[]{:S(2)}, u32[]{:S(2)}) %collective-permute-start.6) | collective-permute-done | bytes 131104 | tf_op jit(solution)/shard_map/ppermute | solution.py:358
  27.4 0.0 collective-permute-done.5
  27.5 0.9 %collective-permute-start.7 = (f32[32,1024]{1,0:T(8,128)S(1)}, f32[32,1024]{1,0:T(8,128)S(1)}, u32[]{:S(2)}, u32[]{:S(2)}) collective-permute-start(f32[32,1024]{1,0:T(8,128)S(1)} %get-tuple-element.57), channel_id=1, source_target_pairs={{0,1},{1,0},{2,3},{3,2},{4,5},{5,4},{6,7},{7,6},{8,9},{9,8},{10,11... | collective-permute-start | bytes 393224 | tf_op jit(solution)/shard_map/ppermute | solution.py:358
  28.4 1.0 %collective-permute-done.7.passed_ref = f32[32,1024]{1,0:T(8,128)S(1)} collective-permute-done((f32[32,1024]{1,0:T(8,128)S(1)}, f32[32,1024]{1,0:T(8,128)S(1)}, u32[]{:S(2)}, u32[]{:S(2)}) %collective-permute-start.7) | collective-permute-done | bytes 131104 | tf_op jit(solution)/shard_map/ppermute | solution.py:358
  29.4 0.7 %last.1 = f32[32,2,512]{2,1,0:T(2,128)} custom-call(f32[32,1024]{1,0:T(8,128)S(1)} %get-tuple-element.58.arrived_ref, f32[32,1024]{1,0:T(8,128)S(1)} %collective-permute-done.7.passed_ref, f32[32,1024]{1,0:T(8,128)S(1)} %prior.1.prior_ref), custom_call_target="tpu_custom_call" | custom-call | tf_op jit(solution)/shard_map/last/pallas_call | solution.py:504
  (5 shorter events, 0.1 us)
Async XLA Ops:
  0.0 1.9 %collective-permute-start = (f32[32,2,512]{2,1,0:T(2,128)}, f32[32,2,512]{2,1,0:T(2,128)S(1)}, u32[]{:S(2)}, u32[]{:S(2)}) collective-permute-start(f32[32,2,512]{2,1,0:T(2,128)} %bitcast.8), channel_id=1, source_target_pairs={{0,1},{1,0},{2,3},{3,2},{4,5},{5,4},{6,7},{7,6},{8,9},{9,8},{10,11... | collective-permute-start | bytes 393224 | tf_op jit(solution)/shard_map/ppermute | solution.py:358
  2.2 8.5 %collective-permute-start.2 = (bf16[72,1024]{1,0:T(8,128)(2,1)S(1)}, bf16[72,1024]{1,0:T(8,128)(2,1)S(1)}, u32[]{:S(2)}, u32[]{:S(2)}) collective-permute-start(bf16[72,1024]{1,0:T(8,128)(2,1)S(1)} %join.1.both_ref), channel_id=1, source_target_pairs={{4,8},{6,10},{12,16},{14,18},{20,24},{22,26},{3,5},{7,9},{11,13},{... | collective-permute-start | bytes 442376 | tf_op jit(solution)/shard_map/ppermute | solution.py:358
  6.5 5.1 %collective-permute-start.1 = (bf16[72,1024]{1,0:T(8,128)(2,1)S(1)}, bf16[72,1024]{1,0:T(8,128)(2,1)S(1)}, u32[]{:S(2)}, u32[]{:S(2)}) collective-permute-start(bf16[72,1024]{1,0:T(8,128)(2,1)S(1)} %join.1.both_ref), channel_id=1, source_target_pairs={{0,2},{4,6},{8,10},{12,14},{16,18},{20,22},{24,26},{28,30},{1,5},{... | collective-permute-start | bytes 442376 | tf_op jit(solution)/shard_map/ppermute | solution.py:358
  11.6 1.9 %collective-permute-start.3 = (bf16[144,1024]{1,0:T(8,128)(2,1)S(1)}, bf16[144,1024]{1,0:T(8,128)(2,1)S(1)}, u32[]{:S(2)}, u32[]{:S(2)}) collective-permute-start(bf16[144,1024]{1,0:T(8,128)(2,1)S(1)} %pad_maximum_fusion), channel_id=1, source_target_pairs={{0,1},{1,0},{2,3},{3,2},{4,5},{5,4},{6,7},{7,6},{8,9},{9,8},{10,11... | collective-permute-start | bytes 884744 | tf_op jit(solution)/shard_map/ppermute | solution.py:358
  16.1 2.5 %collective-permute-start.4 = (f32[128,1024]{1,0:T(8,128)S(1)}, f32[128,1024]{1,0:T(8,128)S(1)}, u32[]{:S(2)}, u32[]{:S(2)}) collective-permute-start(f32[128,1024]{1,0:T(8,128)S(1)} %get-tuple-element.47), channel_id=1, source_target_pairs={{0,1},{1,0},{2,3},{3,2},{4,5},{5,4},{6,7},{7,6},{8,9},{9,8},{10,11... | collective-permute-start | bytes 1572872 | tf_op jit(solution)/shard_map/ppermute | solution.py:358
  18.7 8.7 %collective-permute-start.6 = (bf16[64,1024]{1,0:T(8,128)(2,1)S(1)}, bf16[64,1024]{1,0:T(8,128)(2,1)S(1)}, u32[]{:S(2)}, u32[]{:S(2)}) collective-permute-start(bf16[64,1024]{1,0:T(8,128)(2,1)S(1)} %get-tuple-element.59), channel_id=1, source_target_pairs={{4,8},{6,10},{12,16},{14,18},{20,24},{22,26},{3,5},{7,9},{11,13},{... | collective-permute-start | bytes 393224 | tf_op jit(solution)/shard_map/ppermute | solution.py:358
  22.0 5.5 %collective-permute-start.5 = (bf16[64,1024]{1,0:T(8,128)(2,1)S(1)}, bf16[64,1024]{1,0:T(8,128)(2,1)S(1)}, u32[]{:S(2)}, u32[]{:S(2)}) collective-permute-start(bf16[64,1024]{1,0:T(8,128)(2,1)S(1)} %get-tuple-element.60), channel_id=1, source_target_pairs={{0,2},{4,6},{8,10},{12,14},{16,18},{20,22},{24,26},{28,30},{1,5},{... | collective-permute-start | bytes 393224 | tf_op jit(solution)/shard_map/ppermute | solution.py:358
  27.5 1.9 %collective-permute-start.7 = (f32[32,1024]{1,0:T(8,128)S(1)}, f32[32,1024]{1,0:T(8,128)S(1)}, u32[]{:S(2)}, u32[]{:S(2)}) collective-permute-start(f32[32,1024]{1,0:T(8,128)S(1)} %get-tuple-element.57), channel_id=1, source_target_pairs={{0,1},{1,0},{2,3},{3,2},{4,5},{5,4},{6,7},{7,6},{8,9},{9,8},{10,11... | collective-permute-start | bytes 393224 | tf_op jit(solution)/shard_map/ppermute | solution.py:358

commit v5 on v4

--- a/solution.py
+++ b/solution.py
@@ -8,6 +8,7 @@
 from jax.sharding import PartitionSpec as P
 
 AXES = ("grp", "view")
+APART = 4
 DELTA = 0.5
 PRIOR_WEIGHT = 2.0
 
@@ -23,12 +24,13 @@
     edge_d = [(i, i + 1) for i in range(1, chips - 1, 2)]
     edge_a = [(i + j, i + j + 2) for i in range(0, chips, 4) for j in (0, 1)]
     edge_b = [(i + j, i + j + 2) for i in range(2, chips - 2, 4) for j in (0, 1)]
+    idle = [(0, 1), (chips - 2, chips - 1)]
     on_core = lambda edges, core: [(2 * a + core, 2 * b + core) for a, b in edges]
     last = devices - 1
-    ends = [(0, 1), (1, 2), (2, 0), (last, last - 1), (last - 1, last - 3), (last - 3, last)]
-    long = both_ways(on_core(edge_b, 0) + on_core(edge_d, 1)) + ends
-    short = both_ways(on_core(edge_y, 0) + on_core(edge_a, 1))
-    return swap, long, short
+    ends = [(0, 4), (4, 1), (1, 0), (last - 1, last - 5), (last - 5, last), (last, last - 1)]
+    first = both_ways(on_core(edge_a[1:-1], 0) + on_core(edge_d, 1)) + ends
+    second = both_ways(on_core(edge_b + idle, 0) + on_core(edge_y, 1))
+    return swap, first, second
 
 
 def load_kernel(source, target, sem):
@@ -55,7 +57,7 @@
         out_ref[2 * slices : 2 * slices + 8, cols] = spare
 
 
-def window_rows(block, position, local_blocks, slab):
+def window_rows(block, position, chips, local_blocks, slab):
     part = local_blocks * slab
     piece = 2 * part
     core = lax.rem(position, 2)
@@ -68,58 +70,84 @@
     nearer = jnp.abs(delta) == 1
     is_y = flag(up == 1 - lax.rem(chip, 2))
     is_a = flag(up == flag(lax.rem(chip, 4) < 2))
-    short = jnp.where(nearer, is_y, is_a)
-    via = jnp.where(nearer, 1 - is_y, is_a)
-    away = (2 * jnp.abs(via - core) + short) * piece + jnp.abs(owner_core - via) * part
+    second = jnp.where(nearer, is_y, 1 - is_a)
+    via = flag(nearer)
+    end = flag((chip == 0) | (chip == chips - 1))
+    held = jnp.where(nearer, 1, is_a * end)
+    away = (2 * jnp.abs(held - core) + second) * piece + jnp.abs(owner_core - via) * part
     here = 4 * piece + jnp.abs(owner_core - core) * part
     return jnp.where(delta == 0, here, away) + lax.rem(block, local_blocks) * slab
 
 
 class Pairs:
+    FIELDS = 5
+    GROUPS = 3
+
     def __init__(self, ref):
         self.ref = ref
 
     def each(self, group, do):
         def body(i, carry):
-            do(*(self.ref[3 * group + k, i] for k in range(3)))
+            do(*(self.ref[self.FIELDS * group + k, i] for k in range(4)))
             return carry
 
-        lax.fori_loop(0, self.ref[9, group], body, 0)
-
-
-def list_pairs(scal, lists, near_rows, det_rows):
+        lax.fori_loop(0, self.ref[self.FIELDS * self.GROUPS, group], body, 0)
+
+    def apart(self, group):
+        return self.ref[self.FIELDS * self.GROUPS + 1, group]
+
+    def target(self, group, i):
+        return self.ref[self.FIELDS * group + 4, i]
+
+
+def list_pairs(scal, lists, seen, near_rows, det_rows, tables, slab):
     slots = (scal.shape[0] - 2) // 2
-
-    def body(view, used):
+    fields, groups = Pairs.FIELDS, Pairs.GROUPS
+
+    def clear(i, carry):
+        seen[i] = jnp.int32(0)
+        return carry
+
+    lax.fori_loop(0, seen.shape[0], clear, 0)
+    for k in range(groups):
+        lists[fields * groups, k] = jnp.int32(0)
+        lists[fields * groups + 1, k] = jnp.int32(0)
+
+    def body(view, carry):
         count = scal[2 * slots, view]
         table = scal[2 * slots + 1, view]
         for slot in range(slots):
-            row = scal[slot, view]
-            group = jnp.minimum(row // near_rows, 2)
-            at = jnp.where(group == 0, used[0], jnp.where(group == 1, used[1], used[2]))
 
             @pl.when(slot < count)
             def _():
-                lists[3 * group, at] = view * det_rows + scal[slots + slot, view]
-                lists[3 * group + 1, at] = table
-                lists[3 * group + 2, at] = row
-
-            used = tuple(
-                n + jnp.where((group == k) & (slot < count), 1, 0) for k, n in enumerate(used)
-            )
-        return used
-
-    zero = jnp.int32(0)
-    used = lax.fori_loop(0, scal.shape[1], body, (zero, zero, zero))
-    for k, n in enumerate(used):
-        lists[9, k] = n
-
-
-def place(pairs, group, sino, proj, first_row, slab):
+                row = scal[slot, view]
+                group = jnp.minimum(row // near_rows, groups - 1)
+                local = row - group * near_rows
+                at = lists[fields * groups, group]
+                spare = lists[fields * groups + 1, group]
+                first = fields * group
+                bucket = (row // slab) * tables + table
+                taken = seen[bucket]
+                rows = jnp.where(group == groups - 1, near_rows // 2, near_rows)
+                lists[first, at] = view * det_rows + scal[slots + slot, view]
+                lists[first + 1, at] = table
+                lists[first + 2, at] = local
+                lists[first + 3, at] = jnp.where(taken == 0, local, rows + spare * slab)
+                lists[first + 4, spare] = local
+                lists[fields * groups, group] = at + 1
+                lists[fields * groups + 1, group] = spare + taken
+                seen[bucket] = jnp.int32(1)
+
+        return carry
+
+    lax.fori_loop(0, scal.shape[1], body, 0)
+
+
+def place(pairs, group, sino, proj, slab):
     width = sino.shape[0] * 128
 
-    def add(target, table, row):
-        source = pl.ds(pl.multiple_of(row - first_row, slab), slab)
+    def add(target, table, local, dest):
+        source = pl.ds(pl.multiple_of(local, slab), slab)
         for tile in range(sino.shape[0]):
             cols = pl.ds(pl.multiple_of(table * width + tile * 128, 128), 128)
             sino[tile, pl.ds(target, slab), :] += proj[source, cols]
@@ -127,28 +155,55 @@
     pairs.each(group, add)
 
 
-def gather(pairs, group, sino, decay, sums, first_row, slab):
+def clear_rows(picked, rows):
+    picked[0:rows, :] = jnp.zeros((rows, picked.shape[1]), picked.dtype)
+
+
+def gather(pairs, group, sino, decay, picked, static_rows, slab):
     width = sino.shape[0] * 128
-
-    def add(source, table, row):
-        target = pl.ds(pl.multiple_of(row - first_row, slab), slab)
+    chunk = APART * slab
+
+    def clear(i, carry):
+        here = pl.ds(pl.multiple_of(static_rows + i * chunk, chunk), chunk)
+        picked[here, :] = jnp.zeros((chunk, picked.shape[1]), picked.dtype)
+        return carry
+
+    lax.fori_loop(0, (pairs.apart(group) - 1) // APART, clear, 0)
+
+    def take(source, table, local, dest):
+        target = pl.ds(pl.multiple_of(dest, slab), slab)
         here = pl.ds(source, slab)
         for tile in range(sino.shape[0]):
             cols = pl.ds(pl.multiple_of(table * width + tile * 128, 128), 128)
-            value = (decay[tile, here, :] * sino[tile, here, :]).astype(jnp.bfloat16)
-            sums[target, cols] += value.astype(jnp.float32)
-
-    pairs.each(group, add)
-
-
-def back_project(sums, turned_ref):
-    rows = sums.shape[0]
-    value = sums[...]
-    high = value.astype(jnp.bfloat16)
-    low = (value - high.astype(jnp.float32)).astype(jnp.bfloat16)
-    both = jnp.concatenate([high, low], axis=0)
-    got = jnp.dot(both, turned_ref[...], preferred_element_type=jnp.float32)
-    return got[:rows] + got[rows:]
+            value = decay[tile, here, :] * sino[tile, here, :]
+            picked[target, cols] = value.astype(jnp.bfloat16)
+
+    pairs.each(group, take)
+
+
+def back_project(pairs, group, picked, turned_ref, extra, out_ref, slab):
+    rows = out_ref.shape[0]
+    chunk = APART * slab
+    apart = pairs.apart(group)
+
+    def add(i, carry):
+        target = pl.ds(pl.multiple_of(pairs.target(group, i), slab), slab)
+        source = pl.ds(pl.multiple_of(lax.rem(i, APART) * slab, slab), slab)
+        out_ref[target, :] += extra[source, :]
+        return carry
+
+    got = jnp.dot(picked[0 : rows + chunk, :], turned_ref[...], preferred_element_type=jnp.float32)
+    out_ref[...] = got[0:rows]
+    extra[...] = got[rows:]
+    lax.fori_loop(0, jnp.minimum(apart, APART), add, 0)
+
+    def further(c, carry):
+        here = pl.ds(pl.multiple_of(rows + c * chunk, chunk), chunk)
+        extra[...] = jnp.dot(picked[here, :], turned_ref[...], preferred_element_type=jnp.float32)
+        lax.fori_loop(c * APART, jnp.minimum(apart, (c + 1) * APART), add, 0)
+        return carry
+
+    lax.fori_loop(1, (apart + APART - 1) // APART, further, 0)
 
 
 def early_kernel(
@@ -172,9 +227,11 @@
     index,
     scal,
     lists,
+    seen,
     proj,
     sems,
     *,
+    chips,
     local_blocks,
     slab,
     here,
@@ -193,7 +250,7 @@
         copy.start()
     for copy in copies[:4]:
         copy.wait()
-    index[0:slots, :] = window_rows(cover[...], here(), local_blocks, slab)
+    index[0:slots, :] = window_rows(cover[...], here(), chips, local_blocks, slab)
     index[slots : 2 * slots, :] = offset[...]
     index[2 * slots : 2 * slots + 1, :] = count[...]
     index[2 * slots + 1 : 2 * slots + 2, :] = angle[...]
@@ -203,21 +260,21 @@
     def fade(view, carry):
         rows = pl.ds(pl.multiple_of(view * det_rows, det_rows), det_rows)
         for tile in range(sino_ref.shape[0]):
-            seen = measured[view, :, tile * 128 : (tile + 1) * 128].astype(jnp.float32)
-            decay_ref[tile, rows, :] = jnp.exp(-seen)
-            sino_ref[tile, rows, :] = -seen
+            value = measured[view, :, tile * 128 : (tile + 1) * 128].astype(jnp.float32)
+            decay_ref[tile, rows, :] = jnp.exp(-value)
+            sino_ref[tile, rows, :] = -value
         return carry
 
     lax.fori_loop(0, views, fade, 0)
     load.wait()
-    list_pairs(scal, lists, 2 * piece, det_rows)
+    list_pairs(scal, lists, seen, 2 * piece, det_rows, tables, slab)
     save = fetch(lists, lists_ref, sems.at[0])
     for table in range(tables):
         copies[5 + table].wait()
         cols = slice(table * channels, (table + 1) * channels)
         turned_ref[cols, :] = table_ref[:, cols].T
     proj[...] = jnp.dot(both_ref[0:piece, :], table_ref[...], preferred_element_type=jnp.float32)
-    place(Pairs(lists), 2, sino_ref, proj, 4 * piece, slab)
+    place(Pairs(lists), 2, sino_ref, proj, slab)
     save.wait()
 
 
@@ -227,26 +284,25 @@
     return load
 
 
-def project(load, lists, group, long_ref, short_ref, table_ref, begun_ref, sino_ref, proj, slab):
-    piece = long_ref.shape[0] - 8
+def project(load, lists, group, window, table_ref, begun_ref, sino_ref, proj, slab):
     sino_ref[...] = begun_ref[...]
-    window = jnp.concatenate([long_ref[0:piece, :], short_ref[0:piece, :]], axis=0)
     proj[...] = jnp.dot(window, table_ref[...], preferred_element_type=jnp.float32)
     load.wait()
-    place(Pairs(lists), group, sino_ref, proj, group * 2 * piece, slab)
+    place(Pairs(lists), group, sino_ref, proj, slab)
 
 
 def middle_kernel(
-    lists_ref, long_ref, short_ref, table_ref, begun_ref, sino_ref, lists, proj, sem, *, slab
+    lists_ref, first_ref, second_ref, table_ref, begun_ref, sino_ref, lists, proj, sem, *, slab
 ):
     load = fetch(lists_ref, lists, sem)
-    project(load, lists, 0, long_ref, short_ref, table_ref, begun_ref, sino_ref, proj, slab)
+    piece = first_ref.shape[0] - 8
+    window = jnp.concatenate([first_ref[0:piece, :], second_ref[0:piece, :]], axis=0)
+    project(load, lists, 0, window, table_ref, begun_ref, sino_ref, proj, slab)
 
 
 def main_kernel(
     lists_ref,
-    long_ref,
-    short_ref,
+    far_ref,
     table_ref,
     turned_ref,
     begun_ref,
@@ -255,30 +311,37 @@
     give_ref,
     lists,
     proj,
-    sums,
+    picked,
+    extra,
     sem,
     *,
     slab,
 ):
     load = fetch(lists_ref, lists, sem)
-    sums[...] = jnp.zeros_like(sums)
-    project(load, lists, 1, long_ref, short_ref, table_ref, begun_ref, sino_ref, proj, slab)
-    gather(Pairs(lists), 1, sino_ref, decay_ref, sums, sums.shape[0], slab)
-    give_ref[...] = back_project(sums, turned_ref)
+    static_rows = give_ref.shape[0] + extra.shape[0]
+    clear_rows(picked, static_rows)
+    step = far_ref.shape[0] // 2
+    window = jnp.concatenate([far_ref[0 : step - 8, :], far_ref[step : 2 * step - 8, :]], axis=0)
+    project(load, lists, 1, window, table_ref, begun_ref, sino_ref, proj, slab)
+    pairs = Pairs(lists)
+    gather(pairs, 1, sino_ref, decay_ref, picked, static_rows, slab)
+    back_project(pairs, 1, picked, turned_ref, extra, give_ref, slab)
 
 
 def rest_kernel(
-    lists_ref, turned_ref, sino_ref, decay_ref, out_ref, lists, sums, sem, *, group, first_row, slab
+    lists_ref, turned_ref, sino_ref, decay_ref, out_ref, lists, picked, extra, sem, *, group, slab
 ):
     load = fetch(lists_ref, lists, sem)
-    sums[...] = jnp.zeros_like(sums)
+    static_rows = out_ref.shape[0] + extra.shape[0]
+    clear_rows(picked, static_rows)
     load.wait()
-    gather(Pairs(lists), group, sino_ref, decay_ref, sums, first_row, slab)
-    out_ref[...] = back_project(sums, turned_ref)
+    pairs = Pairs(lists)
+    gather(pairs, group, sino_ref, decay_ref, picked, static_rows, slab)
+    back_project(pairs, group, picked, turned_ref, extra, out_ref, slab)
 
 
 def prior_kernel(
-    vol_ref, other_ref, long_ref, far_long_ref, short_ref, far_short_ref, out_ref, *, devices, here
+    vol_ref, other_ref, first_ref, second_ref, far_ref, out_ref, *, devices, here
 ):
     slices, strip, row = vol_ref.shape
     part = slices
@@ -287,10 +350,10 @@
     core = lax.rem(position, 2)
     odd = lax.rem(position // 2, 2)
 
-    def chip_slice(ref, which, via):
+    def chip_slice(ref, which, via, base=0):
         sub = which ^ via
-        at = sub * part + (part - 1) * which
-        tail = piece + 4 * sub + 2 * which
+        at = base + sub * part + (part - 1) * which
+        tail = base + piece + 4 * sub + 2 * which
         whole = ref[at : at + 1, :].astype(jnp.float32)
         more = ref[tail : tail + 2, :].astype(jnp.float32)
         whole = whole + (more[0:1] + more[1:2])
@@ -324,19 +387,19 @@
 
     @pl.when((core == 0) & (odd == 0))
     def _():
-        emit(chip_slice(far_long_ref, 1, 1), core_slice(0))
+        emit(chip_slice(far_ref, 1, 1), core_slice(0))
 
     @pl.when((core == 0) & (odd == 1))
     def _():
-        emit(chip_slice(short_ref, 1, 0), core_slice(0))
+        emit(chip_slice(far_ref, 1, 1, piece + 8), core_slice(0))
 
     @pl.when((core == 1) & (odd == 0))
     def _():
-        emit(core_slice(1), chip_slice(far_short_ref, 0, 0))
+        emit(core_slice(1), chip_slice(second_ref, 0, 1))
 
     @pl.when((core == 1) & (odd == 1))
     def _():
-        emit(core_slice(1), chip_slice(long_ref, 0, 1))
+        emit(core_slice(1), chip_slice(first_ref, 0, 1))
 
 
 def last_kernel(arrived_ref, passed_ref, prior_ref, out_ref):
@@ -354,7 +417,8 @@
     plane = strip * row
     devices = lax.axis_size(AXES)
     position = lax.axis_index(AXES)
-    swap, long, short = exchange_pairs(devices)
+    swap, first, second = exchange_pairs(devices)
+    back = lambda pairs: [(b, a) for a, b in pairs]
     send = lambda value, pairs: lax.ppermute(value, AXES, pairs)
     part = local_blocks * slab
     piece = 2 * part
@@ -390,13 +454,15 @@
         compiler_params=room(4),
         name="join",
     )(mine, other)
-    got_short = send(both, short)
-    got_long = send(both, long)
+    got_second = send(both, second)
+    got_first = send(both, first)
 
     sino_shape = shape((channels // 128, views * det_rows, 128), jnp.float32)
-    lists_shape = (10, views * slots)
+    lists_shape = (Pairs.FIELDS * Pairs.GROUPS + 2, views * slots)
     table_vmem, turned, lists, sino, decay = pl.pallas_call(
-        functools.partial(early_kernel, local_blocks=local_blocks, slab=slab, here=here),
+        functools.partial(
+            early_kernel, chips=devices // 2, local_blocks=local_blocks, slab=slab, here=here
+        ),
         out_shape=(
             shape((plane, tables * channels), table.dtype),
             shape((tables * channels, plane), table.dtype),
@@ -415,6 +481,7 @@
             pltpu.VMEM((2 * slots + 2, views), jnp.int32),
             pltpu.SMEM((2 * slots + 2, views), jnp.int32),
             pltpu.SMEM(lists_shape, jnp.int32),
+            pltpu.SMEM((5 * piece // slab * tables,), jnp.int32),
             pltpu.VMEM((piece, tables * channels), jnp.float32),
             pltpu.SemaphoreType.DMA((5 + tables,)),
         ],
@@ -430,15 +497,18 @@
         stay(count.reshape(1, views)),
         stay(angle_index.reshape(1, views)),
     )
-    got_short, got_long, table_vmem, turned, lists, sino, decay = lax.optimization_barrier(
-        (got_short, got_long, table_vmem, turned, lists, sino, decay)
+    got_second, got_first, table_vmem, turned, lists, sino, decay = lax.optimization_barrier(
+        (got_second, got_first, table_vmem, turned, lists, sino, decay)
     )
     index = [pltpu.SMEM(lists_shape, jnp.int32)]
     waits = [pltpu.SemaphoreType.DMA]
     rows_of = lambda rows: [pltpu.VMEM((rows, tables * channels), jnp.float32)]
-
-    far = send(jnp.concatenate([got_long, got_short], axis=0), swap)
-    far_long, far_short = far[: piece + 8], far[piece + 8 :]
+    picks_of = lambda rows: [
+        pltpu.VMEM((rows + (views * slots + APART) * slab, tables * channels), jnp.bfloat16),
+        pltpu.VMEM((APART * slab, plane), jnp.float32),
+    ]
+
+    far = send(jnp.concatenate([got_first, got_second], axis=0), swap)
     sino = pl.pallas_call(
         functools.partial(middle_kernel, slab=slab),
         out_shape=sino_shape,
@@ -448,40 +518,40 @@
         compiler_params=room(16),
         cost_estimate=cost(1, 1),
         name="middle",
-    )(lists, got_long, got_short, table_vmem, sino)
-    far_short, far_long, sino = lax.optimization_barrier((far_short, far_long, sino))
+    )(lists, got_first, got_second, table_vmem, sino)
+    far, sino = lax.optimization_barrier((far, sino))
     sino, give = pl.pallas_call(
         functools.partial(main_kernel, slab=slab),
         out_shape=(sino_shape, shape((2 * piece, plane), jnp.float32)),
-        in_specs=[vmem] * 7,
+        in_specs=[vmem] * 6,
         out_specs=(vmem, vmem),
-        scratch_shapes=index + rows_of(2 * piece) + rows_of(2 * piece) + waits,
+        scratch_shapes=index + rows_of(2 * piece) + picks_of(2 * piece) + waits,
         compiler_params=room(16),
         cost_estimate=cost(1, 1),
         name="main",
-    )(lists, far_long, far_short, table_vmem, turned, sino, decay)
+    )(lists, far, table_vmem, turned, sino, decay)
     taken = send(give, swap)
     keep = pl.pallas_call(
-        functools.partial(rest_kernel, group=0, first_row=0, slab=slab),
+        functools.partial(rest_kernel, group=0, slab=slab),
         out_shape=shape((2 * piece, plane), jnp.float32),
         in_specs=[vmem] * 4,
         out_specs=vmem,
-        scratch_shapes=index + rows_of(2 * piece) + waits,
+        scratch_shapes=index + picks_of(2 * piece) + waits,
         compiler_params=room(16),
         cost_estimate=cost(1, 1),
         name="rest",
     )(lists, turned, sino, decay)
     taken, keep = lax.optimization_barrier((taken, keep))
     wire = (keep + taken).astype(jnp.bfloat16)
-    back_short = send(wire[piece:], short)
-    back_long = send(wire[:piece], long)
+    back_second = send(wire[piece:], back(second))
+    back_first = send(wire[:piece], back(first))
 
     home = pl.pallas_call(
-        functools.partial(rest_kernel, group=2, first_row=4 * piece, slab=slab),
+        functools.partial(rest_kernel, group=2, slab=slab),
         out_shape=shape((piece, plane), jnp.float32),
         in_specs=[vmem] * 4,
         out_specs=vmem,
-        scratch_shapes=index + rows_of(piece) + waits,
+        scratch_shapes=index + picks_of(piece) + waits,
         compiler_params=room(16),
         cost_estimate=cost(1, 1),
         name="home",
@@ -489,17 +559,17 @@
     prior = pl.pallas_call(
         functools.partial(prior_kernel, devices=devices, here=here),
         out_shape=shape((part, plane), jnp.float32),
-        in_specs=[vmem] * 6,
+        in_specs=[vmem] * 5,
         out_specs=vmem,
         compiler_params=room(8),
         cost_estimate=cost(1, 1),
         name="prior",
-    )(mine, other, got_long, far_long, got_short, far_short)
-    back_short, back_long, home, prior = lax.optimization_barrier(
-        (back_short, back_long, home, prior)
+    )(mine, other, got_first, got_second, far)
+    back_second, back_first, home, prior = lax.optimization_barrier(
+        (back_second, back_first, home, prior)
     )
 
-    arrived = (back_short.astype(jnp.float32) + back_long.astype(jnp.float32)) + home
+    arrived = (back_second.astype(jnp.float32) + back_first.astype(jnp.float32)) + home
     passed = send(arrived[part:], swap)
     out = pl.pallas_call(
         last_kernel,

time: 30.2 us -> 30 us (level)
  starting transfers between devices: 10.4 us -> 9.23 us
  waiting for transfers between devices: 6.92 us -> 7.92 us
    ppermute x8, starting transfers between devices: 10.4 us -> 9.23 us  [shards(): send = lambda value, pairs: lax.ppermute(value, AXES, pairs)]
    ppermute x8, waiting for transfers between devices: 6.92 us -> 7.92 us  [shards(): send = lambda value, pairs: lax.ppermute(value, AXES, pairs)]
    pallas_call x1, Pallas kernels: 2.48 us -> 2.09 us  [shards(): pl.pallas_call(functools.partial(main_kernel, slab=slab), out_shape=(sino...]
    pallas_call x3, Pallas kernels: 7.07 us -> 7.44 us  [the longest x1 4.25 us: shards(): pl.pallas_call(functools.partial(early_kernel, chips=devices // 2, local_...]
  transfers between devices with their start and end apart: 8 -> 8, of which waited for: 6 -> 6; matrix products, arithmetic and copies ran while one was open for 0% -> 0% of each run, Pallas kernels for 30% -> 31%
where the time goes in v5:
time: 30 us
  Pallas kernels  12.5 us (42%)
  starting transfers between devices  9.23 us (31%)
  waiting for transfers between devices  7.92 us (26%)
    ppermute x8, starting transfers between devices, shards(): send = lambda value, pairs: lax.ppermute(value, AXES, pairs)  9.23 us
    ppermute x8, waiting for transfers between devices, shards(): send = lambda value, pairs: lax.ppermute(value, AXES, pairs)  7.92 us
    pallas_call x1, Pallas kernels, shards(): pl.pallas_call(functools.partial(early_kernel, chips=devices // 2, local_...  4.25 us
    pallas_call x1, Pallas kernels, shards(): pl.pallas_call(functools.partial(main_kernel, slab=slab), out_shape=(sino...  2.09 us
    pallas_call x1, Pallas kernels, shards(): pl.pallas_call(functools.partial(rest_kernel, group=0, slab=slab), out_sh...  1.82 us
    pallas_call x1, Pallas kernels, shards(): pl.pallas_call(functools.partial(rest_kernel, group=2, slab=slab), out_sh...  1.37 us
    pallas_call x1, Pallas kernels, shards(): pl.pallas_call(load_kernel, out_shape=shape(flat.shape, flat.dtype), in_s...  0.91 us
    pallas_call x1, Pallas kernels, shards(): pl.pallas_call(functools.partial(middle_kernel, slab=slab), out_shape=sin...  0.86 us
  transfers between devices with their start and end apart: 8, of which 6 were waited for; matrix products, arithmetic and copies ran while one was open for 0% of the time, Pallas kernels for 31%

profile of v5, /device:TPU:3, one launch (start us, length us, event | category | flops | bytes accessed | tf_op | source)
XLA Modules:
  0.0 30.0 jit_solution(5929665942554455479)
XLA Ops:
  0.0 0.7 %collective-permute-start = (f32[32,2,512]{2,1,0:T(2,128)}, f32[32,2,512]{2,1,0:T(2,128)S(1)}, u32[]{:S(2)}, u32[]{:S(2)}) collective-permute-start(f32[32,2,512]{2,1,0:T(2,128)} %bitcast.8), channel_id=1, source_target_pairs={{0,1},{1,0},{2,3},{3,2},{4,5},{5,4},{6,7},{7,6},{8,9},{9,8},{10,11... | collective-permute-start | bytes 393224 | tf_op jit(solution)/shard_map/ppermute | solution.py:422
  0.7 0.9 %load.1.own_ref.vol_ref = f32[32,2,512]{2,1,0:T(2,128)S(1)} custom-call(f32[32,2,512]{2,1,0:T(2,128)} %bitcast.9), custom_call_target="tpu_custom_call" | custom-call | flops 1 | bytes 1 | tf_op jit(solution)/shard_map/load/pallas_call | solution.py:438
  1.6 0.3 collective-permute-done.other_ref
  1.9 0.3 %join.1.both_ref = bf16[72,1024]{1,0:T(8,128)(2,1)S(1)} custom-call(f32[32,2,512]{2,1,0:T(2,128)S(1)} %load.1.own_ref.vol_ref, f32[32,2,512]{2,1,0:T(2,128)S(1)} %collective-permute-done.other_ref), custom_call_target="tpu_custom_call" | custom-call | tf_op jit(solution)/shard_map/join/pallas_call | solution.py:449
  2.2 4.3 %collective-permute-start.2 = (bf16[72,1024]{1,0:T(8,128)(2,1)S(1)}, bf16[72,1024]{1,0:T(8,128)(2,1)S(1)}, u32[]{:S(2)}, u32[]{:S(2)}) collective-permute-start(bf16[72,1024]{1,0:T(8,128)(2,1)S(1)} %join.1.both_ref), channel_id=1, source_target_pairs={{2,6},{8,12},{10,14},{16,20},{18,22},{24,28},{3,5},{7,9},{11,13},{... | collective-permute-start | bytes 442376 | tf_op jit(solution)/shard_map/ppermute | solution.py:422
  6.5 0.0 collective-permute-start.1
  6.5 4.2 %early.1 = (bf16[1024,1792]{1,0:T(8,128)(2,1)S(1)}, bf16[1792,1024]{1,0:T(8,128)(2,1)S(1)}, s32[17,32]{1,0:T(8,128)S(1)}, f32[7,512,128]{2,1,0:T(8,128)S(1)}, f32[7,512,128]{2,1,0:T(8,128)S(1)}) custom-call(bf16[72,1024]{1,0:T(8,128)(2,1)S(1)} %join.1.both_ref, bf16[2,1024,896]{2,1,0:T(8,128)(2,1)} %bitcast.7, bf16[8,64,896]{2,1,0:T(8,128)(2,1)} %measured_hbm.1, ...), custom_call_target="tpu_custom_call" | custom-call | flops 1 | bytes 1 | tf_op jit(solution)/shard_map/early/pallas_call | solution.py:462
  10.7 0.5 %collective-permute-done.2.first_ref = bf16[72,1024]{1,0:T(8,128)(2,1)S(1)} collective-permute-done((bf16[72,1024]{1,0:T(8,128)(2,1)S(1)}, bf16[72,1024]{1,0:T(8,128)(2,1)S(1)}, u32[]{:S(2)}, u32[]{:S(2)}) %collective-permute-start.2) | collective-permute-done | bytes 147488 | tf_op jit(solution)/shard_map/ppermute | solution.py:422
  11.2 0.7 %collective-permute-done.1.second_ref = bf16[72,1024]{1,0:T(8,128)(2,1)S(1)} collective-permute-done((bf16[72,1024]{1,0:T(8,128)(2,1)S(1)}, bf16[72,1024]{1,0:T(8,128)(2,1)S(1)}, u32[]{:S(2)}, u32[]{:S(2)}) %collective-permute-start.1) | collective-permute-done | bytes 147488 | tf_op jit(solution)/shard_map/ppermute | solution.py:422
  12.0 1.0 %collective-permute-start.3 = (bf16[144,1024]{1,0:T(8,128)(2,1)S(1)}, bf16[144,1024]{1,0:T(8,128)(2,1)S(1)}, u32[]{:S(2)}, u32[]{:S(2)}) collective-permute-start(bf16[144,1024]{1,0:T(8,128)(2,1)S(1)} %pad_maximum_fusion), channel_id=1, source_target_pairs={{0,1},{1,0},{2,3},{3,2},{4,5},{5,4},{6,7},{7,6},{8,9},{9,8},{10,11... | collective-permute-start | bytes 884744 | tf_op jit(solution)/shard_map/ppermute | solution.py:422
  13.0 0.9 %middle.1.begun_ref = f32[7,512,128]{2,1,0:T(8,128)S(1)} custom-call(s32[17,32]{1,0:T(8,128)S(1)} %get-tuple-element.36.lists_ref, bf16[72,1024]{1,0:T(8,128)(2,1)S(1)} %collective-permute-done.2.first_ref, bf16[72,1024]{1,0:T(8,128)(2,1)S(1)} %collective-permute-done.1.second_ref, bf16[1024,1792]{1,0:T(8,128)(2,1)S(1)} %get-tuple-element.39.table_ref, ...), custom_call_target="tpu_custom_call" | custom-call | flops 1 | bytes 1 | tf_op jit(solution)/shard_map/middle/pallas_call | solution.py:512
  13.9 0.3 %collective-permute-done.3.far_ref = bf16[144,1024]{1,0:T(8,128)(2,1)S(1)} collective-permute-done((bf16[144,1024]{1,0:T(8,128)(2,1)S(1)}, bf16[144,1024]{1,0:T(8,128)(2,1)S(1)}, u32[]{:S(2)}, u32[]{:S(2)}) %collective-permute-start.3) | collective-permute-done | bytes 294944 | tf_op jit(solution)/shard_map/ppermute | solution.py:422
  14.2 2.1 %main.1 = (f32[7,512,128]{2,1,0:T(8,128)S(1)}, f32[128,1024]{1,0:T(8,128)S(1)}) custom-call(s32[17,32]{1,0:T(8,128)S(1)} %get-tuple-element.36.lists_ref, bf16[144,1024]{1,0:T(8,128)(2,1)S(1)} %collective-permute-done.3.far_ref, bf16[1024,1792]{1,0:T(8,128)(2,1)S(1)} %get-tuple-element.39.table_ref, bf16[1792,1024]{1,0:T(8,128)(2,1)S(1)} %get-tuple-element.42.turned_ref, ...), custom_call_target="tpu_custom_call" | custom-call | flops 1 | bytes 1 | tf_op jit(solution)/shard_map/main/pallas_call | solution.py:523
  16.3 0.5 %collective-permute-start.4 = (f32[128,1024]{1,0:T(8,128)S(1)}, f32[128,1024]{1,0:T(8,128)S(1)}, u32[]{:S(2)}, u32[]{:S(2)}) collective-permute-start(f32[128,1024]{1,0:T(8,128)S(1)} %get-tuple-element.45), channel_id=1, source_target_pairs={{0,1},{1,0},{2,3},{3,2},{4,5},{5,4},{6,7},{7,6},{8,9},{9,8},{10,11... | collective-permute-start | bytes 1572872 | tf_op jit(solution)/shard_map/ppermute | solution.py:422
  16.8 1.8 %rest.1 = f32[128,1024]{1,0:T(8,128)S(1)} custom-call(s32[17,32]{1,0:T(8,128)S(1)} %get-tuple-element.36.lists_ref, bf16[1792,1024]{1,0:T(8,128)(2,1)S(1)} %get-tuple-element.42.turned_ref, f32[7,512,128]{2,1,0:T(8,128)S(1)} %get-tuple-element.46.sino_ref, f32[7,512,128]{2,1,0:T(8,128)S(1)} %get-tuple-element.44.decay_ref), custom_call_target="tpu_custom_call" | custom-call | flops 1 | bytes 1 | tf_op jit(solution)/shard_map/rest/pallas_call | solution.py:534
  18.7 0.0 collective-permute-done.4
  18.7 0.1 add_convert_fusion
  18.8 2.6 %collective-permute-start.6 = (bf16[64,1024]{1,0:T(8,128)(2,1)S(1)}, bf16[64,1024]{1,0:T(8,128)(2,1)S(1)}, u32[]{:S(2)}, u32[]{:S(2)}) collective-permute-start(bf16[64,1024]{1,0:T(8,128)(2,1)S(1)} %get-tuple-element.55), channel_id=1, source_target_pairs={{6,2},{12,8},{14,10},{20,16},{22,18},{28,24},{5,3},{9,7},{13,11},{... | collective-permute-start | bytes 393224 | tf_op jit(solution)/shard_map/ppermute | solution.py:422
  21.4 0.0 collective-permute-start.5
  21.4 0.2 prior.1.prior_ref
  21.6 1.4 %home.1 = f32[64,1024]{1,0:T(8,128)S(1)} custom-call(s32[17,32]{1,0:T(8,128)S(1)} %get-tuple-element.36.lists_ref, bf16[1792,1024]{1,0:T(8,128)(2,1)S(1)} %get-tuple-element.42.turned_ref, f32[7,512,128]{2,1,0:T(8,128)S(1)} %get-tuple-element.46.sino_ref, f32[7,512,128]{2,1,0:T(8,128)S(1)} %get-tuple-element.44.decay_ref), custom_call_target="tpu_custom_call" | custom-call | flops 1 | bytes 1 | tf_op jit(solution)/shard_map/home/pallas_call | solution.py:549
  23.0 4.8 %collective-permute-done.6 = bf16[64,1024]{1,0:T(8,128)(2,1)S(1)} collective-permute-done((bf16[64,1024]{1,0:T(8,128)(2,1)S(1)}, bf16[64,1024]{1,0:T(8,128)(2,1)S(1)}, u32[]{:S(2)}, u32[]{:S(2)}) %collective-permute-start.6) | collective-permute-done | bytes 131104 | tf_op jit(solution)/shard_map/ppermute | solution.py:422
  27.7 0.0 collective-permute-done.5
  27.8 0.1 add_add_fusion
  27.8 0.1 collective-permute-start.7
  27.9 1.3 %collective-permute-done.7.passed_ref = f32[32,1024]{1,0:T(8,128)S(1)} collective-permute-done((f32[32,1024]{1,0:T(8,128)S(1)}, f32[32,1024]{1,0:T(8,128)S(1)}, u32[]{:S(2)}, u32[]{:S(2)}) %collective-permute-start.7) | collective-permute-done | bytes 131104 | tf_op jit(solution)/shard_map/ppermute | solution.py:422
  29.2 0.7 %last.1 = f32[32,2,512]{2,1,0:T(2,128)} custom-call(f32[32,1024]{1,0:T(8,128)S(1)} %get-tuple-element.54.arrived_ref, f32[32,1024]{1,0:T(8,128)S(1)} %collective-permute-done.7.passed_ref, f32[32,1024]{1,0:T(8,128)S(1)} %prior.1.prior_ref), custom_call_target="tpu_custom_call" | custom-call | tf_op jit(solution)/shard_map/last/pallas_call | solution.py:574
  (3 shorter events, 0.1 us)
Async XLA Ops:
  0.0 1.9 %collective-permute-start = (f32[32,2,512]{2,1,0:T(2,128)}, f32[32,2,512]{2,1,0:T(2,128)S(1)}, u32[]{:S(2)}, u32[]{:S(2)}) collective-permute-start(f32[32,2,512]{2,1,0:T(2,128)} %bitcast.8), channel_id=1, source_target_pairs={{0,1},{1,0},{2,3},{3,2},{4,5},{5,4},{6,7},{7,6},{8,9},{9,8},{10,11... | collective-permute-start | bytes 393224 | tf_op jit(solution)/shard_map/ppermute | solution.py:422
  2.2 9.0 %collective-permute-start.2 = (bf16[72,1024]{1,0:T(8,128)(2,1)S(1)}, bf16[72,1024]{1,0:T(8,128)(2,1)S(1)}, u32[]{:S(2)}, u32[]{:S(2)}) collective-permute-start(bf16[72,1024]{1,0:T(8,128)(2,1)S(1)} %join.1.both_ref), channel_id=1, source_target_pairs={{2,6},{8,12},{10,14},{16,20},{18,22},{24,28},{3,5},{7,9},{11,13},{... | collective-permute-start | bytes 442376 | tf_op jit(solution)/shard_map/ppermute | solution.py:422
  6.5 5.5 %collective-permute-start.1 = (bf16[72,1024]{1,0:T(8,128)(2,1)S(1)}, bf16[72,1024]{1,0:T(8,128)(2,1)S(1)}, u32[]{:S(2)}, u32[]{:S(2)}) collective-permute-start(bf16[72,1024]{1,0:T(8,128)(2,1)S(1)} %join.1.both_ref), channel_id=1, source_target_pairs={{4,8},{6,10},{12,16},{14,18},{20,24},{22,26},{0,2},{28,30},{1,3},{... | collective-permute-start | bytes 442376 | tf_op jit(solution)/shard_map/ppermute | solution.py:422
  12.0 2.2 %collective-permute-start.3 = (bf16[144,1024]{1,0:T(8,128)(2,1)S(1)}, bf16[144,1024]{1,0:T(8,128)(2,1)S(1)}, u32[]{:S(2)}, u32[]{:S(2)}) collective-permute-start(bf16[144,1024]{1,0:T(8,128)(2,1)S(1)} %pad_maximum_fusion), channel_id=1, source_target_pairs={{0,1},{1,0},{2,3},{3,2},{4,5},{5,4},{6,7},{7,6},{8,9},{9,8},{10,11... | collective-permute-start | bytes 884744 | tf_op jit(solution)/shard_map/ppermute | solution.py:422
  16.3 2.4 %collective-permute-start.4 = (f32[128,1024]{1,0:T(8,128)S(1)}, f32[128,1024]{1,0:T(8,128)S(1)}, u32[]{:S(2)}, u32[]{:S(2)}) collective-permute-start(f32[128,1024]{1,0:T(8,128)S(1)} %get-tuple-element.45), channel_id=1, source_target_pairs={{0,1},{1,0},{2,3},{3,2},{4,5},{5,4},{6,7},{7,6},{8,9},{9,8},{10,11... | collective-permute-start | bytes 1572872 | tf_op jit(solution)/shard_map/ppermute | solution.py:422
  18.8 9.0 %collective-permute-start.6 = (bf16[64,1024]{1,0:T(8,128)(2,1)S(1)}, bf16[64,1024]{1,0:T(8,128)(2,1)S(1)}, u32[]{:S(2)}, u32[]{:S(2)}) collective-permute-start(bf16[64,1024]{1,0:T(8,128)(2,1)S(1)} %get-tuple-element.55), channel_id=1, source_target_pairs={{6,2},{12,8},{14,10},{20,16},{22,18},{28,24},{5,3},{9,7},{13,11},{... | collective-permute-start | bytes 393224 | tf_op jit(solution)/shard_map/ppermute | solution.py:422
  21.4 6.4 %collective-permute-start.5 = (bf16[64,1024]{1,0:T(8,128)(2,1)S(1)}, bf16[64,1024]{1,0:T(8,128)(2,1)S(1)}, u32[]{:S(2)}, u32[]{:S(2)}) collective-permute-start(bf16[64,1024]{1,0:T(8,128)(2,1)S(1)} %get-tuple-element.56), channel_id=1, source_target_pairs={{8,4},{10,6},{16,12},{18,14},{24,20},{26,22},{2,0},{30,28},{3,1},{... | collective-permute-start | bytes 393224 | tf_op jit(solution)/shard_map/ppermute | solution.py:422
  27.8 1.4 %collective-permute-start.7 = (f32[32,1024]{1,0:T(8,128)S(1)}, f32[32,1024]{1,0:T(8,128)S(1)}, u32[]{:S(2)}, u32[]{:S(2)}) collective-permute-start(f32[32,1024]{1,0:T(8,128)S(1)} %get-tuple-element.53), channel_id=1, source_target_pairs={{0,1},{1,0},{2,3},{3,2},{4,5},{5,4},{6,7},{7,6},{8,9},{9,8},{10,11... | collective-permute-start | bytes 393224 | tf_op jit(solution)/shard_map/ppermute | solution.py:422

commit v6 on v5

--- a/solution.py
+++ b/solution.py
@@ -8,7 +8,8 @@
 from jax.sharding import PartitionSpec as P
 
 AXES = ("grp", "view")
-APART = 4
+STATIC = 12
+MORE = 4
 DELTA = 0.5
 PRIOR_WEIGHT = 2.0
 
@@ -33,28 +34,39 @@
     return swap, first, second
 
 
-def load_kernel(source, target, sem):
+def pack(plane, out_ref, first_row, cols):
+    high = plane.astype(jnp.bfloat16)
+    out_ref[first_row : first_row + plane.shape[0], cols] = high
+    ends = []
+    for at in (0, plane.shape[0] - 1):
+        rest = plane[at : at + 1] - high[at : at + 1].astype(jnp.float32)
+        mid = rest.astype(jnp.bfloat16).astype(jnp.float32)
+        ends += [mid, rest - mid]
+    return ends
+
+
+def load_kernel(source, target, own_ref, sem):
     copy = pltpu.make_async_copy(source, target, sem)
     copy.start()
     copy.wait()
-
-
-def join_kernel(own_ref, other_ref, out_ref):
-    slices, strip, row = own_ref.shape
+    slices, strip, row = target.shape
     for y in range(strip):
         cols = slice(y * row, (y + 1) * row)
-        spare = []
-        for k, ref in enumerate((own_ref, other_ref)):
-            plane = ref[:, y, :]
-            high = plane.astype(jnp.bfloat16)
-            out_ref[k * slices : (k + 1) * slices, cols] = high
-            rest = plane - high.astype(jnp.float32)
-            mid = rest.astype(jnp.bfloat16).astype(jnp.float32)
-            low = rest - mid
-            for at in (0, slices - 1):
-                spare += [mid[at : at + 1], low[at : at + 1]]
-        spare = jnp.concatenate(spare, axis=0).astype(jnp.bfloat16)
-        out_ref[2 * slices : 2 * slices + 8, cols] = spare
+        ends = pack(target[:, y, :], own_ref, 0, cols)
+        own_ref[slices : slices + 8, cols] = jnp.concatenate(ends + ends, axis=0).astype(
+            jnp.bfloat16
+        )
+
+
+def join_kernel(own_ref, other_ref, out_ref):
+    slices, strip, row = other_ref.shape
+    out_ref[0:slices, :] = own_ref[0:slices, :]
+    mine = own_ref[slices : slices + 8, :].astype(jnp.float32)
+    for y in range(strip):
+        cols = slice(y * row, (y + 1) * row)
+        ends = pack(other_ref[:, y, :], out_ref, slices, cols)
+        spare = jnp.concatenate([mine[0:4, cols]] + ends, axis=0)
+        out_ref[2 * slices : 2 * slices + 8, cols] = spare.astype(jnp.bfloat16)
 
 
 def window_rows(block, position, chips, local_blocks, slab):
@@ -93,22 +105,25 @@
 
         lax.fori_loop(0, self.ref[self.FIELDS * self.GROUPS, group], body, 0)
 
-    def apart(self, group):
+    def gathered(self, group):
         return self.ref[self.FIELDS * self.GROUPS + 1, group]
 
     def target(self, group, i):
         return self.ref[self.FIELDS * group + 4, i]
 
 
-def list_pairs(scal, lists, seen, near_rows, det_rows, tables, slab):
+def list_pairs(scal, lists, seen, height, held, near_rows, det_rows, tables, slab):
     slots = (scal.shape[0] - 2) // 2
+    most = held.shape[1]
     fields, groups = Pairs.FIELDS, Pairs.GROUPS
 
     def clear(i, carry):
-        seen[i] = jnp.int32(0)
+        height[i] = jnp.int32(0)
+        for table in range(tables):
+            seen[i, table] = jnp.int32(0)
         return carry
 
-    lax.fori_loop(0, seen.shape[0], clear, 0)
+    lax.fori_loop(0, height.shape[0], clear, 0)
     for k in range(groups):
         lists[fields * groups, k] = jnp.int32(0)
         lists[fields * groups + 1, k] = jnp.int32(0)
@@ -121,22 +136,26 @@
             @pl.when(slot < count)
             def _():
                 row = scal[slot, view]
+                block = row // slab
                 group = jnp.minimum(row // near_rows, groups - 1)
                 local = row - group * near_rows
+                first = fields * group
                 at = lists[fields * groups, group]
-                spare = lists[fields * groups + 1, group]
-                first = fields * group
-                bucket = (row // slab) * tables + table
-                taken = seen[bucket]
-                rows = jnp.where(group == groups - 1, near_rows // 2, near_rows)
+                used = lists[fields * groups + 1, group]
+                rank = seen[block, table]
+                top = height[block]
+                fresh = rank >= top
+                mine = jnp.where(fresh, used, held[block, rank])
+                held[block, rank] = mine
+                seen[block, table] = rank + 1
+                height[block] = jnp.where(fresh, rank + 1, top)
                 lists[first, at] = view * det_rows + scal[slots + slot, view]
                 lists[first + 1, at] = table
                 lists[first + 2, at] = local
-                lists[first + 3, at] = jnp.where(taken == 0, local, rows + spare * slab)
-                lists[first + 4, spare] = local
+                lists[first + 3, at] = mine * slab
+                lists[first + 4, mine] = local
                 lists[fields * groups, group] = at + 1
-                lists[fields * groups + 1, group] = spare + taken
-                seen[bucket] = jnp.int32(1)
+                lists[fields * groups + 1, group] = used + jnp.where(fresh, 1, 0)
 
         return carry
 
@@ -155,20 +174,21 @@
     pairs.each(group, add)
 
 
-def clear_rows(picked, rows):
-    picked[0:rows, :] = jnp.zeros((rows, picked.shape[1]), picked.dtype)
+def clear_rows(picked, static_rows):
+    picked[0:static_rows, :] = jnp.zeros((static_rows, picked.shape[1]), picked.dtype)
 
 
 def gather(pairs, group, sino, decay, picked, static_rows, slab):
     width = sino.shape[0] * 128
-    chunk = APART * slab
+    chunk = MORE * slab
 
     def clear(i, carry):
         here = pl.ds(pl.multiple_of(static_rows + i * chunk, chunk), chunk)
         picked[here, :] = jnp.zeros((chunk, picked.shape[1]), picked.dtype)
         return carry
 
-    lax.fori_loop(0, (pairs.apart(group) - 1) // APART, clear, 0)
+    more = pairs.gathered(group) * slab - static_rows
+    lax.fori_loop(0, (more + chunk - 1) // chunk, clear, 0)
 
     def take(source, table, local, dest):
         target = pl.ds(pl.multiple_of(dest, slab), slab)
@@ -181,29 +201,36 @@
     pairs.each(group, take)
 
 
-def back_project(pairs, group, picked, turned_ref, extra, out_ref, slab):
-    rows = out_ref.shape[0]
-    chunk = APART * slab
-    apart = pairs.apart(group)
-
-    def add(i, carry):
-        target = pl.ds(pl.multiple_of(pairs.target(group, i), slab), slab)
-        source = pl.ds(pl.multiple_of(lax.rem(i, APART) * slab, slab), slab)
-        out_ref[target, :] += extra[source, :]
+def back_project(pairs, group, picked, turned_ref, spread, out_ref, slab):
+    static_rows = spread.shape[0]
+    static = static_rows // slab
+    blocks = pairs.gathered(group)
+    out_ref[...] = jnp.zeros_like(out_ref)
+
+    def add_from(begin):
+        def add(i, carry):
+            target = pl.ds(pl.multiple_of(pairs.target(group, i), slab), slab)
+            source = pl.ds(pl.multiple_of((i - begin) * slab, slab), slab)
+            out_ref[target, :] += spread[source, :]
+            return carry
+
+        return add
+
+    spread[...] = jnp.dot(
+        picked[0:static_rows, :], turned_ref[...], preferred_element_type=jnp.float32
+    )
+    lax.fori_loop(0, jnp.minimum(blocks, static), add_from(0), 0)
+
+    def further(c, carry):
+        begin = static + c * MORE
+        here = pl.ds(pl.multiple_of(begin * slab, MORE * slab), MORE * slab)
+        spread[0 : MORE * slab, :] = jnp.dot(
+            picked[here, :], turned_ref[...], preferred_element_type=jnp.float32
+        )
+        lax.fori_loop(begin, jnp.minimum(blocks, begin + MORE), add_from(begin), 0)
         return carry
 
-    got = jnp.dot(picked[0 : rows + chunk, :], turned_ref[...], preferred_element_type=jnp.float32)
-    out_ref[...] = got[0:rows]
-    extra[...] = got[rows:]
-    lax.fori_loop(0, jnp.minimum(apart, APART), add, 0)
-
-    def further(c, carry):
-        here = pl.ds(pl.multiple_of(rows + c * chunk, chunk), chunk)
-        extra[...] = jnp.dot(picked[here, :], turned_ref[...], preferred_element_type=jnp.float32)
-        lax.fori_loop(c * APART, jnp.minimum(apart, (c + 1) * APART), add, 0)
-        return carry
-
-    lax.fori_loop(1, (apart + APART - 1) // APART, further, 0)
+    lax.fori_loop(0, (blocks - static + MORE - 1) // MORE, further, 0)
 
 
 def early_kernel(
@@ -228,6 +255,8 @@
     scal,
     lists,
     seen,
+    height,
+    held,
     proj,
     sems,
     *,
@@ -267,7 +296,7 @@
 
     lax.fori_loop(0, views, fade, 0)
     load.wait()
-    list_pairs(scal, lists, seen, 2 * piece, det_rows, tables, slab)
+    list_pairs(scal, lists, seen, height, held, 2 * piece, det_rows, tables, slab)
     save = fetch(lists, lists_ref, sems.at[0])
     for table in range(tables):
         copies[5 + table].wait()
@@ -312,32 +341,30 @@
     lists,
     proj,
     picked,
-    extra,
+    spread,
     sem,
     *,
     slab,
 ):
     load = fetch(lists_ref, lists, sem)
-    static_rows = give_ref.shape[0] + extra.shape[0]
-    clear_rows(picked, static_rows)
+    clear_rows(picked, spread.shape[0])
     step = far_ref.shape[0] // 2
     window = jnp.concatenate([far_ref[0 : step - 8, :], far_ref[step : 2 * step - 8, :]], axis=0)
     project(load, lists, 1, window, table_ref, begun_ref, sino_ref, proj, slab)
     pairs = Pairs(lists)
-    gather(pairs, 1, sino_ref, decay_ref, picked, static_rows, slab)
-    back_project(pairs, 1, picked, turned_ref, extra, give_ref, slab)
+    gather(pairs, 1, sino_ref, decay_ref, picked, spread.shape[0], slab)
+    back_project(pairs, 1, picked, turned_ref, spread, give_ref, slab)
 
 
 def rest_kernel(
-    lists_ref, turned_ref, sino_ref, decay_ref, out_ref, lists, picked, extra, sem, *, group, slab
+    lists_ref, turned_ref, sino_ref, decay_ref, out_ref, lists, picked, spread, sem, *, group, slab
 ):
     load = fetch(lists_ref, lists, sem)
-    static_rows = out_ref.shape[0] + extra.shape[0]
-    clear_rows(picked, static_rows)
+    clear_rows(picked, spread.shape[0])
     load.wait()
     pairs = Pairs(lists)
-    gather(pairs, group, sino_ref, decay_ref, picked, static_rows, slab)
-    back_project(pairs, group, picked, turned_ref, extra, out_ref, slab)
+    gather(pairs, group, sino_ref, decay_ref, picked, spread.shape[0], slab)
+    back_project(pairs, group, picked, turned_ref, spread, out_ref, slab)
 
 
 def prior_kernel(
@@ -435,17 +462,17 @@
     stay = lambda value: pltpu.with_memory_space_constraint(value, pltpu.HBM)
 
     other = send(flat, swap)
-    mine = pl.pallas_call(
+    mine, packed = pl.pallas_call(
         load_kernel,
-        out_shape=shape(flat.shape, flat.dtype),
+        out_shape=(shape(flat.shape, flat.dtype), shape((part + 8, plane), jnp.bfloat16)),
         in_specs=[hbm],
-        out_specs=vmem,
+        out_specs=(vmem, vmem),
         scratch_shapes=[pltpu.SemaphoreType.DMA],
         compiler_params=room(4),
         cost_estimate=cost(1, 1),
         name="load",
     )(stay(flat))
-    other, mine = lax.optimization_barrier((other, mine))
+    other, mine, packed = lax.optimization_barrier((other, mine, packed))
     both = pl.pallas_call(
         join_kernel,
         out_shape=shape((piece + 8, plane), jnp.bfloat16),
@@ -453,7 +480,7 @@
         out_specs=vmem,
         compiler_params=room(4),
         name="join",
-    )(mine, other)
+    )(packed, other)
     got_second = send(both, second)
     got_first = send(both, first)
 
@@ -481,7 +508,9 @@
             pltpu.VMEM((2 * slots + 2, views), jnp.int32),
             pltpu.SMEM((2 * slots + 2, views), jnp.int32),
             pltpu.SMEM(lists_shape, jnp.int32),
-            pltpu.SMEM((5 * piece // slab * tables,), jnp.int32),
+            pltpu.SMEM((5 * piece // slab, tables), jnp.int32),
+            pltpu.SMEM((5 * piece // slab,), jnp.int32),
+            pltpu.SMEM((5 * piece // slab, views * slots), jnp.int32),
             pltpu.VMEM((piece, tables * channels), jnp.float32),
             pltpu.SemaphoreType.DMA((5 + tables,)),
         ],
@@ -503,9 +532,9 @@
     index = [pltpu.SMEM(lists_shape, jnp.int32)]
     waits = [pltpu.SemaphoreType.DMA]
     rows_of = lambda rows: [pltpu.VMEM((rows, tables * channels), jnp.float32)]
-    picks_of = lambda rows: [
-        pltpu.VMEM((rows + (views * slots + APART) * slab, tables * channels), jnp.bfloat16),
-        pltpu.VMEM((APART * slab, plane), jnp.float32),
+    picks_of = lambda blocks: [
+        pltpu.VMEM(((max(views * slots, blocks) + MORE) * slab, tables * channels), jnp.bfloat16),
+        pltpu.VMEM((blocks * slab, plane), jnp.float32),
     ]
 
     far = send(jnp.concatenate([got_first, got_second], axis=0), swap)
@@ -525,7 +554,7 @@
         out_shape=(sino_shape, shape((2 * piece, plane), jnp.float32)),
         in_specs=[vmem] * 6,
         out_specs=(vmem, vmem),
-        scratch_shapes=index + rows_of(2 * piece) + picks_of(2 * piece) + waits,
+        scratch_shapes=index + rows_of(2 * piece) + picks_of(STATIC) + waits,
         compiler_params=room(16),
         cost_estimate=cost(1, 1),
         name="main",
@@ -536,7 +565,7 @@
         out_shape=shape((2 * piece, plane), jnp.float32),
         in_specs=[vmem] * 4,
         out_specs=vmem,
-        scratch_shapes=index + picks_of(2 * piece) + waits,
+        scratch_shapes=index + picks_of(STATIC) + waits,
         compiler_params=room(16),
         cost_estimate=cost(1, 1),
         name="rest",
@@ -551,7 +580,7 @@
         out_shape=shape((piece, plane), jnp.float32),
         in_specs=[vmem] * 4,
         out_specs=vmem,
-        scratch_shapes=index + picks_of(piece) + waits,
+        scratch_shapes=index + picks_of(8) + waits,
         compiler_params=room(16),
         cost_estimate=cost(1, 1),
         name="home",

time: 30 us -> 29.5 us (0.983)
  waiting for transfers between devices: 7.92 us -> 6.26 us
  starting transfers between devices: 9.23 us -> 9.77 us
  Pallas kernels: 12.5 us -> 12.9 us
    ppermute x8, waiting for transfers between devices: 7.92 us -> 6.26 us  [shards(): send = lambda value, pairs: lax.ppermute(value, AXES, pairs)]
    ppermute x8, starting transfers between devices: 9.23 us -> 9.77 us  [shards(): send = lambda value, pairs: lax.ppermute(value, AXES, pairs)]
  transfers between devices with their start and end apart: 8 -> 8, of which waited for: 6 -> 6; matrix products, arithmetic and copies ran while one was open for 0% -> 0% of each run, Pallas kernels for 31% -> 34%
where the time goes in v6:
time: 29.5 us; the launch traced here: 29.3 us
  Pallas kernels  12.9 us (44%)
  starting transfers between devices  9.77 us (33%)
  waiting for transfers between devices  6.26 us (21%)
    ppermute x8, starting transfers between devices, shards(): send = lambda value, pairs: lax.ppermute(value, AXES, pairs)  9.77 us
    ppermute x8, waiting for transfers between devices, shards(): send = lambda value, pairs: lax.ppermute(value, AXES, pairs)  6.26 us
    pallas_call x1, Pallas kernels, shards(): pl.pallas_call(functools.partial(early_kernel, chips=devices // 2, local_...  4.45 us
    pallas_call x1, Pallas kernels, shards(): pl.pallas_call(functools.partial(main_kernel, slab=slab), out_shape=(sino...  2.21 us
    pallas_call x1, Pallas kernels, shards(): pl.pallas_call(functools.partial(rest_kernel, group=0, slab=slab), out_sh...  1.79 us
    pallas_call x1, Pallas kernels, shards(): pl.pallas_call(functools.partial(rest_kernel, group=2, slab=slab), out_sh...  1.52 us
    pallas_call x1, Pallas kernels, shards(): pl.pallas_call(load_kernel, out_shape=(shape(flat.shape, flat.dtype), sha...  1.08 us
    pallas_call x1, Pallas kernels, shards(): pl.pallas_call(functools.partial(middle_kernel, slab=slab), out_shape=sin...  0.81 us
  transfers between devices with their start and end apart: 8, of which 6 were waited for; matrix products, arithmetic and copies ran while one was open for 0% of the time, Pallas kernels for 34%

profile of v6, /device:TPU:3, one launch (start us, length us, event | category | flops | bytes accessed | tf_op | source)
XLA Modules:
  0.0 29.3 jit_solution(13163148603592068848)
XLA Ops:
  0.0 0.7 %collective-permute-start = (f32[32,2,512]{2,1,0:T(2,128)}, f32[32,2,512]{2,1,0:T(2,128)S(1)}, u32[]{:S(2)}, u32[]{:S(2)}) collective-permute-start(f32[32,2,512]{2,1,0:T(2,128)} %bitcast.8), channel_id=1, source_target_pairs={{0,1},{1,0},{2,3},{3,2},{4,5},{5,4},{6,7},{7,6},{8,9},{9,8},{10,11... | collective-permute-start | bytes 393224 | tf_op jit(solution)/shard_map/ppermute | solution.py:449
  0.7 1.1 %load.1 = (f32[32,2,512]{2,1,0:T(2,128)S(1)}, bf16[40,1024]{1,0:T(8,128)(2,1)S(1)}) custom-call(f32[32,2,512]{2,1,0:T(2,128)} %bitcast.9), custom_call_target="tpu_custom_call" | custom-call | flops 1 | bytes 1 | tf_op jit(solution)/shard_map/load/pallas_call | solution.py:465
  1.8 0.1 collective-permute-done.other_ref
  1.9 0.2 join.1.both_ref
  2.0 4.3 %collective-permute-start.2 = (bf16[72,1024]{1,0:T(8,128)(2,1)S(1)}, bf16[72,1024]{1,0:T(8,128)(2,1)S(1)}, u32[]{:S(2)}, u32[]{:S(2)}) collective-permute-start(bf16[72,1024]{1,0:T(8,128)(2,1)S(1)} %join.1.both_ref), channel_id=1, source_target_pairs={{2,6},{8,12},{10,14},{16,20},{18,22},{24,28},{3,5},{7,9},{11,13},{... | collective-permute-start | bytes 442376 | tf_op jit(solution)/shard_map/ppermute | solution.py:449
  6.3 0.0 collective-permute-start.1
  6.3 4.4 %early.1 = (bf16[1024,1792]{1,0:T(8,128)(2,1)S(1)}, bf16[1792,1024]{1,0:T(8,128)(2,1)S(1)}, s32[17,32]{1,0:T(8,128)S(1)}, f32[7,512,128]{2,1,0:T(8,128)S(1)}, f32[7,512,128]{2,1,0:T(8,128)S(1)}) custom-call(bf16[72,1024]{1,0:T(8,128)(2,1)S(1)} %join.1.both_ref, bf16[2,1024,896]{2,1,0:T(8,128)(2,1)} %bitcast.7, bf16[8,64,896]{2,1,0:T(8,128)(2,1)} %measured_hbm.1, ...), custom_call_target="tpu_custom_call" | custom-call | flops 1 | bytes 1 | tf_op jit(solution)/shard_map/early/pallas_call | solution.py:489
  10.8 0.3 %collective-permute-done.2.first_ref = bf16[72,1024]{1,0:T(8,128)(2,1)S(1)} collective-permute-done((bf16[72,1024]{1,0:T(8,128)(2,1)S(1)}, bf16[72,1024]{1,0:T(8,128)(2,1)S(1)}, u32[]{:S(2)}, u32[]{:S(2)}) %collective-permute-start.2) | collective-permute-done | bytes 147488 | tf_op jit(solution)/shard_map/ppermute | solution.py:449
  11.1 0.7 %collective-permute-done.1.second_ref = bf16[72,1024]{1,0:T(8,128)(2,1)S(1)} collective-permute-done((bf16[72,1024]{1,0:T(8,128)(2,1)S(1)}, bf16[72,1024]{1,0:T(8,128)(2,1)S(1)}, u32[]{:S(2)}, u32[]{:S(2)}) %collective-permute-start.1) | collective-permute-done | bytes 147488 | tf_op jit(solution)/shard_map/ppermute | solution.py:449
  11.8 1.0 %collective-permute-start.3 = (bf16[144,1024]{1,0:T(8,128)(2,1)S(1)}, bf16[144,1024]{1,0:T(8,128)(2,1)S(1)}, u32[]{:S(2)}, u32[]{:S(2)}) collective-permute-start(bf16[144,1024]{1,0:T(8,128)(2,1)S(1)} %pad_maximum_fusion), channel_id=1, source_target_pairs={{0,1},{1,0},{2,3},{3,2},{4,5},{5,4},{6,7},{7,6},{8,9},{9,8},{10,11... | collective-permute-start | bytes 884744 | tf_op jit(solution)/shard_map/ppermute | solution.py:449
  12.8 0.8 %middle.1.begun_ref = f32[7,512,128]{2,1,0:T(8,128)S(1)} custom-call(s32[17,32]{1,0:T(8,128)S(1)} %get-tuple-element.41.lists_ref, bf16[72,1024]{1,0:T(8,128)(2,1)S(1)} %collective-permute-done.2.first_ref, bf16[72,1024]{1,0:T(8,128)(2,1)S(1)} %collective-permute-done.1.second_ref, bf16[1024,1792]{1,0:T(8,128)(2,1)S(1)} %get-tuple-element.44.table_ref, ...), custom_call_target="tpu_custom_call" | custom-call | flops 1 | bytes 1 | tf_op jit(solution)/shard_map/middle/pallas_call | solution.py:541
  13.7 0.4 %collective-permute-done.3.far_ref = bf16[144,1024]{1,0:T(8,128)(2,1)S(1)} collective-permute-done((bf16[144,1024]{1,0:T(8,128)(2,1)S(1)}, bf16[144,1024]{1,0:T(8,128)(2,1)S(1)}, u32[]{:S(2)}, u32[]{:S(2)}) %collective-permute-start.3) | collective-permute-done | bytes 294944 | tf_op jit(solution)/shard_map/ppermute | solution.py:449
  14.1 2.2 %main.1 = (f32[7,512,128]{2,1,0:T(8,128)S(1)}, f32[128,1024]{1,0:T(8,128)S(1)}) custom-call(s32[17,32]{1,0:T(8,128)S(1)} %get-tuple-element.41.lists_ref, bf16[144,1024]{1,0:T(8,128)(2,1)S(1)} %collective-permute-done.3.far_ref, bf16[1024,1792]{1,0:T(8,128)(2,1)S(1)} %get-tuple-element.44.table_ref, bf16[1792,1024]{1,0:T(8,128)(2,1)S(1)} %get-tuple-element.47.turned_ref, ...), custom_call_target="tpu_custom_call" | custom-call | flops 1 | bytes 1 | tf_op jit(solution)/shard_map/main/pallas_call | solution.py:552
  16.3 0.4 %collective-permute-start.4 = (f32[128,1024]{1,0:T(8,128)S(1)}, f32[128,1024]{1,0:T(8,128)S(1)}, u32[]{:S(2)}, u32[]{:S(2)}) collective-permute-start(f32[128,1024]{1,0:T(8,128)S(1)} %get-tuple-element.50), channel_id=1, source_target_pairs={{0,1},{1,0},{2,3},{3,2},{4,5},{5,4},{6,7},{7,6},{8,9},{9,8},{10,11... | collective-permute-start | bytes 1572872 | tf_op jit(solution)/shard_map/ppermute | solution.py:449
  16.7 1.8 %rest.1 = f32[128,1024]{1,0:T(8,128)S(1)} custom-call(s32[17,32]{1,0:T(8,128)S(1)} %get-tuple-element.41.lists_ref, bf16[1792,1024]{1,0:T(8,128)(2,1)S(1)} %get-tuple-element.47.turned_ref, f32[7,512,128]{2,1,0:T(8,128)S(1)} %get-tuple-element.51.sino_ref, f32[7,512,128]{2,1,0:T(8,128)S(1)} %get-tuple-element.49.decay_ref), custom_call_target="tpu_custom_call" | custom-call | flops 1 | bytes 1 | tf_op jit(solution)/shard_map/rest/pallas_call | solution.py:563
  18.5 0.0 collective-permute-done.4
  18.5 0.1 add_convert_fusion
  18.6 2.8 %collective-permute-start.6 = (bf16[64,1024]{1,0:T(8,128)(2,1)S(1)}, bf16[64,1024]{1,0:T(8,128)(2,1)S(1)}, u32[]{:S(2)}, u32[]{:S(2)}) collective-permute-start(bf16[64,1024]{1,0:T(8,128)(2,1)S(1)} %get-tuple-element.61), channel_id=1, source_target_pairs={{6,2},{12,8},{14,10},{20,16},{22,18},{28,24},{5,3},{9,7},{13,11},{... | collective-permute-start | bytes 393224 | tf_op jit(solution)/shard_map/ppermute | solution.py:449
  21.4 0.0 collective-permute-start.5
  21.4 1.5 %home.1 = f32[64,1024]{1,0:T(8,128)S(1)} custom-call(s32[17,32]{1,0:T(8,128)S(1)} %get-tuple-element.41.lists_ref, bf16[1792,1024]{1,0:T(8,128)(2,1)S(1)} %get-tuple-element.47.turned_ref, f32[7,512,128]{2,1,0:T(8,128)S(1)} %get-tuple-element.51.sino_ref, f32[7,512,128]{2,1,0:T(8,128)S(1)} %get-tuple-element.49.decay_ref), custom_call_target="tpu_custom_call" | custom-call | flops 1 | bytes 1 | tf_op jit(solution)/shard_map/home/pallas_call | solution.py:578
  22.9 0.2 prior.1.prior_ref
  23.1 3.8 %collective-permute-done.6 = bf16[64,1024]{1,0:T(8,128)(2,1)S(1)} collective-permute-done((bf16[64,1024]{1,0:T(8,128)(2,1)S(1)}, bf16[64,1024]{1,0:T(8,128)(2,1)S(1)}, u32[]{:S(2)}, u32[]{:S(2)}) %collective-permute-start.6) | collective-permute-done | bytes 131104 | tf_op jit(solution)/shard_map/ppermute | solution.py:449
  26.9 0.0 collective-permute-done.5
  26.9 0.1 add_add_fusion
  27.0 0.6 %collective-permute-start.7 = (f32[32,1024]{1,0:T(8,128)S(1)}, f32[32,1024]{1,0:T(8,128)S(1)}, u32[]{:S(2)}, u32[]{:S(2)}) collective-permute-start(f32[32,1024]{1,0:T(8,128)S(1)} %get-tuple-element.59), channel_id=1, source_target_pairs={{0,1},{1,0},{2,3},{3,2},{4,5},{5,4},{6,7},{7,6},{8,9},{9,8},{10,11... | collective-permute-start | bytes 393224 | tf_op jit(solution)/shard_map/ppermute | solution.py:449
  27.6 1.0 %collective-permute-done.7.passed_ref = f32[32,1024]{1,0:T(8,128)S(1)} collective-permute-done((f32[32,1024]{1,0:T(8,128)S(1)}, f32[32,1024]{1,0:T(8,128)S(1)}, u32[]{:S(2)}, u32[]{:S(2)}) %collective-permute-start.7) | collective-permute-done | bytes 131104 | tf_op jit(solution)/shard_map/ppermute | solution.py:449
  28.6 0.7 %last.1 = f32[32,2,512]{2,1,0:T(2,128)} custom-call(f32[32,1024]{1,0:T(8,128)S(1)} %get-tuple-element.60.arrived_ref, f32[32,1024]{1,0:T(8,128)S(1)} %collective-permute-done.7.passed_ref, f32[32,1024]{1,0:T(8,128)S(1)} %prior.1.prior_ref), custom_call_target="tpu_custom_call" | custom-call | tf_op jit(solution)/shard_map/last/pallas_call | solution.py:603
  (3 shorter events, 0.1 us)
Async XLA Ops:
  0.0 1.9 %collective-permute-start = (f32[32,2,512]{2,1,0:T(2,128)}, f32[32,2,512]{2,1,0:T(2,128)S(1)}, u32[]{:S(2)}, u32[]{:S(2)}) collective-permute-start(f32[32,2,512]{2,1,0:T(2,128)} %bitcast.8), channel_id=1, source_target_pairs={{0,1},{1,0},{2,3},{3,2},{4,5},{5,4},{6,7},{7,6},{8,9},{9,8},{10,11... | collective-permute-start | bytes 393224 | tf_op jit(solution)/shard_map/ppermute | solution.py:449
  2.0 9.0 %collective-permute-start.2 = (bf16[72,1024]{1,0:T(8,128)(2,1)S(1)}, bf16[72,1024]{1,0:T(8,128)(2,1)S(1)}, u32[]{:S(2)}, u32[]{:S(2)}) collective-permute-start(bf16[72,1024]{1,0:T(8,128)(2,1)S(1)} %join.1.both_ref), channel_id=1, source_target_pairs={{2,6},{8,12},{10,14},{16,20},{18,22},{24,28},{3,5},{7,9},{11,13},{... | collective-permute-start | bytes 442376 | tf_op jit(solution)/shard_map/ppermute | solution.py:449
  6.3 5.5 %collective-permute-start.1 = (bf16[72,1024]{1,0:T(8,128)(2,1)S(1)}, bf16[72,1024]{1,0:T(8,128)(2,1)S(1)}, u32[]{:S(2)}, u32[]{:S(2)}) collective-permute-start(bf16[72,1024]{1,0:T(8,128)(2,1)S(1)} %join.1.both_ref), channel_id=1, source_target_pairs={{4,8},{6,10},{12,16},{14,18},{20,24},{22,26},{0,2},{28,30},{1,3},{... | collective-permute-start | bytes 442376 | tf_op jit(solution)/shard_map/ppermute | solution.py:449
  11.8 2.2 %collective-permute-start.3 = (bf16[144,1024]{1,0:T(8,128)(2,1)S(1)}, bf16[144,1024]{1,0:T(8,128)(2,1)S(1)}, u32[]{:S(2)}, u32[]{:S(2)}) collective-permute-start(bf16[144,1024]{1,0:T(8,128)(2,1)S(1)} %pad_maximum_fusion), channel_id=1, source_target_pairs={{0,1},{1,0},{2,3},{3,2},{4,5},{5,4},{6,7},{7,6},{8,9},{9,8},{10,11... | collective-permute-start | bytes 884744 | tf_op jit(solution)/shard_map/ppermute | solution.py:449
  16.3 2.2 %collective-permute-start.4 = (f32[128,1024]{1,0:T(8,128)S(1)}, f32[128,1024]{1,0:T(8,128)S(1)}, u32[]{:S(2)}, u32[]{:S(2)}) collective-permute-start(f32[128,1024]{1,0:T(8,128)S(1)} %get-tuple-element.50), channel_id=1, source_target_pairs={{0,1},{1,0},{2,3},{3,2},{4,5},{5,4},{6,7},{7,6},{8,9},{9,8},{10,11... | collective-permute-start | bytes 1572872 | tf_op jit(solution)/shard_map/ppermute | solution.py:449
  18.6 8.3 %collective-permute-start.6 = (bf16[64,1024]{1,0:T(8,128)(2,1)S(1)}, bf16[64,1024]{1,0:T(8,128)(2,1)S(1)}, u32[]{:S(2)}, u32[]{:S(2)}) collective-permute-start(bf16[64,1024]{1,0:T(8,128)(2,1)S(1)} %get-tuple-element.61), channel_id=1, source_target_pairs={{6,2},{12,8},{14,10},{20,16},{22,18},{28,24},{5,3},{9,7},{13,11},{... | collective-permute-start | bytes 393224 | tf_op jit(solution)/shard_map/ppermute | solution.py:449
  21.4 5.5 %collective-permute-start.5 = (bf16[64,1024]{1,0:T(8,128)(2,1)S(1)}, bf16[64,1024]{1,0:T(8,128)(2,1)S(1)}, u32[]{:S(2)}, u32[]{:S(2)}) collective-permute-start(bf16[64,1024]{1,0:T(8,128)(2,1)S(1)} %get-tuple-element.62), channel_id=1, source_target_pairs={{8,4},{10,6},{16,12},{18,14},{24,20},{26,22},{2,0},{30,28},{3,1},{... | collective-permute-start | bytes 393224 | tf_op jit(solution)/shard_map/ppermute | solution.py:449
  27.0 1.6 %collective-permute-start.7 = (f32[32,1024]{1,0:T(8,128)S(1)}, f32[32,1024]{1,0:T(8,128)S(1)}, u32[]{:S(2)}, u32[]{:S(2)}) collective-permute-start(f32[32,1024]{1,0:T(8,128)S(1)} %get-tuple-element.59), channel_id=1, source_target_pairs={{0,1},{1,0},{2,3},{3,2},{4,5},{5,4},{6,7},{7,6},{8,9},{9,8},{10,11... | collective-permute-start | bytes 393224 | tf_op jit(solution)/shard_map/ppermute | solution.py:449
